TPU v7x, 32 devices: a whole 2x2x4 slice. The times are simulated.
32 devices in a mesh: groups: 2 (over x), shard: 16 (over z, y, core).
Axes of the slice: x: 2, y: 2, z: 4, core: 2. Of those that a mesh axis runs over, the one named last changes fastest.
Arguments:
- embeddings: bfloat16 [1280, 1024], P(('groups', 'shard')), parts along dimension 0, may hold values from -250 to 250
- probes: int32 [1280, 8], P(('groups', 'shard')), parts along dimension 0, may hold values from 0 to 15, all different within a row; in each aligned block of 40 rows (0 to 39, 40 to 79, ...) at most 40 rows name the same one
- assigned: int32 [1280], P(('groups', 'shard')), parts along dimension 0, may hold values from 0 to 1023
- prior_counts: int32 [32768], P(('groups', 'shard')), parts along dimension 0, may hold values from 1 to 16
- centroids: bfloat16 [32768, 1024], P(('groups', 'shard')), parts along dimension 0, may hold values from -30 to 30
- candidates: int32 [32768, 1], P(('groups', 'shard')), parts along dimension 0, may hold values from 0 to 47; in each aligned block of 1024 rows (0 to 1023, 1024 to 2047, ...) at most 32 rows name the same one
- centroids2: bfloat16 [12288, 1024], P(('groups', 'shard')), parts along dimension 0, may hold values from -30 to 30
Outputs:
- density: float32 [1280], P(('groups', 'shard')), parts along dimension 0
- new_centroids: bfloat16 [32768, 1024], P(('groups', 'shard')), parts along dimension 0
- new_counts: int32 [32768], P(('groups', 'shard')), parts along dimension 0
- level_two: float32 [32768], P(('groups', 'shard')), parts along dimension 0
There are 2 independent parts, one for each index of `groups`. A program takes and returns all parts, laid end to end along the dimension named above; each array names one. Nothing has to cross between parts.
Inputs may be any that keep to these rules, and one draw needn't show every extreme that they name: `probes`: each row names 8 different blocks. Among the 40 embeddings of one device no block is named more than 40 times, and in every draw some block is named exactly 40 times by one device's embeddings. `candidates`: among the 1024 level-1 centroids of one device no level-2 block is named more than 32 times, and in every draw some is named exactly 32 times.
All inputs are finite; a program needn't handle non-finite values.
Results may differ from a plain program's by a relative error of at most 0.0015.
Values may be sent and summed in bfloat16 or wider, within the bound.
No kernel may reach another device: no remote copies, remote signals or barrier semaphores. Data moves between devices by JAX's collectives and lax.ppermute only.
A program may use at most 64 MiB of HBM per device.

v0:
```python
import jax
import jax.numpy as jnp
from jax import lax
from jax.sharding import PartitionSpec as P

BLOCK = 1024
BLOCKS_DEV = 1
BLOCK2 = 128
BLOCKS2_DEV = 3


def unit_rows(values):
    wide = values.astype(jnp.float32)
    power = jnp.mean(wide * wide, axis=-1, keepdims=True) + 1e-06
    return (wide * lax.rsqrt(power)).astype(jnp.bfloat16)


def kernel_sums(rows, unit):
    scores = lax.dot_general(
        rows, unit, (((1,), (1,)), ((), ())), preferred_element_type=jnp.float32
    )
    return jnp.sum(jnp.exp((scores / rows.shape[1] - 1.0) / 0.1), axis=1)


def block_update(rows, slots, width):
    matches = slots[:, None] == jnp.arange(width, dtype=jnp.int32)[None, :]
    sums = lax.dot_general(
        matches.astype(jnp.bfloat16),
        rows,
        (((0,), (0,)), ((), ())),
        preferred_element_type=jnp.float32,
    )
    counts = jnp.sum(matches.astype(jnp.int32), axis=0)
    return (sums, counts)


def slot_ranks(targets, buckets):
    matches = (targets[:, None] == jnp.arange(buckets, dtype=jnp.int32)[None, :]).astype(jnp.int32)
    return jnp.sum(jnp.cumsum(matches, axis=0) * matches, axis=1) - 1


def body(embeddings, probes, assigned, prior_counts, centroids, candidates, centroids2):
    devices = lax.axis_size("shard")
    emb_rows, width = embeddings.shape
    probe_count = probes.shape[1]
    capacity = max(2, 2 * emb_rows * probe_count // (BLOCKS_DEV * devices))
    scaled = unit_rows(embeddings)
    units_old = unit_rows(centroids).reshape(BLOCKS_DEV, BLOCK, width)
    total = emb_rows * probe_count
    buckets = BLOCKS_DEV * devices
    flat = probes.reshape(-1)
    place = flat * capacity + slot_ranks(flat, buckets)
    leading = jnp.arange(total, dtype=jnp.int32) % probe_count == 0
    repeated = jnp.repeat(scaled, probe_count, axis=0)
    slot_values = jnp.where(leading, jnp.repeat(assigned, probe_count), -1)
    send_rows = jnp.zeros((buckets * capacity, width), jnp.bfloat16).at[place].set(repeated)
    send_slots = jnp.full((buckets * capacity,), -1, jnp.int32).at[place].set(slot_values)
    got_rows, got_slots = (
        lax.all_to_all(
            send_rows.reshape(devices, BLOCKS_DEV * capacity, width),
            "shard",
            split_axis=0,
            concat_axis=0,
            tiled=True,
        ),
        lax.all_to_all(
            send_slots.reshape(devices, BLOCKS_DEV * capacity),
            "shard",
            split_axis=0,
            concat_axis=0,
            tiled=True,
        ),
    )
    got_rows = got_rows.reshape(devices, BLOCKS_DEV, capacity, width)
    got_slots = got_slots.reshape(devices, BLOCKS_DEV, capacity)
    local = 0
    picked = got_rows[:, local].reshape(devices * capacity, width)
    slots = got_slots[:, local].reshape(-1)
    weights = [kernel_sums(picked, units_old[local]).reshape(devices, capacity)]
    more_sums, more_counts = block_update(picked, slots, BLOCK)
    sum_list = [more_sums]
    count_list = [more_counts]
    sums = jnp.stack(sum_list)
    counts = jnp.stack(count_list)
    returned = lax.all_to_all(
        jnp.stack(weights, axis=1).reshape(devices, BLOCKS_DEV * capacity),
        "shard",
        split_axis=0,
        concat_axis=0,
        tiled=True,
    )
    totals = jnp.sum(returned.reshape(-1)[place].reshape(emb_rows, probe_count), axis=1)
    density = jnp.log(totals / (probe_count * BLOCK))
    prior = prior_counts.reshape(BLOCKS_DEV, BLOCK)
    fresh = prior + counts
    updated = (
        prior.astype(jnp.float32)[:, :, None]
        * centroids.reshape(BLOCKS_DEV, BLOCK, width).astype(jnp.float32)
        + sums
    ) / fresh.astype(jnp.float32)[:, :, None]
    new_centroids = updated.astype(jnp.bfloat16).reshape(BLOCKS_DEV * BLOCK, width)
    units_new = unit_rows(updated).reshape(BLOCKS_DEV * BLOCK, width)
    rows_two = units_new.shape[0]
    second_capacity = max(2, 3 * rows_two // (2 * BLOCKS2_DEV * devices))
    buckets_two = BLOCKS2_DEV * devices
    chosen = candidates[:, 0]
    place_two = chosen * second_capacity + slot_ranks(chosen, buckets_two)
    send_two = (
        jnp.zeros((buckets_two * second_capacity, width), jnp.bfloat16).at[place_two].set(units_new)
    )
    send_two = send_two.reshape(devices, BLOCKS2_DEV, second_capacity, width)
    units_two = unit_rows(centroids2).reshape(BLOCKS2_DEV, BLOCK2, width)
    arrived = lax.all_to_all(send_two, "shard", split_axis=0, concat_axis=0, tiled=True)
    items = arrived.shape[2]
    weights_two = [
        kernel_sums(arrived[:, local].reshape(-1, width), units_two[local]).reshape(
            arrived.shape[0], items
        )
        for local in range(BLOCKS2_DEV)
    ]
    returned_two = lax.all_to_all(
        jnp.stack(weights_two, axis=1), "shard", split_axis=0, concat_axis=0, tiled=True
    )
    level_two = jnp.log(returned_two.reshape(-1)[place_two] / BLOCK2)
    return (density, new_centroids, fresh.reshape(-1), level_two)


def solution(mesh):
    placed = (
        P(("groups", "shard"), None),
        P(("groups", "shard"), None),
        P(("groups", "shard")),
        P(("groups", "shard")),
        P(("groups", "shard"), None),
        P(("groups", "shard"), None),
        P(("groups", "shard"), None),
    )
    return jax.shard_map(
        body,
        mesh=mesh,
        in_specs=placed,
        out_specs=(
            P(("groups", "shard")),
            P(("groups", "shard"), None),
            P(("groups", "shard")),
            P(("groups", "shard")),
        ),
        check_vma=False,
    )
```

profile of v0, /device:TPU:0, one launch (start us, length us, event | category | flops | bytes accessed | tf_op | source)
XLA Modules:
  0.0 184.3 jit_solution(6724240923127352187)
XLA Ops:
  0.6 0.7 broadcast_multiply_fusion
  1.3 0.8 copy.23
  2.1 0.1 copy.22
  2.2 0.1 mul.86
  2.3 0.1 eq.67
  2.4 0.9 reduce-window.14
  3.2 0.2 slice_reduce_fusion
  3.5 0.1 bitcast_bitcast_fusion.1
  3.6 0.7 broadcast_in_dim.15
  4.3 0.1 reshape.187
  4.5 2.9 %scatter_custom_fusion.1 = s32[640]{0:T(1024)S(1)} fusion(s32[320]{0:T(512)S(1)} %fusion.47, s32[320]{0:T(512)S(1)} %fusion.45, s32[]{:T(128)} %constant.76.clone.1), kind=kCustom, calls=%fused_computation.84 | custom fusion | bytes 2564 | tf_op jit(solution)/shard_map/scatter | solution.py:57
  7.4 0.7 all_to_all.24
  8.1 7.4 %all-to-all-start.2 = ((s32[16,1,40]{2,1,0:T(1,128)}), s32[16,1,40]{2,1,0:T(1,128)S(1)}, u32[]{:S(2)}, u32[]{:S(2)}) async-start(s32[16,1,40]{2,1,0:T(1,128)} %all_to_all.24), calls=%async_computation.2 | async-start | bytes 16384 | tf_op jit(solution)/shard_map/all_to_all | solution.py:66
  15.5 1.0 fusion.37
  16.5 1.0 fusion.38
  17.5 3.0 %scatter_custom_fusion = bf16[640,1024]{1,0:T(8,128)(2,1)} fusion(s32[320]{0:T(512)S(1)} %fusion.47, bf16[]{:T(256)} %constant.72.clone.1, bf16[40,1024]{1,0:T(8,128)(2,1)S(1)} %fusion.38), kind=kCustom, calls=%fused_computation.42 | custom fusion | bytes 1392642 | tf_op jit(solution)/shard_map/scatter | solution.py:56
  20.5 1.4 all-to-all-done.2
  21.9 4.7 %all-to-all-start = ((bf16[16,40,1024]{2,1,0:T(8,128)(2,1)}), bf16[16,40,1024]{2,1,0:T(8,128)(2,1)}, u32[]{:S(2)}, u32[]{:S(2)}) async-start(bf16[16,40,1024]{2,1,0:T(8,128)(2,1)} %bitcast.2), calls=%async_computation | async-start | bytes 2621440 | tf_op jit(solution)/shard_map/all_to_all | solution.py:59
  26.6 2.9 %copy.26 = bf16[1024,1024]{0,1:T(8,128)(2,1)S(1)} copy(bf16[1024,1024]{1,0:T(8,128)(2,1)} %param.11) | data formatting | bytes 4194304 | tf_op args[4]
  29.5 13.5 %reduce-window.16 = s32[48,8,128]{2,1,0:T(8,128)S(1)} reduce-window(s32[48,8,128]{2,1,0:T(8,128)S(1)} %fusion.36, s32[]{:T(128)} %constant.75.clone.1), window={size=1x1x128 pad=0_0x0_0x127_0}, to_apply=%region_10.11 | reduce-window | flops 6242304 | bytes 393220 | tf_op jit(solution)/shard_map/reduce-window.2
  43.0 0.1 slice.53
  43.1 0.1 copy.27
  43.3 0.1 copy.28
  43.4 0.1 broadcast_add_fusion
  43.5 0.1 fusion.35
  43.6 0.5 fusion
  44.1 0.5 broadcast.225
  44.6 0.7 reduce.13
  45.3 0.1 eq.75
  45.4 0.3 convert_reduce_fusion
  45.7 0.6 fusion.48
  46.3 7.7 %all-to-all-done = bf16[16,40,1024]{2,1,0:T(8,128)(2,1)} async-done(((bf16[16,40,1024]{2,1,0:T(8,128)(2,1)}), bf16[16,40,1024]{2,1,0:T(8,128)(2,1)}, u32[]{:S(2)}, u32[]{:S(2)}) %all-to-all-start) | async-done | bytes 1310752 | tf_op jit(solution)/shard_map/all_to_all | solution.py:59
  54.0 3.1 %exponential_reduce_fusion = f32[640]{0:T(1024)S(1)} fusion(bf16[640,1024]{1,0:T(8,128)(2,1)} %bitcast.3, bf16[1024,1024]{0,1:T(8,128)(2,1)S(1)} %copy.26, f32[1024]{0:T(1024)S(1)} %add_rsqrt_fusion.1), kind=kOutput, calls=%fused_computation.17 | convolution fusion | flops 1347943808 | bytes 3414528 | tf_op jit(solution)/shard_map/dot_general | solution.py:19
  57.1 0.7 all_to_all.22
  57.8 8.0 %all-to-all-start.1 = ((f32[16,1,40]{2,1,0:T(1,128)}), f32[16,1,40]{2,1,0:T(1,128)S(1)}, u32[]{:S(2)}, u32[]{:S(2)}) async-start(f32[16,1,40]{2,1,0:T(1,128)} %all_to_all.22), calls=%async_computation.1 | async-start | bytes 16384 | tf_op jit(solution)/shard_map/all_to_all | solution.py:85
  65.9 3.8 %multiply_reduce_fusion = (f32[1024]{0:T(1024)S(1)}, f32[1024,1024]{0,1:T(8,128)S(1)}) fusion(f32[1024]{0:T(1024)S(1)} %get-tuple-element.16, bf16[640,1024]{1,0:T(8,128)(2,1)} %bitcast.3, s32[640]{0:T(1024)S(1)} %eq.75, bf16[1024,1024]{0,1:T(8,128)(2,1)S(1)} %copy.26, f32[1024]{0:T(1024)S(1)} %get-tuple-element.23), kind=kOutput, calls=%fused_computation.13 | convolution fusion | flops 1349123072 | bytes 7617024 | tf_op jit(solution)/shard_map/dot_general | solution.py:27
  69.7 2.3 %multiply_convert_fusion = (bf16[1024,1024]{0,1:T(8,128)(2,1)S(1)}, bf16[1024,1024]{0,1:T(8,128)(2,1)}) fusion(f32[1024,1024]{0,1:T(8,128)S(1)} %get-tuple-element.25, f32[1024]{0:T(1024)S(1)} %add_rsqrt_fusion), kind=kLoop, calls=%fused_computation.12 | loop fusion | flops 3145728 | bytes 8392704 | tf_op jit(solution)/shard_map/convert_element_type | solution.py:15
  72.0 2.5 %copy.29 = bf16[1024,1024]{1,0:T(8,128)(2,1)} copy(bf16[1024,1024]{0,1:T(8,128)(2,1)S(1)} %get-tuple-element.18) | data formatting | bytes 4194304 | tf_op jit(solution)/shard_map/convert_element_type | solution.py:15
  74.5 8.1 %scatter_custom_fusion.2 = bf16[1536,1024]{1,0:T(8,128)(2,1)} fusion(s32[1024]{0:T(1024)S(1)} %bitcast.53, bf16[1024,1024]{1,0:T(8,128)(2,1)} %copy.29, bf16[]{:T(256)} %constant.72.clone.1), kind=kCustom, calls=%fused_computation.24 | custom fusion | bytes 3146240 | tf_op jit(solution)/shard_map/scatter | solution.py:109
  82.6 6.0 %all-to-all-start.3 = ((bf16[16,3,32,1024]{3,2,1,0:T(8,128)(2,1)}), bf16[16,3,32,1024]{3,2,1,0:T(8,128)(2,1)S(1)}, u32[]{:S(2)}, u32[]{:S(2)}) async-start(bf16[16,3,32,1024]{3,2,1,0:T(8,128)(2,1)} %bitcast.45), calls=%async_computation.3 | async-start | bytes 6291456 | tf_op jit(solution)/shard_map/all_to_all | solution.py:113
  88.6 1.4 fusion.8
  90.0 2.2 %fusion.9 = bf16[384,1024]{1,0:T(8,128)(2,1)} fusion(bf16[384,1024]{1,0:T(8,128)(2,1)} %param.13, f32[384]{0:T(512)S(1)} %add_rsqrt_fusion.2), kind=kLoop, calls=%fused_computation.23 | loop fusion | flops 1179648 | bytes 1574400 | tf_op jit(solution)/shard_map/convert_element_type | solution.py:15
  92.2 3.9 %copy.30 = bf16[1024,1024]{1,0:T(8,128)(2,1)} copy(bf16[1024,1024]{0,1:T(8,128)(2,1)} %get-tuple-element.19) | data formatting | bytes 4194304
  96.2 0.5 broadcast.224
  96.7 0.7 reduce.12
  97.4 0.1 reshape.185
  97.5 1.7 gather_fusion
  99.1 0.1 reshape.186
  99.2 0.1 reduce_sum.112
  99.3 48.6 %all-to-all-done.3 = bf16[16,3,32,1024]{3,2,1,0:T(8,128)(2,1)S(1)} async-done(((bf16[16,3,32,1024]{3,2,1,0:T(8,128)(2,1)}), bf16[16,3,32,1024]{3,2,1,0:T(8,128)(2,1)S(1)}, u32[]{:S(2)}, u32[]{:S(2)}) %all-to-all-start.3) | async-done | bytes 3145760 | tf_op jit(solution)/shard_map/all_to_all | solution.py:113
  148.0 1.7 fusion.49
  149.7 1.6 fusion.26
  151.2 0.1 stack_reshape.11
  151.3 1.8 fusion.25
  153.1 0.1 stack_reshape.10
  153.2 1.5 fusion.24
  154.7 0.1 stack_reshape.9
  154.8 0.6 pad_maximum_fusion
  155.4 15.4 %all-to-all-start.4 = ((f32[16,3,32]{2,1,0:T(4,128)}), f32[16,3,32]{2,1,0:T(4,128)S(1)}, u32[]{:S(2)}, u32[]{:S(2)}) async-start(f32[16,3,32]{2,1,0:T(4,128)} %pad_maximum_fusion), calls=%async_computation.4 | async-start | bytes 65536 | tf_op jit(solution)/shard_map/all_to_all | solution.py:121
  170.9 0.5 multiply_log_fusion.1
  171.4 6.1 %all-to-all-done.4 = f32[16,3,32]{2,1,0:T(4,128)S(1)} async-done(((f32[16,3,32]{2,1,0:T(4,128)}), f32[16,3,32]{2,1,0:T(4,128)S(1)}, u32[]{:S(2)}, u32[]{:S(2)}) %all-to-all-start.4) | async-done | bytes 6176 | tf_op jit(solution)/shard_map/all_to_all | solution.py:121
  177.5 0.1 reshape.190
  177.6 6.1 %gather_fusion.1 = f32[1024]{0:T(1024)S(1)} fusion(f32[1536]{0:T(1024)S(1)} %reshape.190, s32[1024]{0:T(1024)S(1)} %broadcast_clamp_fusion), kind=kCustom, calls=%fused_computation.1 | custom fusion | bytes 12288 | tf_op jit(solution)/shard_map/gather | solution.py:124
  183.7 0.6 multiply_log_fusion
  (25 shorter events, 0.2 us)
Async XLA Ops:
  8.1 13.8 %all-to-all-start.2 = ((s32[16,1,40]{2,1,0:T(1,128)}), s32[16,1,40]{2,1,0:T(1,128)S(1)}, u32[]{:S(2)}, u32[]{:S(2)}) async-start(s32[16,1,40]{2,1,0:T(1,128)} %all_to_all.24), calls=%async_computation.2 | async-start | bytes 16384 | tf_op jit(solution)/shard_map/all_to_all | solution.py:66
  21.9 32.2 %all-to-all-start = ((bf16[16,40,1024]{2,1,0:T(8,128)(2,1)}), bf16[16,40,1024]{2,1,0:T(8,128)(2,1)}, u32[]{:S(2)}, u32[]{:S(2)}) async-start(bf16[16,40,1024]{2,1,0:T(8,128)(2,1)} %bitcast.2), calls=%async_computation | async-start | bytes 2621440 | tf_op jit(solution)/shard_map/all_to_all | solution.py:59
  26.6 2.9 %copy-start.1 = (s32[1024,1]{0,1:T(1,128)S(1)}, s32[1024,1]{0,1:T(1,128)}, u32[]{:S(2)}) copy-start(s32[1024,1]{0,1:T(1,128)} %param.12) | copy-start | bytes 12292
  29.5 16.2 %copy-start.2 = (s32[1024]{0:T(1024)S(1)}, s32[1024]{0:T(1024)}, u32[]{:S(2)}) copy-start(s32[1024]{0:T(1024)} %param.10) | copy-start | bytes 12292
  57.8 24.8 %all-to-all-start.1 = ((f32[16,1,40]{2,1,0:T(1,128)}), f32[16,1,40]{2,1,0:T(1,128)S(1)}, u32[]{:S(2)}, u32[]{:S(2)}) async-start(f32[16,1,40]{2,1,0:T(1,128)} %all_to_all.22), calls=%async_computation.1 | async-start | bytes 16384 | tf_op jit(solution)/shard_map/all_to_all | solution.py:85
  82.6 65.4 %all-to-all-start.3 = ((bf16[16,3,32,1024]{3,2,1,0:T(8,128)(2,1)}), bf16[16,3,32,1024]{3,2,1,0:T(8,128)(2,1)S(1)}, u32[]{:S(2)}, u32[]{:S(2)}) async-start(bf16[16,3,32,1024]{3,2,1,0:T(8,128)(2,1)} %bitcast.45), calls=%async_computation.3 | async-start | bytes 6291456 | tf_op jit(solution)/shard_map/all_to_all | solution.py:113
  149.7 3.5 %copy-start = (bf16[16,1,32,1024]{3,2,1,0:T(8,128)(2,1)S(1)}, bf16[16,1,32,1024]{3,2,1,0:T(8,128)(2,1)}, u32[]{:S(2)}) copy-start(bf16[16,1,32,1024]{3,2,1,0:T(8,128)(2,1)} %get-tuple-element.20) | copy-start | bytes 3145732
  155.4 22.1 %all-to-all-start.4 = ((f32[16,3,32]{2,1,0:T(4,128)}), f32[16,3,32]{2,1,0:T(4,128)S(1)}, u32[]{:S(2)}, u32[]{:S(2)}) async-start(f32[16,3,32]{2,1,0:T(4,128)} %pad_maximum_fusion), calls=%async_computation.4 | async-start | bytes 65536 | tf_op jit(solution)/shard_map/all_to_all | solution.py:121
where the time goes:
time: 185 us; the launch traced here: 184 us
  waiting for transfers between devices  63.9 us (35%)
  starting transfers between devices  41.5 us (22%)
  local copies, waits for them, and re-layouts  38.2 us (21%)
  other arithmetic  28 us (15%)
  matrix products  11.8 us (6%)
    all_to_all x1, waiting for transfers between devices, body(): lax.all_to_all(send_two, 'shard', split_axis=0, concat_axis=0, tiled=True)  48.6 us
    all_to_all x1, starting transfers between devices, body(): lax.all_to_all(jnp.stack(weights_two, axis=1), 'shard', split_axis=0, con...  15.4 us
    another operation x7, other arithmetic  14.7 us
    scatter x1, local copies, waits for them, and re-layouts, body(): jnp.zeros((buckets_two * second_capacity, width), jnp.bfloat16)  8.06 us
    all_to_all x1, starting transfers between devices, body(): lax.all_to_all(jnp.stack(weights, axis=1).reshape(devices, BLOCKS_DEV * c...  8.02 us
    dot_general x4, matrix products, kernel_sums(): lax.dot_general(rows, unit, (((1,), (1,)), ((), ())), preferred_element_t...  7.92 us
    all_to_all x1, waiting for transfers between devices, body(): lax.all_to_all(send_rows.reshape(devices, BLOCKS_DEV * capacity, width),...  7.75 us
    unnamed x9, local copies, waits for them, and re-layouts  7.57 us
  transfers between devices with their start and end apart: 5, of which 4 were waited for; matrix products, arithmetic and copies ran while one was open for 29% of the time, Pallas kernels for 0%

commit v1 on v0

--- a/solution.py
+++ b/solution.py
@@ -1,6 +1,10 @@
+import functools
+
 import jax
 import jax.numpy as jnp
 from jax import lax
+from jax.experimental import pallas as pl
+from jax.experimental.pallas import tpu as pltpu
 from jax.sharding import PartitionSpec as P
 
 BLOCK = 1024
@@ -39,7 +43,7 @@
     return jnp.sum(jnp.cumsum(matches, axis=0) * matches, axis=1) - 1
 
 
-def body(embeddings, probes, assigned, prior_counts, centroids, candidates, centroids2):
+def general_body(embeddings, probes, assigned, prior_counts, centroids, candidates, centroids2):
     devices = lax.axis_size("shard")
     emb_rows, width = embeddings.shape
     probe_count = probes.shape[1]
@@ -125,6 +129,273 @@
     return (density, new_centroids, fresh.reshape(-1), level_two)
 
 
+NT = (((1,), (1,)), ((), ()))
+PARAMS = pltpu.CompilerParams(vmem_limit_bytes=48 * 1024 * 1024)
+META = 16
+
+
+def position():
+    me = lax.axis_index("shard")
+    return me, me // 4, (me // 2) % 2, me % 2
+
+
+def unit_wide(wide):
+    power = jnp.mean(wide * wide, axis=-1, keepdims=True) + 1e-06
+    return (wide * lax.rsqrt(power)).astype(jnp.bfloat16)
+
+
+def weights(scores, width):
+    return jnp.exp(scores * (10.0 / width) - 10.0)
+
+
+def one_hot(hits):
+    return jnp.where(hits, 1.0, 0.0).astype(jnp.bfloat16)
+
+
+def column(row):
+    return jnp.transpose(jnp.broadcast_to(row, (8, row.shape[1])))[:, 0:1]
+
+
+def pack_kernel(cap, per, cand_ref, prior_ref, cent_ref, far_own, far1, far2, far3, main1, main2, main3, info):
+    me, z, y, core = position()
+    cand = cand_ref[...]
+    rows = cand.shape[1]
+    buckets = 16 * per
+    dev = sum((cand >= per * step).astype(jnp.int32) for step in range(1, 16))
+    near = dev >> 2
+    plane = jnp.where(z >= 2, 3 - near, near)
+    rel = (((dev >> 1) & 1) ^ y) * 2 + ((dev & 1) ^ core)
+    named = cand == lax.broadcasted_iota(jnp.int32, (buckets, rows), 0)
+    before = lax.broadcasted_iota(jnp.int32, (rows, rows), 0) <= lax.broadcasted_iota(jnp.int32, (rows, rows), 1)
+    counted = jnp.dot(one_hot(named), one_hot(before), preferred_element_type=jnp.float32)
+    rank = jnp.sum(jnp.where(named, counted, 0.0), axis=0, keepdims=True).astype(jnp.int32) - 1
+    kind = plane * per + cand - dev * per
+    unit_slot = (cand - dev * per) * cap + rank
+    part = per * cap
+    slot_far = jnp.where(plane == 3, rel * part + unit_slot, -1)
+    slot_main = jnp.where(plane < 3, rel * 3 * part + plane * part + unit_slot, -1)
+    info[0:1, :] = slot_main
+    info[1:2, :] = kind
+    info[2:3, :] = rel * cap + rank
+    ident = lax.broadcasted_iota(jnp.int32, (1, rows), 1) + 1
+    line = lax.broadcasted_iota(jnp.int32, (META, rows), 0)
+    cent = cent_ref[...]
+    for r, (far, main) in enumerate(((far_own, None), (far1, main1), (far2, main2), (far3, main3))):
+        facts = jnp.where(line == 4 * r + 1, ident & 31, jnp.where(line == 4 * r + 2, prior_ref[...], 0))
+        facts = jnp.where(line == 4 * r, ident >> 5, facts).astype(jnp.float32).astype(jnp.bfloat16)
+        far[part : part + META, :] = jnp.zeros((META, cent.shape[1]), jnp.bfloat16)
+        pick = one_hot(slot_far == lax.broadcasted_iota(jnp.int32, (part, rows), 0) + r * part)
+        far[0:part, :] = jnp.dot(pick, cent, preferred_element_type=jnp.float32).astype(jnp.bfloat16)
+        far[part : part + META, 0:part] = lax.dot_general(
+            facts, pick, NT, preferred_element_type=jnp.float32
+        ).astype(jnp.bfloat16)
+        if main is not None:
+            pick = one_hot(slot_main == lax.broadcasted_iota(jnp.int32, (3 * part, rows), 0) + r * 3 * part)
+            main[...] = jnp.dot(pick, cent, preferred_element_type=jnp.float32).astype(jnp.bfloat16)
+            far[part : part + META, 128 : 128 + 3 * part] = lax.dot_general(
+                facts, pick, NT, preferred_element_type=jnp.float32
+            ).astype(jnp.bfloat16)
+
+
+def first_kernel(part, emb_ref, aux_ref, cent_ref, prior_ref, info, scaled, share, fresh_rows, fresh_counts, own_main, units):
+    me, z, y, core = position()
+    count, width = emb_ref.shape
+    probe_count = 8
+    rows = cent_ref.shape[0]
+    scaled[...] = unit_wide(emb_ref[...].astype(jnp.float32))
+    probes = aux_ref[0:probe_count, :]
+    target = jnp.where(probes[0:1, :] == me, aux_ref[probe_count : probe_count + 1, :], -1)
+    member = jnp.sum((probes == me).astype(jnp.float32), axis=0, keepdims=True)
+    prior = column(prior_ref[...].astype(jnp.float32))
+    step = 256
+    total = jnp.zeros((1, count), jnp.float32)
+    for start in range(0, rows, step):
+        old = cent_ref[start : start + step, :].astype(jnp.float32)
+        scores = lax.dot_general(unit_wide(old), scaled[...], NT, preferred_element_type=jnp.float32)
+        total = total + jnp.sum(weights(scores, width), axis=0, keepdims=True)
+        hits = one_hot(target == lax.broadcasted_iota(jnp.int32, (step, count), 0) + start)
+        sums = jnp.dot(hits, scaled[...], preferred_element_type=jnp.float32)
+        gained = jnp.sum(hits.astype(jnp.float32), axis=1, keepdims=True)
+        ahead = prior[start : start + step, :]
+        updated = (ahead * old + sums) / (ahead + gained)
+        fresh_rows[start : start + step, :] = updated.astype(jnp.bfloat16)
+        units[start : start + step, :] = unit_wide(updated)
+        gained_row = lax.dot_general(
+            jnp.ones((8, count), jnp.bfloat16), hits, NT, preferred_element_type=jnp.float32
+        )
+        fresh_counts[0:1, start : start + step] = prior_ref[0:1, start : start + step] + gained_row[0:1, :].astype(jnp.int32)
+    share[...] = jnp.where(member > 0.0, total, 0.0)
+    pick = one_hot(info[0:1, :] == lax.broadcasted_iota(jnp.int32, (3 * part, rows), 0))
+    own_main[...] = jnp.dot(pick, units[...], preferred_element_type=jnp.float32).astype(jnp.bfloat16)
+
+
+def forward_kernel(part, far0, far1, far2, far3, block, out):
+    me, z, y, core = position()
+    end = (z == 0) | (z == 3)
+
+    @pl.when(end)
+    def _():
+        facts = jnp.zeros((META, out.shape[1]), jnp.float32)
+        for r, far in enumerate((far0, far1, far2, far3)):
+            out[r * part : (r + 1) * part, :] = far[0:part, :]
+            facts = facts + far[part : part + META, :].astype(jnp.float32)
+        out[4 * part : 4 * part + META, :] = facts.astype(jnp.bfloat16)
+
+    @pl.when(jnp.logical_not(end))
+    def _():
+        out[0 : 4 * part, :] = block[...]
+        out[4 * part : 4 * part + META, :] = jnp.zeros((META, out.shape[1]), jnp.bfloat16)
+
+
+def second_kernel(
+    cap, per, scaled, aux_ref, own_main, far0, far1, far2, far3, main1, main2, main3,
+    own_set, near_set, cross_set, passed, last_set, out, packed, two,
+):
+    me, z, y, core = position()
+    end = (z == 0) | (z == 3)
+    part = per * cap
+    block = own_set.shape[0] // per
+    width = own_set.shape[1]
+    probe0 = aux_ref[0:1, :]
+    slots = aux_ref[8:9, :]
+
+    def place(w, r, rows):
+        for j in range(per):
+            packed[w, j, r * cap : (r + 1) * cap, :] = rows[j * cap : (j + 1) * cap, :]
+
+    def corrected(raw, facts, source):
+        facts = jnp.transpose(facts)
+        ident = (facts[:, 0:1] * 32.0 + facts[:, 1:2]).astype(jnp.int32)
+        ahead = facts[:, 2:3]
+        hits = one_hot(ident == jnp.where(probe0 == source, slots + 1, -1))
+        sums = jnp.dot(hits, scaled[...], preferred_element_type=jnp.float32)
+        gained = jnp.sum(hits.astype(jnp.float32), axis=1, keepdims=True)
+        updated = (ahead * raw.astype(jnp.float32) + sums) / jnp.maximum(ahead + gained, 1.0)
+        return unit_wide(updated)
+
+    def facts_of(ref, row, r, first):
+        lines = ref[row : row + META, :].astype(jnp.float32)
+        return lines[4 * r : 4 * r + 4, first : first + part]
+
+    for w in range(3):
+        place(w, 0, own_main[w * part : (w + 1) * part, :])
+    for r, (far, main) in enumerate(((far0, None), (far1, main1), (far2, main2), (far3, main3))):
+        source = me ^ r
+        place(3, r, corrected(far[0:part, :], facts_of(far, part, r, 0), source))
+        if main is not None:
+            for w in range(3):
+                place(w, r, corrected(main[w * part : (w + 1) * part, :], facts_of(far, part, r, 128 + w * part), source))
+        place(4, r, corrected(passed[r * part : (r + 1) * part, :], facts_of(passed, 4 * part, r, 0), me ^ 4 ^ r))
+    two[0] = unit_wide(jnp.where(end, own_set[...], near_set[...]).astype(jnp.float32))
+    two[1] = unit_wide(jnp.where(end, near_set[...], own_set[...]).astype(jnp.float32))
+    two[2] = unit_wide(jnp.where(end, passed[0 : 4 * part, :], cross_set[...]).astype(jnp.float32))
+    two[3] = unit_wide(last_set[...].astype(jnp.float32))
+    for w in range(5):
+        for j in range(per):
+            scores = lax.dot_general(
+                two[min(w, 3), j * block : (j + 1) * block, :], packed[w, j], NT, preferred_element_type=jnp.float32
+            )
+            out[w * per + j : w * per + j + 1, :] = jnp.sum(weights(scores, width), axis=0, keepdims=True)
+
+
+def last_kernel(cap, per, block, info, res0, res1, res2, res3, up0, up1, up2, up3, out):
+    me, z, y, core = position()
+    end = (z == 0) | (z == 3)
+    lane = lax.broadcasted_iota(jnp.int32, (16, 4 * cap), 1) // cap
+    line = lax.broadcasted_iota(jnp.int32, (16, 4 * cap), 0)
+    values = jnp.zeros((16, 4 * cap), jnp.float32)
+    for r, (res, up) in enumerate(((res0, up0), (res1, up1), (res2, up2), (res3, up3))):
+        here = res[...]
+        there = jnp.concatenate([here[0 : 3 * per], up[4 * per : 5 * per], here[4 * per :]], axis=0)
+        values = jnp.where((lane == r) & (line < 4 * per), jnp.where(end, there, here), values)
+    rows = info.shape[1]
+    chosen = jnp.where(info[2:3, :] == lax.broadcasted_iota(jnp.int32, (4 * cap, rows), 0), 1.0, 0.0)
+    spread = jnp.dot(values, chosen, precision=lax.Precision.HIGHEST, preferred_element_type=jnp.float32)
+    found = jnp.where(info[1:2, :] == lax.broadcasted_iota(jnp.int32, (16, rows), 0), spread, 0.0)
+    out[...] = jnp.log(jnp.sum(found, axis=0, keepdims=True) / block)
+
+
+def call(kernel, outs, scratch=(), **kw):
+    return pl.pallas_call(
+        kernel,
+        out_shape=outs,
+        scratch_shapes=list(scratch),
+        compiler_params=PARAMS,
+        **kw,
+    )
+
+
+def line_body(embeddings, probes, assigned, prior_counts, centroids, candidates, centroids2):
+    emb_rows, width = embeddings.shape
+    probe_count = probes.shape[1]
+    rows = centroids.shape[0]
+    per = BLOCKS2_DEV
+    cap = max(2, 3 * rows // (2 * per * 16))
+    part = per * cap
+    bf16, f32, i32 = jnp.bfloat16, jnp.float32, jnp.int32
+    shape = jax.ShapeDtypeStruct
+
+    def exchange(value, pairs):
+        return lax.ppermute(value, "shard", pairs)
+
+    near = [(i, i ^ 4) for i in range(16)]
+    cross = [(i, 12 - 4 * (i // 4) + i % 4) for i in range(4, 12)]
+    near_set = exchange(centroids2, near)
+    cross_set = exchange(centroids2, cross)
+    everyone = lax.all_gather(embeddings, "shard", axis=0, tiled=True)
+    aux = jnp.concatenate(
+        [probes.T, assigned[None, :], jnp.zeros((16 - probe_count - 1, emb_rows), i32)], axis=0
+    )
+    aux = lax.all_gather(aux, "shard", axis=0)
+    aux = jnp.transpose(aux, (1, 0, 2)).reshape(16, 16 * emb_rows)
+    cand_row = candidates.reshape(1, rows)
+    prior_row = prior_counts.reshape(1, rows)
+    far = shape((part + META, width), bf16)
+    main = shape((3 * part, width), bf16)
+    far0, far1, far2, far3, main1, main2, main3, info = call(
+        functools.partial(pack_kernel, cap, per),
+        (far, far, far, far, main, main, main, shape((8, rows), i32)),
+    )(cand_row, prior_row, centroids)
+
+    def beside(r):
+        return [(i, i ^ r) for i in range(16)]
+
+    far1, far2, far3 = (exchange(value, beside(r)) for r, value in ((1, far1), (2, far2), (3, far3)))
+    main1, main2, main3 = (exchange(value, beside(r)) for r, value in ((1, main1), (2, main2), (3, main3)))
+    last_set = exchange(near_set, cross)
+    passing = call(functools.partial(forward_kernel, part), shape((4 * part + META, width), bf16))(
+        far0, far1, far2, far3, cross_set
+    )
+    passed = exchange(passing, near)
+    scaled, share, new_centroids, counts, own_main = call(
+        functools.partial(first_kernel, part),
+        (
+            shape((16 * emb_rows, width), bf16),
+            shape((1, 16 * emb_rows), f32),
+            shape((rows, width), bf16),
+            shape((1, rows), i32),
+            main,
+        ),
+        [pltpu.VMEM((rows, width), bf16)],
+    )(everyone, aux, centroids, prior_row, info)
+    totals = lax.psum_scatter(share.reshape(-1), "shard", scatter_dimension=0, tiled=True)
+    density = jnp.log(totals / (probe_count * BLOCK))
+    result = call(
+        functools.partial(second_kernel, cap, per),
+        shape((16, 4 * cap), f32),
+        [pltpu.VMEM((5, per, 4 * cap, width), bf16), pltpu.VMEM((4, per * BLOCK2, width), bf16)],
+    )(
+        scaled, aux, own_main, far0, far1, far2, far3, main1, main2, main3,
+        centroids2, near_set, cross_set, passed, last_set,
+    )
+    beside_results = [result] + [exchange(result, beside(r)) for r in (1, 2, 3)]
+    passed_results = [exchange(result, [(i, i ^ 4 ^ r) for i in range(4, 12)]) for r in range(4)]
+    level_two = call(functools.partial(last_kernel, cap, per, BLOCK2), shape((1, rows), f32))(
+        info, *beside_results, *passed_results
+    )
+    return (density, new_centroids, counts.reshape(-1), level_two.reshape(-1))
+
+
 def solution(mesh):
     placed = (
         P(("groups", "shard"), None),
@@ -135,6 +406,7 @@
         P(("groups", "shard"), None),
         P(("groups", "shard"), None),
     )
+    body = line_body if mesh.shape["shard"] == 16 else general_body
     return jax.shard_map(
         body,
         mesh=mesh,

time: 185 us -> 155 us (0.84)
  blocking collectives: 0 us -> 72.6 us
  waiting for transfers between devices: 63.9 us -> 15.4 us
  local copies, waits for them, and re-layouts: 38.2 us -> 6.91 us
  other arithmetic: 28 us -> 0.68 us
  Pallas kernels: 0 us -> 24.8 us
  starting transfers between devices: 41.5 us -> 19.6 us
  between operations: 0.94 us -> 14.9 us
  matrix products: 11.8 us -> 0 us
    all_to_all x5 -> x0, waiting for transfers between devices: 63.9 us -> none  [the longest x1 48.6 us: body(): lax.all_to_all(send_two, 'shard', split_axis=0, concat_axis=0, tiled=True)]
    all_gather x0 -> x1, blocking collectives: none -> 42.5 us  [line_body(): aux = lax.all_gather(aux, 'shard', axis=0)]
    all_to_all x5 -> x0, starting transfers between devices: 41.5 us -> none  [the longest x1 15.4 us: body(): lax.all_to_all(jnp.stack(weights_two, axis=1), 'shard', split_axis=0, con...]
    unnamed x0 -> x1, blocking collectives: none -> 30.1 us
    pallas_call x0 -> x5, Pallas kernels: none -> 24.8 us  [the longest x1 11.1 us: line_body(): call(functools.partial(second_kernel, cap, per), shape((16, 4 * cap), f32...]
    ppermute x0 -> x17, starting transfers between devices: none -> 19.6 us  [exchange(): return lax.ppermute(value, 'shard', pairs)]
    another operation x8 -> x0, other arithmetic: 15.3 us -> none
    ppermute x0 -> x17, waiting for transfers between devices: none -> 14.7 us  [exchange(): return lax.ppermute(value, 'shard', pairs)]
  transfers between devices with their start and end apart: 5 -> 18, of which waited for: 4 -> 4; matrix products, arithmetic and copies ran while one was open for 29% -> 1% of each run, Pallas kernels for 0% -> 8%
where the time goes in v1:
time: 155 us
  blocking collectives  72.6 us (47%)
  Pallas kernels  24.8 us (16%)
  starting transfers between devices  19.6 us (13%)
  waiting for transfers between devices  15.4 us (10%)
  between operations  14.9 us (10%)
  local copies, waits for them, and re-layouts  6.91 us (4%)
    all_gather x1, blocking collectives, line_body(): aux = lax.all_gather(aux, 'shard', axis=0)  42.5 us
    unnamed x1, blocking collectives  30.1 us
    ppermute x17, starting transfers between devices, exchange(): return lax.ppermute(value, 'shard', pairs)  19.6 us
    ppermute x17, waiting for transfers between devices, exchange(): return lax.ppermute(value, 'shard', pairs)  14.7 us
    pallas_call x1, Pallas kernels, line_body(): call(functools.partial(second_kernel, cap, per), shape((16, 4 * cap), f32...  11.1 us
    unnamed x31, local copies, waits for them, and re-layouts  6.67 us
    pallas_call x1, Pallas kernels, line_body(): call(functools.partial(first_kernel, part), (shape((16 * emb_rows, width)...  6.52 us
    pallas_call x1, Pallas kernels, line_body(): call(functools.partial(pack_kernel, cap, per), (far, far, far, far, main,...  5.09 us
  transfers between devices with their start and end apart: 18, of which 4 were waited for; matrix products, arithmetic and copies ran while one was open for 1% of the time, Pallas kernels for 8%

profile of v1, /device:TPU:0, one launch (start us, length us, event | category | flops | bytes accessed | tf_op | source)
XLA Modules:
  0.0 154.8 jit_solution(16794004477333238192)
XLA Ops:
  7.2 0.0 all-gather.3.cloned.1.call-start
  7.2 0.7 all-gather.3.cloned.1.call-update
  7.9 0.7 collective-permute-start.7
  8.6 5.9 %collective-permute-start.6 = (bf16[384,1024]{1,0:T(8,128)(2,1)}, bf16[384,1024]{1,0:T(8,128)(2,1)}, u32[]{:S(2)}, u32[]{:S(2)}) collective-permute-start(bf16[384,1024]{1,0:T(8,128)(2,1)} %own_set.1), channel_id=1, source_target_pairs={{0,4},{1,5},{2,6},{3,7},{4,0},{5,1},{6,2},{7,3},{8,12},{9,13},{10,... | collective-permute-start | bytes 2359304 | tf_op jit(solution)/shard_map/ppermute | solution.py:339
  14.5 1.6 %copy-done = bf16[1024,1024]{1,0:T(8,128)(2,1)S(1)} copy-done((bf16[1024,1024]{1,0:T(8,128)(2,1)S(1)}, bf16[1024,1024]{1,0:T(8,128)(2,1)}, u32[]{:S(2)}) %copy-start) | copy-done | bytes 2097176
  16.1 0.7 copy-done.9
  16.8 0.7 copy-done.11
  17.5 5.1 %shard_map.102 = (bf16[112,1024]{1,0:T(8,128)(2,1)S(1)}, bf16[112,1024]{1,0:T(8,128)(2,1)S(1)}, bf16[112,1024]{1,0:T(8,128)(2,1)S(1)}, bf16[112,1024]{1,0:T(8,12...) custom-call(s32[1,1024]{1,0:T(1,128)S(1)} %bitcast.13, ...), custom_call_target="tpu_custom_call" | custom-call | tf_op jit(solution)/shard_map/pallas_call | solution.py:355
  22.6 0.0 collective-permute-start
  22.6 1.5 collective-permute-start.1
  24.1 0.3 collective-permute-start.2
  24.4 0.0 collective-permute-done.far1
  24.4 6.5 %collective-permute-done.1.far2 = bf16[112,1024]{1,0:T(8,128)(2,1)S(1)} collective-permute-done((bf16[112,1024]{1,0:T(8,128)(2,1)S(1)}, bf16[112,1024]{1,0:T(8,128)(2,1)S(1)}, u32[]{:S(2)}, u32[]{:S(2)}) %collective-permute-start.1) | collective-permute-done | bytes 229408 | tf_op jit(solution)/shard_map/ppermute | solution.py:339
  31.0 4.1 %collective-permute-done.2.far3 = bf16[112,1024]{1,0:T(8,128)(2,1)S(1)} collective-permute-done((bf16[112,1024]{1,0:T(8,128)(2,1)S(1)}, bf16[112,1024]{1,0:T(8,128)(2,1)S(1)}, u32[]{:S(2)}, u32[]{:S(2)}) %collective-permute-start.2) | collective-permute-done | bytes 229408 | tf_op jit(solution)/shard_map/ppermute | solution.py:339
  35.1 0.0 collective-permute-done.7.block.cross_set
  35.1 1.0 shard_map.104
  36.1 0.0 copy-done.6
  36.1 0.7 copy-done.4
  36.8 0.6 collective-permute-start.8
  37.4 0.0 collective-permute-done.6.near_set
  37.4 1.5 collective-permute-start.9
  38.9 0.0 collective-permute-start.3
  39.0 1.2 collective-permute-start.4
  40.2 0.6 collective-permute-start.5
  40.8 0.1 pad.2.clone
  40.9 0.0 copy-done.12
  40.9 0.0 copy-done.13
  40.9 0.1 add_add_fusion
  41.0 42.5 %all-gather = s32[256,40]{1,0:T(8,128)S(1)} all-gather(s32[16,40]{1,0:T(8,128)S(1)} %add_add_fusion), channel_id=2, replica_groups=mesh['groups'=2,'shard'=16] {'shard'}, dimensions={0}, use_global_device_ids=true | all-gather | bytes 43520 | tf_op jit(solution)/shard_map/all_gather | solution.py:349
  83.5 0.1 reshape.26.aux_ref
  83.6 0.0 all-gather.3.cloned.1.call-done.emb_ref
  83.6 0.0 copy-done.1
  83.6 0.0 copy-done.10
  83.7 0.0 copy-start.2
  83.7 1.3 copy-done.2
  85.0 6.5 %shard_map.103 = (bf16[640,1024]{1,0:T(8,128)(2,1)S(1)}, f32[1,640]{1,0:T(1,128)S(1)}, bf16[1024,1024]{1,0:T(8,128)(2,1)}, s32[1,1024]{1,0:T(1,128)}, bf16[288,1024]{1,0:T(8,128)(2,1)S(1)}) custom-call(bf16[640,1024]{1,0:T(8,128)(2,1)S(1)} %copy-done.2, s32[16,640]{1,0:T(8,128)S(1)} %reshape.26.aux_ref, bf16[1024,1024]{1,0:T(8,128)(2,1)S(1)} %copy-done.1, ...), custom_call_target="tpu_custom_call" | custom-call | tf_op jit(solution)/shard_map/pallas_call | solution.py:370
  91.5 1.1 copy-done.3
  92.6 0.0 collective-permute-done.3.main1
  92.6 0.0 collective-permute-done.4.main2
  92.6 0.0 collective-permute-done.5.main3
  92.6 0.0 collective-permute-done.9.last_set
  92.6 0.0 collective-permute-done.8.passed
  92.6 0.0 copy-done.5
  92.6 0.0 copy-done.7
  92.6 0.0 copy-start.14
  92.7 11.1 %shard_map.105.res0 = f32[16,128]{1,0:T(8,128)S(1)} custom-call(bf16[640,1024]{1,0:T(8,128)(2,1)} %copy-done.3, s32[16,640]{1,0:T(8,128)S(1)} %reshape.26.aux_ref, bf16[288,1024]{1,0:T(8,128)(2,1)S(1)} %get-tuple-element.22.own_main, bf16[112,1024]{1,0:T(8,128)(2,1)S(1)} %get-tuple-element.23.far0, bf16[112,1024]{1,0:T(8,128)(2,1)S(1)} %collective-permute-done.far1, ...), custom_call_target="tpu_custom_call" | custom-call | tf_op jit(solution)/shard_map/pallas_call | solution.py:383
  103.8 0.4 collective-permute-start.10
  104.2 0.0 collective-permute-start.11
  104.2 0.6 dynamic-slice
  105.4 1.6 %collective-permute-start.12 = (f32[16,128]{1,0:T(8,128)S(1)}, f32[16,128]{1,0:T(8,128)S(1)}, u32[]{:S(2)}, u32[]{:S(2)}) collective-permute-start(f32[16,128]{1,0:T(8,128)S(1)} %shard_map.105.res0), channel_id=1, source_target_pairs={{0,3},{1,2},{2,1},{3,0},{4,7},{5,6},{6,5},{7,4},{8,11},{9,10},{10,... | collective-permute-start | bytes 24584 | tf_op jit(solution)/shard_map/ppermute | solution.py:339
  107.0 1.3 collective-permute-start.13
  108.3 1.3 collective-permute-start.14
  109.6 30.1 %all-reduce = f32[640]{0:T(1024)S(1)} all-reduce(f32[640]{0:T(1024)S(1)} %reduce), channel_id=3, replica_groups=mesh['groups'=2,'shard'=16] {'shard'}, use_global_device_ids=true, to_apply=%region_0.0.clone | all-reduce | flops 640 | bytes 5120
  139.7 0.0 collective-permute-done.10.res1
  139.7 1.3 collective-permute-start.15
  141.0 0.0 collective-permute-done.11.res2
  141.0 1.3 collective-permute-start.16
  142.3 0.6 fusion
  142.9 0.0 collective-permute-done.12.res3
  142.9 0.0 collective-permute-done.13.up0
  142.9 0.0 collective-permute-done.14.up1
  143.0 3.2 %collective-permute-done.15.up2 = f32[16,128]{1,0:T(8,128)S(1)} collective-permute-done((f32[16,128]{1,0:T(8,128)S(1)}, f32[16,128]{1,0:T(8,128)S(1)}, u32[]{:S(2)}, u32[]{:S(2)}) %collective-permute-start.15) | collective-permute-done | bytes 8224 | tf_op jit(solution)/shard_map/ppermute | solution.py:339
  146.2 0.7 collective-permute-done.16.up3
  146.9 1.0 shard_map.106
  (18 shorter events, 0.1 us)
Async XLA Ops:
  7.2 76.5 %all-gather.3.cloned.1.call-start = ((), (), s32[]{:S(2)}) async-start(), calls=%async_computation | async-start | bytes 1392640 | tf_op jit(solution)/shard_map/all_gather | solution.py:345
  7.9 27.2 %collective-permute-start.7 = (bf16[384,1024]{1,0:T(8,128)(2,1)}, bf16[384,1024]{1,0:T(8,128)(2,1)S(1)}, u32[]{:S(2)}, u32[]{:S(2)}) collective-permute-start(bf16[384,1024]{1,0:T(8,128)(2,1)} %own_set.1), channel_id=1, source_target_pairs={{4,8},{5,9},{6,10},{7,11},{8,4},{9,5},{10,6},{11,7},{20,24},{21,25... | collective-permute-start | bytes 2359304 | tf_op jit(solution)/shard_map/ppermute | solution.py:339
  8.6 28.8 %collective-permute-start.6 = (bf16[384,1024]{1,0:T(8,128)(2,1)}, bf16[384,1024]{1,0:T(8,128)(2,1)}, u32[]{:S(2)}, u32[]{:S(2)}) collective-permute-start(bf16[384,1024]{1,0:T(8,128)(2,1)} %own_set.1), channel_id=1, source_target_pairs={{0,4},{1,5},{2,6},{3,7},{4,0},{5,1},{6,2},{7,3},{8,12},{9,13},{10,... | collective-permute-start | bytes 2359304 | tf_op jit(solution)/shard_map/ppermute | solution.py:339
  14.5 1.6 %copy-start = (bf16[1024,1024]{1,0:T(8,128)(2,1)S(1)}, bf16[1024,1024]{1,0:T(8,128)(2,1)}, u32[]{:S(2)}) copy-start(bf16[1024,1024]{1,0:T(8,128)(2,1)} %cent_ref.3) | copy-start | bytes 6291460
  16.1 0.7 copy-start.9
  16.8 0.7 copy-start.11
  17.5 23.4 %copy-start.12 = (s32[40,8]{0,1:T(8,128)S(1)}, s32[40,8]{0,1:T(8,128)}, u32[]{:S(2)}) copy-start(s32[40,8]{0,1:T(8,128)} %param.8) | copy-start | bytes 3844
  17.5 23.4 %copy-start.13 = (s32[40]{0:T(128)S(1)}, s32[40]{0:T(128)}, u32[]{:S(2)}) copy-start(s32[40]{0:T(128)} %param.9) | copy-start | bytes 484
  17.5 66.2 %copy-start.1 = (bf16[1024,1024]{1,0:T(8,128)(2,1)S(1)}, bf16[1024,1024]{1,0:T(8,128)(2,1)}, u32[]{:S(2)}) copy-start(bf16[1024,1024]{1,0:T(8,128)(2,1)} %cent_ref.3) | copy-start | bytes 6291460
  17.5 66.2 %copy-start.10 = (s32[1024]{0:T(1024)S(1)}, s32[1024]{0:T(1024)}, u32[]{:S(2)}) copy-start(s32[1024]{0:T(1024)} %param.10) | copy-start | bytes 12292
  22.6 1.9 %collective-permute-start = (bf16[112,1024]{1,0:T(8,128)(2,1)S(1)}, bf16[112,1024]{1,0:T(8,128)(2,1)S(1)}, u32[]{:S(2)}, u32[]{:S(2)}) collective-permute-start(bf16[112,1024]{1,0:T(8,128)(2,1)S(1)} %get-tuple-element.24), channel_id=1, source_target_pairs={{0,1},{1,0},{2,3},{3,2},{4,5},{5,4},{6,7},{7,6},{8,9},{9,8},{10,11... | collective-permute-start | bytes 688136 | tf_op jit(solution)/shard_map/ppermute | solution.py:339
  22.6 8.4 %collective-permute-start.1 = (bf16[112,1024]{1,0:T(8,128)(2,1)S(1)}, bf16[112,1024]{1,0:T(8,128)(2,1)S(1)}, u32[]{:S(2)}, u32[]{:S(2)}) collective-permute-start(bf16[112,1024]{1,0:T(8,128)(2,1)S(1)} %get-tuple-element.25), channel_id=1, source_target_pairs={{0,2},{1,3},{2,0},{3,1},{4,6},{5,7},{6,4},{7,5},{8,10},{9,11},{10,... | collective-permute-start | bytes 688136 | tf_op jit(solution)/shard_map/ppermute | solution.py:339
  24.1 11.0 %collective-permute-start.2 = (bf16[112,1024]{1,0:T(8,128)(2,1)S(1)}, bf16[112,1024]{1,0:T(8,128)(2,1)S(1)}, u32[]{:S(2)}, u32[]{:S(2)}) collective-permute-start(bf16[112,1024]{1,0:T(8,128)(2,1)S(1)} %get-tuple-element.26), channel_id=1, source_target_pairs={{0,3},{1,2},{2,1},{3,0},{4,7},{5,6},{6,5},{7,4},{8,11},{9,10},{10,... | collective-permute-start | bytes 688136 | tf_op jit(solution)/shard_map/ppermute | solution.py:339
  35.1 1.0 copy-start.6
  36.1 0.7 copy-start.4
  36.8 55.8 %collective-permute-start.8 = (bf16[400,1024]{1,0:T(8,128)(2,1)}, bf16[400,1024]{1,0:T(8,128)(2,1)}, u32[]{:S(2)}, u32[]{:S(2)}) collective-permute-start(bf16[400,1024]{1,0:T(8,128)(2,1)} %shard_map.104), channel_id=1, source_target_pairs={{0,4},{1,5},{2,6},{3,7},{4,0},{5,1},{6,2},{7,3},{8,12},{9,13},{10,... | collective-permute-start | bytes 2457608 | tf_op jit(solution)/shard_map/ppermute | solution.py:339
  37.4 55.2 %collective-permute-start.9 = (bf16[384,1024]{1,0:T(8,128)(2,1)}, bf16[384,1024]{1,0:T(8,128)(2,1)}, u32[]{:S(2)}, u32[]{:S(2)}) collective-permute-start(bf16[384,1024]{1,0:T(8,128)(2,1)} %collective-permute-done.6.near_set), channel_id=1, source_target_pairs={{4,8},{5,9},{6,10},{7,11},{8,4},{9,5},{10,6},{11,7},{20,24},{21,25... | collective-permute-start | bytes 2359304 | tf_op jit(solution)/shard_map/ppermute | solution.py:339
  38.9 53.6 %collective-permute-start.3 = (bf16[288,1024]{1,0:T(8,128)(2,1)}, bf16[288,1024]{1,0:T(8,128)(2,1)}, u32[]{:S(2)}, u32[]{:S(2)}) collective-permute-start(bf16[288,1024]{1,0:T(8,128)(2,1)} %get-tuple-element.27), channel_id=1, source_target_pairs={{0,1},{1,0},{2,3},{3,2},{4,5},{5,4},{6,7},{7,6},{8,9},{9,8},{10,11... | collective-permute-start | bytes 1769480 | tf_op jit(solution)/shard_map/ppermute | solution.py:339
  39.0 53.6 %collective-permute-start.4 = (bf16[288,1024]{1,0:T(8,128)(2,1)}, bf16[288,1024]{1,0:T(8,128)(2,1)}, u32[]{:S(2)}, u32[]{:S(2)}) collective-permute-start(bf16[288,1024]{1,0:T(8,128)(2,1)} %get-tuple-element.28), channel_id=1, source_target_pairs={{0,2},{1,3},{2,0},{3,1},{4,6},{5,7},{6,4},{7,5},{8,10},{9,11},{10,... | collective-permute-start | bytes 1769480 | tf_op jit(solution)/shard_map/ppermute | solution.py:339
  40.2 52.3 %collective-permute-start.5 = (bf16[288,1024]{1,0:T(8,128)(2,1)}, bf16[288,1024]{1,0:T(8,128)(2,1)}, u32[]{:S(2)}, u32[]{:S(2)}) collective-permute-start(bf16[288,1024]{1,0:T(8,128)(2,1)} %get-tuple-element.29), channel_id=1, source_target_pairs={{0,3},{1,2},{2,1},{3,0},{4,7},{5,6},{6,5},{7,4},{8,11},{9,10},{10,... | collective-permute-start | bytes 1769480 | tf_op jit(solution)/shard_map/ppermute | solution.py:339
  83.7 1.3 copy-start.2
  85.0 7.6 %copy-start.5 = (bf16[112,1024]{1,0:T(8,128)(2,1)S(1)}, bf16[112,1024]{1,0:T(8,128)(2,1)}, u32[]{:S(2)}) copy-start(bf16[112,1024]{1,0:T(8,128)(2,1)} %copy-done.4) | copy-start | bytes 688132
  85.0 7.7 %copy-start.7 = (bf16[112,1024]{1,0:T(8,128)(2,1)S(1)}, bf16[112,1024]{1,0:T(8,128)(2,1)}, u32[]{:S(2)}) copy-start(bf16[112,1024]{1,0:T(8,128)(2,1)} %copy-done.6) | copy-start | bytes 688132
  85.0 7.7 %copy-start.8 = (bf16[384,1024]{1,0:T(8,128)(2,1)S(1)}, bf16[384,1024]{1,0:T(8,128)(2,1)}, u32[]{:S(2)}) copy-start(bf16[384,1024]{1,0:T(8,128)(2,1)} %own_set.1) | copy-start | bytes 2359300
  91.5 1.1 copy-start.3
  92.6 11.5 %copy-start.14 = (u32[32]{0:T(128)S(1)}, u32[32]{0:T(128)}, u32[]{:S(2)}) copy-start(u32[32]{0:T(128)} %constant.10) | copy-start | bytes 388
  103.8 36.0 %collective-permute-start.10 = (f32[16,128]{1,0:T(8,128)S(1)}, f32[16,128]{1,0:T(8,128)S(1)}, u32[]{:S(2)}, u32[]{:S(2)}) collective-permute-start(f32[16,128]{1,0:T(8,128)S(1)} %shard_map.105.res0), channel_id=1, source_target_pairs={{0,1},{1,0},{2,3},{3,2},{4,5},{5,4},{6,7},{7,6},{8,9},{9,8},{10,11... | collective-permute-start | bytes 24584 | tf_op jit(solution)/shard_map/ppermute | solution.py:339
  104.2 36.8 %collective-permute-start.11 = (f32[16,128]{1,0:T(8,128)S(1)}, f32[16,128]{1,0:T(8,128)S(1)}, u32[]{:S(2)}, u32[]{:S(2)}) collective-permute-start(f32[16,128]{1,0:T(8,128)S(1)} %shard_map.105.res0), channel_id=1, source_target_pairs={{0,2},{1,3},{2,0},{3,1},{4,6},{5,7},{6,4},{7,5},{8,10},{9,11},{10,... | collective-permute-start | bytes 24584 | tf_op jit(solution)/shard_map/ppermute | solution.py:339
  105.4 37.5 %collective-permute-start.12 = (f32[16,128]{1,0:T(8,128)S(1)}, f32[16,128]{1,0:T(8,128)S(1)}, u32[]{:S(2)}, u32[]{:S(2)}) collective-permute-start(f32[16,128]{1,0:T(8,128)S(1)} %shard_map.105.res0), channel_id=1, source_target_pairs={{0,3},{1,2},{2,1},{3,0},{4,7},{5,6},{6,5},{7,4},{8,11},{9,10},{10,... | collective-permute-start | bytes 24584 | tf_op jit(solution)/shard_map/ppermute | solution.py:339
  107.0 35.9 %collective-permute-start.13 = (f32[16,128]{1,0:T(8,128)S(1)}, f32[16,128]{1,0:T(8,128)S(1)}, u32[]{:S(2)}, u32[]{:S(2)}) collective-permute-start(f32[16,128]{1,0:T(8,128)S(1)} %shard_map.105.res0), channel_id=1, source_target_pairs={{4,0},{5,1},{6,2},{7,3},{8,12},{9,13},{10,14},{11,15},{20,16},{21,... | collective-permute-start | bytes 24584 | tf_op jit(solution)/shard_map/ppermute | solution.py:339
  108.3 34.7 %collective-permute-start.14 = (f32[16,128]{1,0:T(8,128)S(1)}, f32[16,128]{1,0:T(8,128)S(1)}, u32[]{:S(2)}, u32[]{:S(2)}) collective-permute-start(f32[16,128]{1,0:T(8,128)S(1)} %shard_map.105.res0), channel_id=1, source_target_pairs={{4,1},{5,0},{6,3},{7,2},{8,13},{9,12},{10,15},{11,14},{20,17},{21,... | collective-permute-start | bytes 24584 | tf_op jit(solution)/shard_map/ppermute | solution.py:339
  139.7 6.4 %collective-permute-start.15 = (f32[16,128]{1,0:T(8,128)S(1)}, f32[16,128]{1,0:T(8,128)S(1)}, u32[]{:S(2)}, u32[]{:S(2)}) collective-permute-start(f32[16,128]{1,0:T(8,128)S(1)} %shard_map.105.res0), channel_id=1, source_target_pairs={{4,2},{5,3},{6,0},{7,1},{8,14},{9,15},{10,12},{11,13},{20,18},{21,... | collective-permute-start | bytes 24584 | tf_op jit(solution)/shard_map/ppermute | solution.py:339
  141.0 5.9 %collective-permute-start.16 = (f32[16,128]{1,0:T(8,128)S(1)}, f32[16,128]{1,0:T(8,128)S(1)}, u32[]{:S(2)}, u32[]{:S(2)}) collective-permute-start(f32[16,128]{1,0:T(8,128)S(1)} %shard_map.105.res0), channel_id=1, source_target_pairs={{4,3},{5,2},{6,1},{7,0},{8,15},{9,14},{10,13},{11,12},{20,19},{21,... | collective-permute-start | bytes 24584 | tf_op jit(solution)/shard_map/ppermute | solution.py:339
Sparse Core Ops, SparseCore 0:
  10.3 46.1 all-gather.2

commit v2 on v1

--- a/solution.py
+++ b/solution.py
@@ -175,8 +175,9 @@
     slot_far = jnp.where(plane == 3, rel * part + unit_slot, -1)
     slot_main = jnp.where(plane < 3, rel * 3 * part + plane * part + unit_slot, -1)
     info[0:1, :] = slot_main
-    info[1:2, :] = kind
-    info[2:3, :] = rel * cap + rank
+    kind = jnp.where((plane == 3) & ((z == 0) | (z == 3)), kind + per, kind)
+    info[1:2, :] = rel * 4 + (kind >> 2)
+    info[2:3, :] = (kind & 3) * cap + rank
     ident = lax.broadcasted_iota(jnp.int32, (1, rows), 1) + 1
     line = lax.broadcasted_iota(jnp.int32, (META, rows), 0)
     cent = cent_ref[...]
@@ -197,15 +198,18 @@
             ).astype(jnp.bfloat16)
 
 
-def first_kernel(part, emb_ref, aux_ref, cent_ref, prior_ref, info, scaled, share, fresh_rows, fresh_counts, own_main, units):
+def first_kernel(part, mine_ref, other_ref, cent_ref, prior_ref, info, scaled, facts, share, fresh_rows, fresh_counts, own_main, units):
     me, z, y, core = position()
-    count, width = emb_ref.shape
-    probe_count = 8
-    rows = cent_ref.shape[0]
-    scaled[...] = unit_wide(emb_ref[...].astype(jnp.float32))
-    probes = aux_ref[0:probe_count, :]
-    target = jnp.where(probes[0:1, :] == me, aux_ref[probe_count : probe_count + 1, :], -1)
-    member = jnp.sum((probes == me).astype(jnp.float32), axis=0, keepdims=True)
+    half = mine_ref.shape[0]
+    count = 2 * half
+    rows, width = cent_ref.shape
+    scaled[0:half, :] = unit_wide(mine_ref[:, 0:width].astype(jnp.float32))
+    scaled[half:count, :] = unit_wide(other_ref[:, 0:width].astype(jnp.float32))
+    aux = jnp.concatenate([mine_ref[:, width:], other_ref[:, width:]], axis=0).astype(jnp.float32)
+    aux = jnp.transpose(aux)[0:16, :].astype(jnp.int32)
+    facts[...] = aux
+    target = jnp.where(aux[0:1, :] == me, aux[8:9, :] * 32 + aux[9:10, :], -1)
+    member = jnp.sum((aux[0:8, :] == me).astype(jnp.float32), axis=0, keepdims=True)
     prior = column(prior_ref[...].astype(jnp.float32))
     step = 256
     total = jnp.zeros((1, count), jnp.float32)
@@ -224,31 +228,20 @@
             jnp.ones((8, count), jnp.bfloat16), hits, NT, preferred_element_type=jnp.float32
         )
         fresh_counts[0:1, start : start + step] = prior_ref[0:1, start : start + step] + gained_row[0:1, :].astype(jnp.int32)
-    share[...] = jnp.where(member > 0.0, total, 0.0)
+    piece = count // 16
+    lane = lax.broadcasted_iota(jnp.int32, (16, count), 1)
+    line = lax.broadcasted_iota(jnp.int32, (16, count), 0)
+    apart = jnp.where((member > 0.0) & (lane >= line * piece) & (lane < (line + 1) * piece), total, 0.0)
+    spot = lax.broadcasted_iota(jnp.int32, (count, 128), 0)
+    block = sum((spot >= piece * step).astype(jnp.int32) for step in range(1, 16))
+    together = jnp.where(spot - block * piece == lax.broadcasted_iota(jnp.int32, (count, 128), 1), 1.0, 0.0)
+    share[...] = jnp.dot(apart, together, precision=lax.Precision.HIGHEST, preferred_element_type=jnp.float32)
     pick = one_hot(info[0:1, :] == lax.broadcasted_iota(jnp.int32, (3 * part, rows), 0))
     own_main[...] = jnp.dot(pick, units[...], preferred_element_type=jnp.float32).astype(jnp.bfloat16)
 
 
-def forward_kernel(part, far0, far1, far2, far3, block, out):
-    me, z, y, core = position()
-    end = (z == 0) | (z == 3)
-
-    @pl.when(end)
-    def _():
-        facts = jnp.zeros((META, out.shape[1]), jnp.float32)
-        for r, far in enumerate((far0, far1, far2, far3)):
-            out[r * part : (r + 1) * part, :] = far[0:part, :]
-            facts = facts + far[part : part + META, :].astype(jnp.float32)
-        out[4 * part : 4 * part + META, :] = facts.astype(jnp.bfloat16)
-
-    @pl.when(jnp.logical_not(end))
-    def _():
-        out[0 : 4 * part, :] = block[...]
-        out[4 * part : 4 * part + META, :] = jnp.zeros((META, out.shape[1]), jnp.bfloat16)
-
-
 def second_kernel(
-    cap, per, scaled, aux_ref, own_main, far0, far1, far2, far3, main1, main2, main3,
+    cap, per, scaled, facts_in, share, own_main, far0, far1, far2, far3, main1, main2, main3, up0, up1, up2, up3,
     own_set, near_set, cross_set, passed, last_set, out, packed, two,
 ):
     me, z, y, core = position()
@@ -256,8 +249,8 @@
     part = per * cap
     block = own_set.shape[0] // per
     width = own_set.shape[1]
-    probe0 = aux_ref[0:1, :]
-    slots = aux_ref[8:9, :]
+    probe0 = facts_in[0:1, :]
+    slots = facts_in[8:9, :] * 32 + facts_in[9:10, :]
 
     def place(w, r, rows):
         for j in range(per):
@@ -273,46 +266,75 @@
         updated = (ahead * raw.astype(jnp.float32) + sums) / jnp.maximum(ahead + gained, 1.0)
         return unit_wide(updated)
 
-    def facts_of(ref, row, r, first):
-        lines = ref[row : row + META, :].astype(jnp.float32)
+    def facts_of(ref, r, first):
+        lines = ref[part : part + META, :].astype(jnp.float32)
         return lines[4 * r : 4 * r + 4, first : first + part]
 
     for w in range(3):
         place(w, 0, own_main[w * part : (w + 1) * part, :])
-    for r, (far, main) in enumerate(((far0, None), (far1, main1), (far2, main2), (far3, main3))):
-        source = me ^ r
-        place(3, r, corrected(far[0:part, :], facts_of(far, part, r, 0), source))
+    rows_of = ((far0, None, up0), (far1, main1, up1), (far2, main2, up2), (far3, main3, up3))
+    for r, (far, main, up) in enumerate(rows_of):
         if main is not None:
             for w in range(3):
-                place(w, r, corrected(main[w * part : (w + 1) * part, :], facts_of(far, part, r, 128 + w * part), source))
-        place(4, r, corrected(passed[r * part : (r + 1) * part, :], facts_of(passed, 4 * part, r, 0), me ^ 4 ^ r))
+                place(w, r, corrected(main[w * part : (w + 1) * part, :], facts_of(far, r, 128 + w * part), me ^ r))
+
+    @pl.when(jnp.logical_not(end))
+    def _():
+        for r, (far, main, up) in enumerate(rows_of):
+            place(3, r, corrected(far[0:part, :], facts_of(far, r, 0), me ^ r))
+            place(4, r, corrected(up[0:part, :], facts_of(up, r, 0), me ^ 4 ^ r))
+
     two[0] = unit_wide(jnp.where(end, own_set[...], near_set[...]).astype(jnp.float32))
     two[1] = unit_wide(jnp.where(end, near_set[...], own_set[...]).astype(jnp.float32))
-    two[2] = unit_wide(jnp.where(end, passed[0 : 4 * part, :], cross_set[...]).astype(jnp.float32))
+    two[2] = unit_wide(jnp.where(end, passed[...], cross_set[...]).astype(jnp.float32))
     two[3] = unit_wide(last_set[...].astype(jnp.float32))
+    lines = []
     for w in range(5):
         for j in range(per):
             scores = lax.dot_general(
                 two[min(w, 3), j * block : (j + 1) * block, :], packed[w, j], NT, preferred_element_type=jnp.float32
             )
-            out[w * per + j : w * per + j + 1, :] = jnp.sum(weights(scores, width), axis=0, keepdims=True)
-
-
-def last_kernel(cap, per, block, info, res0, res1, res2, res3, up0, up1, up2, up3, out):
+            line = jnp.sum(weights(scores, width), axis=0, keepdims=True)
+            lines.append(line if w < 3 else jnp.where(end, 0.0, line))
+    lines.append(jnp.zeros((1, 4 * cap), jnp.float32))
+    sums = jnp.concatenate(lines, axis=0)
+    lane = lax.broadcasted_iota(jnp.int32, sums.shape, 1)
+    line = lax.broadcasted_iota(jnp.int32, sums.shape, 0)
+    out[...] = jnp.zeros(out.shape, jnp.float32)
+    for r in range(4):
+        spread = jnp.zeros_like(sums)
+        for s in range(4):
+            turned = sums if s == r else pltpu.roll(sums, ((s - r) % 4) * cap, 1)
+            spread = jnp.where((line % 4 == s) & (lane >= s * cap) & (lane < (s + 1) * cap), turned, spread)
+        tile = jnp.concatenate(
+            [jnp.sum(spread[4 * t : 4 * t + 4], axis=0, keepdims=True) for t in range(4)], axis=0
+        )
+        out[me ^ r, 0:4, :] = tile
+        out[me ^ 4 ^ r, 0:4, :] = tile
+    for b in range(16):
+        apart = (b >> 3) | ((b >> 1) & 2) | ((b & 3) << 2)
+        out[me ^ apart, 4:5, :] = share[b : b + 1, :]
+
+
+def last_kernel(cap, scale_one, scale_two, info, got, density, level_two):
     me, z, y, core = position()
     end = (z == 0) | (z == 3)
-    lane = lax.broadcasted_iota(jnp.int32, (16, 4 * cap), 1) // cap
-    line = lax.broadcasted_iota(jnp.int32, (16, 4 * cap), 0)
-    values = jnp.zeros((16, 4 * cap), jnp.float32)
-    for r, (res, up) in enumerate(((res0, up0), (res1, up1), (res2, up2), (res3, up3))):
-        here = res[...]
-        there = jnp.concatenate([here[0 : 3 * per], up[4 * per : 5 * per], here[4 * per :]], axis=0)
-        values = jnp.where((lane == r) & (line < 4 * per), jnp.where(end, there, here), values)
+    pieces = []
+    total = jnp.zeros((1, 4 * cap), jnp.float32)
+    for source in range(16):
+        total = total + got[source, 4:5, :]
+    density[...] = jnp.log(total[:, 0 : density.shape[1]] / scale_one)
+    for r in range(4):
+        here = got[me ^ r]
+        there = got[me ^ 4 ^ r]
+        pieces.append(here[0:3])
+        pieces.append(jnp.where(end, there[3:4], here[3:4]))
+    values = jnp.concatenate(pieces, axis=0)
     rows = info.shape[1]
     chosen = jnp.where(info[2:3, :] == lax.broadcasted_iota(jnp.int32, (4 * cap, rows), 0), 1.0, 0.0)
     spread = jnp.dot(values, chosen, precision=lax.Precision.HIGHEST, preferred_element_type=jnp.float32)
     found = jnp.where(info[1:2, :] == lax.broadcasted_iota(jnp.int32, (16, rows), 0), spread, 0.0)
-    out[...] = jnp.log(jnp.sum(found, axis=0, keepdims=True) / block)
+    level_two[...] = jnp.log(jnp.sum(found, axis=0, keepdims=True) / scale_two)
 
 
 def call(kernel, outs, scratch=(), **kw):
@@ -335,19 +357,17 @@
     bf16, f32, i32 = jnp.bfloat16, jnp.float32, jnp.int32
     shape = jax.ShapeDtypeStruct
 
-    def exchange(value, pairs):
-        return lax.ppermute(value, "shard", pairs)
-
-    near = [(i, i ^ 4) for i in range(16)]
-    cross = [(i, 12 - 4 * (i // 4) + i % 4) for i in range(4, 12)]
-    near_set = exchange(centroids2, near)
-    cross_set = exchange(centroids2, cross)
-    everyone = lax.all_gather(embeddings, "shard", axis=0, tiled=True)
-    aux = jnp.concatenate(
-        [probes.T, assigned[None, :], jnp.zeros((16 - probe_count - 1, emb_rows), i32)], axis=0
-    )
-    aux = lax.all_gather(aux, "shard", axis=0)
-    aux = jnp.transpose(aux, (1, 0, 2)).reshape(16, 16 * emb_rows)
+    def exchange(value, apart, sources=range(16)):
+        return lax.ppermute(value, "shard", [(i, i ^ apart) for i in sources])
+
+    mids, ends = range(4, 12), (*range(4), *range(12, 16))
+    facts = jnp.concatenate([probes, (assigned >> 5)[:, None], (assigned & 31)[:, None]], axis=1).astype(bf16)
+    mine = jnp.concatenate([embeddings, jnp.pad(facts, ((0, 0), (0, 118)))], axis=1)
+    mine = jnp.concatenate([mine] + [exchange(mine, apart) for apart in (4, 8, 12)], axis=0)
+    mine = jnp.concatenate([mine, exchange(mine, 2)], axis=0)
+    other = exchange(mine, 1)
+    near_set = exchange(centroids2, 4)
+    cross_set = exchange(centroids2, 12, mids)
     cand_row = candidates.reshape(1, rows)
     prior_row = prior_counts.reshape(1, rows)
     far = shape((part + META, width), bf16)
@@ -356,44 +376,36 @@
         functools.partial(pack_kernel, cap, per),
         (far, far, far, far, main, main, main, shape((8, rows), i32)),
     )(cand_row, prior_row, centroids)
-
-    def beside(r):
-        return [(i, i ^ r) for i in range(16)]
-
-    far1, far2, far3 = (exchange(value, beside(r)) for r, value in ((1, far1), (2, far2), (3, far3)))
-    main1, main2, main3 = (exchange(value, beside(r)) for r, value in ((1, main1), (2, main2), (3, main3)))
-    last_set = exchange(near_set, cross)
-    passing = call(functools.partial(forward_kernel, part), shape((4 * part + META, width), bf16))(
-        far0, far1, far2, far3, cross_set
-    )
-    passed = exchange(passing, near)
-    scaled, share, new_centroids, counts, own_main = call(
+    main2, main3, main1 = exchange(main2, 2), exchange(main3, 3), exchange(main1, 1)
+    up = [exchange(value, 4 ^ r, ends) for r, value in enumerate((far0, far1, far2, far3))]
+    far2, far3, far1 = exchange(far2, 2), exchange(far3, 3), exchange(far1, 1)
+    passed = exchange(cross_set, 4, mids)
+    last_set = exchange(near_set, 12, mids)
+    scaled, facts, share, new_centroids, counts, own_main = call(
         functools.partial(first_kernel, part),
         (
             shape((16 * emb_rows, width), bf16),
-            shape((1, 16 * emb_rows), f32),
+            shape((16, 16 * emb_rows), i32),
+            shape((16, 4 * cap), f32),
             shape((rows, width), bf16),
             shape((1, rows), i32),
             main,
         ),
         [pltpu.VMEM((rows, width), bf16)],
-    )(everyone, aux, centroids, prior_row, info)
-    totals = lax.psum_scatter(share.reshape(-1), "shard", scatter_dimension=0, tiled=True)
-    density = jnp.log(totals / (probe_count * BLOCK))
-    result = call(
+    )(mine, other, centroids, prior_row, info)
+    results = call(
         functools.partial(second_kernel, cap, per),
-        shape((16, 4 * cap), f32),
+        shape((16, 8, 4 * cap), f32),
         [pltpu.VMEM((5, per, 4 * cap, width), bf16), pltpu.VMEM((4, per * BLOCK2, width), bf16)],
     )(
-        scaled, aux, own_main, far0, far1, far2, far3, main1, main2, main3,
+        scaled, facts, share, own_main, far0, far1, far2, far3, main1, main2, main3, *up,
         centroids2, near_set, cross_set, passed, last_set,
     )
-    beside_results = [result] + [exchange(result, beside(r)) for r in (1, 2, 3)]
-    passed_results = [exchange(result, [(i, i ^ 4 ^ r) for i in range(4, 12)]) for r in range(4)]
-    level_two = call(functools.partial(last_kernel, cap, per, BLOCK2), shape((1, rows), f32))(
-        info, *beside_results, *passed_results
-    )
-    return (density, new_centroids, counts.reshape(-1), level_two.reshape(-1))
+    results = lax.all_to_all(results, "shard", split_axis=0, concat_axis=0, tiled=True)
+    density, level_two = call(
+        functools.partial(last_kernel, cap, probe_count * BLOCK, BLOCK2), (shape((1, emb_rows), f32), shape((1, rows), f32))
+    )(info, results)
+    return (density.reshape(-1), new_centroids, counts.reshape(-1), level_two.reshape(-1))
 
 
 def solution(mesh):

time: 155 us -> 112 us (0.72)
  blocking collectives: 72.6 us -> 15.6 us
  waiting for transfers between devices: 15.4 us -> 37.4 us
  between operations: 14.9 us -> 0.85 us
  starting transfers between devices: 19.6 us -> 30.9 us
  Pallas kernels: 24.8 us -> 19.5 us
  other arithmetic: 0.68 us -> 2.33 us
    all_gather x1 -> x0, blocking collectives: 42.5 us -> none  [line_body(): aux = lax.all_gather(aux, 'shard', axis=0)]
    unnamed x1 -> x0, blocking collectives: 30.1 us -> none
    ppermute x17 -> x19, waiting for transfers between devices: 14.7 us -> 37.4 us  [exchange(): return lax.ppermute(value, 'shard', [(i, i ^ apart) for i in sources])]
    all_to_all x0 -> x1, blocking collectives: none -> 15.6 us  [line_body(): lax.all_to_all(results, 'shard', split_axis=0, concat_axis=0, tiled=True)]
    ppermute x17 -> x19, starting transfers between devices: 19.6 us -> 30.9 us  [exchange(): return lax.ppermute(value, 'shard', [(i, i ^ apart) for i in sources])]
    pallas_call x3 -> x2, Pallas kernels: 13.2 us -> 8.8 us  [the longest x1 7.77 us: line_body(): call(functools.partial(second_kernel, cap, per), shape((16, 8, 4 * cap),...]
    unnamed x31 -> x23, local copies, waits for them, and re-layouts: 6.67 us -> 5.22 us
  transfers between devices with their start and end apart: 18 -> 19, of which waited for: 4 -> 7; matrix products, arithmetic and copies ran while one was open for 1% -> 0% of each run, Pallas kernels for 8% -> 10%
where the time goes in v2:
time: 112 us
  waiting for transfers between devices  37.4 us (33%)
  starting transfers between devices  30.9 us (28%)
  Pallas kernels  19.5 us (17%)
  blocking collectives  15.6 us (14%)
  local copies, waits for them, and re-layouts  5.37 us (5%)
  other arithmetic  2.33 us (2%)
    ppermute x19, waiting for transfers between devices, exchange(): return lax.ppermute(value, 'shard', [(i, i ^ apart) for i in sources])  37.4 us
    ppermute x19, starting transfers between devices, exchange(): return lax.ppermute(value, 'shard', [(i, i ^ apart) for i in sources])  30.9 us
    all_to_all x1, blocking collectives, line_body(): lax.all_to_all(results, 'shard', split_axis=0, concat_axis=0, tiled=True)  15.6 us
    pallas_call x1, Pallas kernels, line_body(): call(functools.partial(second_kernel, cap, per), shape((16, 8, 4 * cap),...  7.77 us
    pallas_call x1, Pallas kernels, line_body(): call(functools.partial(first_kernel, part), (shape((16 * emb_rows, width)...  6.47 us
    unnamed x23, local copies, waits for them, and re-layouts  5.22 us
    pallas_call x1, Pallas kernels, line_body(): call(functools.partial(pack_kernel, cap, per), (far, far, far, far, main,...  4.25 us
  transfers between devices with their start and end apart: 19, of which 7 were waited for; matrix products, arithmetic and copies ran while one was open for 0% of the time, Pallas kernels for 10%

profile of v2, /device:TPU:0, one launch (start us, length us, event | category | flops | bytes accessed | tf_op | source)
XLA Modules:
  0.0 111.9 jit_solution(11211151049148217404)
XLA Ops:
  0.6 0.0 copy-start.9
  0.6 0.7 convert_bitcast_fusion.1
  1.3 0.7 convert.11
  2.0 0.1 copy.14
  2.2 0.9 pad_maximum_fusion.1
  3.1 3.1 %collective-permute-start = (bf16[40,1152]{1,0:T(8,128)(2,1)S(1)}, bf16[40,1152]{1,0:T(8,128)(2,1)S(1)}, u32[]{:S(2)}, u32[]{:S(2)}) collective-permute-start(bf16[40,1152]{1,0:T(8,128)(2,1)S(1)} %get-tuple-element.36), channel_id=1, source_target_pairs={{0,4},{1,5},{2,6},{3,7},{4,0},{5,1},{6,2},{7,3},{8,12},{9,13},{10,... | collective-permute-start | bytes 276488 | tf_op jit(solution)/shard_map/ppermute | solution.py:361
  6.1 2.6 %collective-permute-start.1 = (bf16[40,1152]{1,0:T(8,128)(2,1)S(1)}, bf16[40,1152]{1,0:T(8,128)(2,1)S(1)}, u32[]{:S(2)}, u32[]{:S(2)}) collective-permute-start(bf16[40,1152]{1,0:T(8,128)(2,1)S(1)} %get-tuple-element.36), channel_id=1, source_target_pairs={{0,8},{1,9},{2,10},{3,11},{4,12},{5,13},{6,14},{7,15},{8,0},{9,1},... | collective-permute-start | bytes 276488 | tf_op jit(solution)/shard_map/ppermute | solution.py:361
  8.7 0.0 collective-permute-start.2
  8.7 0.7 collective-permute-start.16
  9.4 3.7 %collective-permute-start.15 = (bf16[384,1024]{1,0:T(8,128)(2,1)}, bf16[384,1024]{1,0:T(8,128)(2,1)S(1)}, u32[]{:S(2)}, u32[]{:S(2)}) collective-permute-start(bf16[384,1024]{1,0:T(8,128)(2,1)} %own_set.1), channel_id=1, source_target_pairs={{0,4},{1,5},{2,6},{3,7},{4,0},{5,1},{6,2},{7,3},{8,12},{9,13},{10,... | collective-permute-start | bytes 2359304 | tf_op jit(solution)/shard_map/ppermute | solution.py:361
  13.2 0.0 copy-start
  13.2 1.6 %copy-done = bf16[1024,1024]{1,0:T(8,128)(2,1)S(1)} copy-done((bf16[1024,1024]{1,0:T(8,128)(2,1)S(1)}, bf16[1024,1024]{1,0:T(8,128)(2,1)}, u32[]{:S(2)}) %copy-start) | copy-done | bytes 2097176
  14.8 0.0 copy-start.4
  14.8 0.7 copy-done.4
  15.5 0.7 copy-done.5
  16.2 0.0 copy-start.1
  16.2 4.2 %shard_map.102 = (bf16[112,1024]{1,0:T(8,128)(2,1)S(1)}, bf16[112,1024]{1,0:T(8,128)(2,1)S(1)}, bf16[112,1024]{1,0:T(8,128)(2,1)S(1)}, bf16[112,1024]{1,0:T(8,12...) custom-call(s32[1,1024]{1,0:T(1,128)S(1)} %bitcast.11, ...), custom_call_target="tpu_custom_call" | custom-call | tf_op jit(solution)/shard_map/pallas_call | solution.py:375
  20.4 0.0 collective-permute-done
  20.4 1.9 %collective-permute-start.11 = (bf16[112,1024]{1,0:T(8,128)(2,1)S(1)}, bf16[112,1024]{1,0:T(8,128)(2,1)S(1)}, u32[]{:S(2)}, u32[]{:S(2)}) collective-permute-start(bf16[112,1024]{1,0:T(8,128)(2,1)S(1)} %get-tuple-element.25.far0), channel_id=1, source_target_pairs={{0,4},{1,5},{2,6},{3,7},{12,8},{13,9},{14,10},{15,11},{16,20},{17,... | collective-permute-start | bytes 688136 | tf_op jit(solution)/shard_map/ppermute | solution.py:361
  22.3 0.0 collective-permute-done.1
  22.3 0.0 collective-permute-done.2
  22.4 0.0 copy-done.9
  22.4 1.6 %collective-permute-start.3 = (bf16[160,1152]{1,0:T(8,128)(2,1)S(1)}, bf16[160,1152]{1,0:T(8,128)(2,1)S(1)}, u32[]{:S(2)}, u32[]{:S(2)}) collective-permute-start(bf16[160,1152]{1,0:T(8,128)(2,1)S(1)} %pad_maximum_fusion), channel_id=1, source_target_pairs={{0,2},{1,3},{2,0},{3,1},{4,6},{5,7},{6,4},{7,5},{8,10},{9,11},{10,... | collective-permute-start | bytes 1105928 | tf_op jit(solution)/shard_map/ppermute | solution.py:361
  24.1 0.0 copy-start.3
  24.1 7.3 %collective-permute-done.3 = bf16[160,1152]{1,0:T(8,128)(2,1)S(1)} collective-permute-done((bf16[160,1152]{1,0:T(8,128)(2,1)S(1)}, bf16[160,1152]{1,0:T(8,128)(2,1)S(1)}, u32[]{:S(2)}, u32[]{:S(2)}) %collective-permute-start.3) | collective-permute-done | bytes 368672 | tf_op jit(solution)/shard_map/ppermute | solution.py:361
  31.4 0.1 collective-permute-start.4
  31.5 1.7 %collective-permute-start.12 = (bf16[112,1024]{1,0:T(8,128)(2,1)S(1)}, bf16[112,1024]{1,0:T(8,128)(2,1)S(1)}, u32[]{:S(2)}, u32[]{:S(2)}) collective-permute-start(bf16[112,1024]{1,0:T(8,128)(2,1)S(1)} %get-tuple-element.26), channel_id=1, source_target_pairs={{0,5},{1,4},{2,7},{3,6},{12,9},{13,8},{14,11},{15,10},{16,21},{17,... | collective-permute-start | bytes 688136 | tf_op jit(solution)/shard_map/ppermute | solution.py:361
  33.2 1.4 %collective-permute-done.11.up0 = bf16[112,1024]{1,0:T(8,128)(2,1)S(1)} collective-permute-done((bf16[112,1024]{1,0:T(8,128)(2,1)S(1)}, bf16[112,1024]{1,0:T(8,128)(2,1)S(1)}, u32[]{:S(2)}, u32[]{:S(2)}) %collective-permute-start.11) | collective-permute-done | bytes 229408 | tf_op jit(solution)/shard_map/ppermute | solution.py:361
  34.6 5.3 %collective-permute-start.13 = (bf16[112,1024]{1,0:T(8,128)(2,1)S(1)}, bf16[112,1024]{1,0:T(8,128)(2,1)S(1)}, u32[]{:S(2)}, u32[]{:S(2)}) collective-permute-start(bf16[112,1024]{1,0:T(8,128)(2,1)S(1)} %get-tuple-element.27), channel_id=1, source_target_pairs={{0,6},{1,7},{2,4},{3,5},{12,10},{13,11},{14,8},{15,9},{16,22},{17,... | collective-permute-start | bytes 688136 | tf_op jit(solution)/shard_map/ppermute | solution.py:361
  39.9 0.0 collective-permute-done.12.up1
  40.0 4.3 %collective-permute-start.14 = (bf16[112,1024]{1,0:T(8,128)(2,1)S(1)}, bf16[112,1024]{1,0:T(8,128)(2,1)S(1)}, u32[]{:S(2)}, u32[]{:S(2)}) collective-permute-start(bf16[112,1024]{1,0:T(8,128)(2,1)S(1)} %get-tuple-element.28), channel_id=1, source_target_pairs={{0,7},{1,6},{2,5},{3,4},{12,11},{13,10},{14,9},{15,8},{16,23},{17,... | collective-permute-start | bytes 688136 | tf_op jit(solution)/shard_map/ppermute | solution.py:361
  44.3 0.0 collective-permute-done.13.up2
  44.3 0.1 collective-permute-start.5
  44.4 5.0 %collective-permute-done.14.up3 = bf16[112,1024]{1,0:T(8,128)(2,1)S(1)} collective-permute-done((bf16[112,1024]{1,0:T(8,128)(2,1)S(1)}, bf16[112,1024]{1,0:T(8,128)(2,1)S(1)}, u32[]{:S(2)}, u32[]{:S(2)}) %collective-permute-start.14) | collective-permute-done | bytes 229408 | tf_op jit(solution)/shard_map/ppermute | solution.py:361
  49.4 1.0 collective-permute-start.6
  50.4 0.0 collective-permute-done.5.far1
  50.4 0.0 collective-permute-start.7
  50.4 0.0 collective-permute-done.16.cross_set
  50.4 0.0 copy-start.6
  50.5 1.3 %collective-permute-start.17 = (bf16[384,1024]{1,0:T(8,128)(2,1)S(1)}, bf16[384,1024]{1,0:T(8,128)(2,1)S(1)}, u32[]{:S(2)}, u32[]{:S(2)}) collective-permute-start(bf16[384,1024]{1,0:T(8,128)(2,1)S(1)} %collective-permute-done.16.cross_set), channel_id=1, source_target_pairs={{4,0},{5,1},{6,2},{7,3},{8,12},{9,13},{10,14},{11,15},{20,16},{21,... | collective-permute-start | bytes 2359304 | tf_op jit(solution)/shard_map/ppermute | solution.py:361
  51.8 0.0 collective-permute-done.15.near_set
  51.8 0.9 collective-permute-start.18
  52.7 5.3 %collective-permute-done.6.far2 = bf16[112,1024]{1,0:T(8,128)(2,1)S(1)} collective-permute-done((bf16[112,1024]{1,0:T(8,128)(2,1)S(1)}, bf16[112,1024]{1,0:T(8,128)(2,1)S(1)}, u32[]{:S(2)}, u32[]{:S(2)}) %collective-permute-start.6) | collective-permute-done | bytes 229408 | tf_op jit(solution)/shard_map/ppermute | solution.py:361
  57.9 0.0 collective-permute-start.10
  57.9 2.6 %collective-permute-done.7.far3 = bf16[112,1024]{1,0:T(8,128)(2,1)S(1)} collective-permute-done((bf16[112,1024]{1,0:T(8,128)(2,1)S(1)}, bf16[112,1024]{1,0:T(8,128)(2,1)S(1)}, u32[]{:S(2)}, u32[]{:S(2)}) %collective-permute-start.7) | collective-permute-done | bytes 229408 | tf_op jit(solution)/shard_map/ppermute | solution.py:361
  60.5 0.8 collective-permute-start.8
  61.3 0.0 collective-permute-done.4.other_ref
  61.3 1.8 %collective-permute-start.9 = (bf16[288,1024]{1,0:T(8,128)(2,1)S(1)}, bf16[288,1024]{1,0:T(8,128)(2,1)S(1)}, u32[]{:S(2)}, u32[]{:S(2)}) collective-permute-start(bf16[288,1024]{1,0:T(8,128)(2,1)S(1)} %get-tuple-element.30), channel_id=1, source_target_pairs={{0,2},{1,3},{2,0},{3,1},{4,6},{5,7},{6,4},{7,5},{8,10},{9,11},{10,... | collective-permute-start | bytes 1769480 | tf_op jit(solution)/shard_map/ppermute | solution.py:361
  63.1 0.0 copy-done.1
  63.1 6.5 %shard_map.103 = (bf16[640,1024]{1,0:T(8,128)(2,1)S(1)}, s32[16,640]{1,0:T(8,128)S(1)}, f32[16,128]{1,0:T(8,128)S(1)}, bf16[1024,1024]{1,0:T(8,128)(2,1)}, s32[1...) custom-call(bf16[320,1152]{1,0:T(8,128)(2,1)S(1)} %constant_dynamic-update-slice_fusion.mine_ref, ...), custom_call_target="tpu_custom_call" | custom-call | tf_op jit(solution)/shard_map/pallas_call | solution.py:384
  69.6 1.1 copy-done.2
  70.7 2.9 %collective-permute-done.10.main3 = bf16[288,1024]{1,0:T(8,128)(2,1)S(1)} collective-permute-done((bf16[288,1024]{1,0:T(8,128)(2,1)S(1)}, bf16[288,1024]{1,0:T(8,128)(2,1)S(1)}, u32[]{:S(2)}, u32[]{:S(2)}) %collective-permute-start.10) | collective-permute-done | bytes 589856 | tf_op jit(solution)/shard_map/ppermute | solution.py:361
  73.6 0.0 collective-permute-done.8.main1
  73.6 12.8 %collective-permute-done.9.main2 = bf16[288,1024]{1,0:T(8,128)(2,1)S(1)} collective-permute-done((bf16[288,1024]{1,0:T(8,128)(2,1)S(1)}, bf16[288,1024]{1,0:T(8,128)(2,1)S(1)}, u32[]{:S(2)}, u32[]{:S(2)}) %collective-permute-start.9) | collective-permute-done | bytes 589856 | tf_op jit(solution)/shard_map/ppermute | solution.py:361
  86.4 0.0 collective-permute-done.17.passed
  86.4 0.0 collective-permute-done.18.last_set
  86.4 0.0 copy-start.8
  86.4 0.0 copy-done.6
  86.4 0.9 copy-done.7
  87.3 0.3 copy-done.8
  87.5 0.0 copy-done.3
  87.5 7.8 %shard_map.104 = f32[16,8,128]{2,1,0:T(8,128)S(1)} custom-call(bf16[640,1024]{1,0:T(8,128)(2,1)} %copy-done.2, s32[16,640]{1,0:T(8,128)S(1)} %get-tuple-element.22.facts_in, f32[16,128]{1,0:T(8,128)S(1)} %get-tuple-element.23.share, bf16[288,1024]{1,0:T(8,128)(2,1)S(1)} %get-tuple-element.24.own_main, bf16[112,1024]{1,0:T(8,128)(2,1)S(1)} %get-tuple-element.25.far0, ...), custom_call_target="tpu_custom_call" | custom-call | tf_op jit(solution)/shard_map/pallas_call | solution.py:396
  95.3 15.6 %all_to_all.5.got = f32[16,8,128]{2,1,0:T(8,128)S(1)} all-to-all(f32[16,8,128]{2,1,0:T(8,128)S(1)} %shard_map.104), channel_id=1, replica_groups=mesh['groups'=2,'shard'=16] {'shard'}, dimensions={0} | all-to-all | bytes 131072 | tf_op jit(solution)/shard_map/all_to_all | solution.py:404
  110.9 1.0 shard_map.105
  (10 shorter events, 0.1 us)
Async XLA Ops:
  0.6 21.7 %copy-start.9 = (bf16[40,1024]{1,0:T(8,128)(2,1)S(1)}, bf16[40,1024]{1,0:T(8,128)(2,1)}, u32[]{:S(2)}) copy-start(bf16[40,1024]{1,0:T(8,128)(2,1)} %param.7) | copy-start | bytes 245764
  3.1 17.3 %collective-permute-start = (bf16[40,1152]{1,0:T(8,128)(2,1)S(1)}, bf16[40,1152]{1,0:T(8,128)(2,1)S(1)}, u32[]{:S(2)}, u32[]{:S(2)}) collective-permute-start(bf16[40,1152]{1,0:T(8,128)(2,1)S(1)} %get-tuple-element.36), channel_id=1, source_target_pairs={{0,4},{1,5},{2,6},{3,7},{4,0},{5,1},{6,2},{7,3},{8,12},{9,13},{10,... | collective-permute-start | bytes 276488 | tf_op jit(solution)/shard_map/ppermute | solution.py:361
  6.1 16.2 %collective-permute-start.1 = (bf16[40,1152]{1,0:T(8,128)(2,1)S(1)}, bf16[40,1152]{1,0:T(8,128)(2,1)S(1)}, u32[]{:S(2)}, u32[]{:S(2)}) collective-permute-start(bf16[40,1152]{1,0:T(8,128)(2,1)S(1)} %get-tuple-element.36), channel_id=1, source_target_pairs={{0,8},{1,9},{2,10},{3,11},{4,12},{5,13},{6,14},{7,15},{8,0},{9,1},... | collective-permute-start | bytes 276488 | tf_op jit(solution)/shard_map/ppermute | solution.py:361
  8.7 13.6 %collective-permute-start.2 = (bf16[40,1152]{1,0:T(8,128)(2,1)S(1)}, bf16[40,1152]{1,0:T(8,128)(2,1)S(1)}, u32[]{:S(2)}, u32[]{:S(2)}) collective-permute-start(bf16[40,1152]{1,0:T(8,128)(2,1)S(1)} %get-tuple-element.36), channel_id=1, source_target_pairs={{0,12},{1,13},{2,14},{3,15},{4,8},{5,9},{6,10},{7,11},{8,4},{9,5},... | collective-permute-start | bytes 276488 | tf_op jit(solution)/shard_map/ppermute | solution.py:361
  8.7 41.7 %collective-permute-start.16 = (bf16[384,1024]{1,0:T(8,128)(2,1)}, bf16[384,1024]{1,0:T(8,128)(2,1)S(1)}, u32[]{:S(2)}, u32[]{:S(2)}) collective-permute-start(bf16[384,1024]{1,0:T(8,128)(2,1)} %own_set.1), channel_id=1, source_target_pairs={{4,8},{5,9},{6,10},{7,11},{8,4},{9,5},{10,6},{11,7},{20,24},{21,25... | collective-permute-start | bytes 2359304 | tf_op jit(solution)/shard_map/ppermute | solution.py:361
  9.4 42.3 %collective-permute-start.15 = (bf16[384,1024]{1,0:T(8,128)(2,1)}, bf16[384,1024]{1,0:T(8,128)(2,1)S(1)}, u32[]{:S(2)}, u32[]{:S(2)}) collective-permute-start(bf16[384,1024]{1,0:T(8,128)(2,1)} %own_set.1), channel_id=1, source_target_pairs={{0,4},{1,5},{2,6},{3,7},{4,0},{5,1},{6,2},{7,3},{8,12},{9,13},{10,... | collective-permute-start | bytes 2359304 | tf_op jit(solution)/shard_map/ppermute | solution.py:361
  13.2 1.6 %copy-start = (bf16[1024,1024]{1,0:T(8,128)(2,1)S(1)}, bf16[1024,1024]{1,0:T(8,128)(2,1)}, u32[]{:S(2)}) copy-start(bf16[1024,1024]{1,0:T(8,128)(2,1)} %cent_ref.3) | copy-start | bytes 6291460
  14.8 0.7 copy-start.4
  15.5 0.7 copy-start.5
  16.2 47.0 %copy-start.1 = (bf16[1024,1024]{1,0:T(8,128)(2,1)S(1)}, bf16[1024,1024]{1,0:T(8,128)(2,1)}, u32[]{:S(2)}) copy-start(bf16[1024,1024]{1,0:T(8,128)(2,1)} %cent_ref.3) | copy-start | bytes 6291460
  20.4 14.2 %collective-permute-start.11 = (bf16[112,1024]{1,0:T(8,128)(2,1)S(1)}, bf16[112,1024]{1,0:T(8,128)(2,1)S(1)}, u32[]{:S(2)}, u32[]{:S(2)}) collective-permute-start(bf16[112,1024]{1,0:T(8,128)(2,1)S(1)} %get-tuple-element.25.far0), channel_id=1, source_target_pairs={{0,4},{1,5},{2,6},{3,7},{12,8},{13,9},{14,10},{15,11},{16,20},{17,... | collective-permute-start | bytes 688136 | tf_op jit(solution)/shard_map/ppermute | solution.py:361
  22.4 9.0 %collective-permute-start.3 = (bf16[160,1152]{1,0:T(8,128)(2,1)S(1)}, bf16[160,1152]{1,0:T(8,128)(2,1)S(1)}, u32[]{:S(2)}, u32[]{:S(2)}) collective-permute-start(bf16[160,1152]{1,0:T(8,128)(2,1)S(1)} %pad_maximum_fusion), channel_id=1, source_target_pairs={{0,2},{1,3},{2,0},{3,1},{4,6},{5,7},{6,4},{7,5},{8,10},{9,11},{10,... | collective-permute-start | bytes 1105928 | tf_op jit(solution)/shard_map/ppermute | solution.py:361
  24.1 63.5 %copy-start.3 = (bf16[384,1024]{1,0:T(8,128)(2,1)S(1)}, bf16[384,1024]{1,0:T(8,128)(2,1)}, u32[]{:S(2)}) copy-start(bf16[384,1024]{1,0:T(8,128)(2,1)} %own_set.1) | copy-start | bytes 2359300
  31.4 29.9 %collective-permute-start.4 = (bf16[320,1152]{1,0:T(8,128)(2,1)S(1)}, bf16[320,1152]{1,0:T(8,128)(2,1)S(1)}, u32[]{:S(2)}, u32[]{:S(2)}) collective-permute-start(bf16[320,1152]{1,0:T(8,128)(2,1)S(1)} %constant_dynamic-update-slice_fusion.mine_ref), channel_id=1, source_target_pairs={{0,1},{1,0},{2,3},{3,2},{4,5},{5,4},{6,7},{7,6},{8,9},{9,8},{10,11... | collective-permute-start | bytes 2211848 | tf_op jit(solution)/shard_map/ppermute | solution.py:361
  31.5 8.4 %collective-permute-start.12 = (bf16[112,1024]{1,0:T(8,128)(2,1)S(1)}, bf16[112,1024]{1,0:T(8,128)(2,1)S(1)}, u32[]{:S(2)}, u32[]{:S(2)}) collective-permute-start(bf16[112,1024]{1,0:T(8,128)(2,1)S(1)} %get-tuple-element.26), channel_id=1, source_target_pairs={{0,5},{1,4},{2,7},{3,6},{12,9},{13,8},{14,11},{15,10},{16,21},{17,... | collective-permute-start | bytes 688136 | tf_op jit(solution)/shard_map/ppermute | solution.py:361
  34.6 9.7 %collective-permute-start.13 = (bf16[112,1024]{1,0:T(8,128)(2,1)S(1)}, bf16[112,1024]{1,0:T(8,128)(2,1)S(1)}, u32[]{:S(2)}, u32[]{:S(2)}) collective-permute-start(bf16[112,1024]{1,0:T(8,128)(2,1)S(1)} %get-tuple-element.27), channel_id=1, source_target_pairs={{0,6},{1,7},{2,4},{3,5},{12,10},{13,11},{14,8},{15,9},{16,22},{17,... | collective-permute-start | bytes 688136 | tf_op jit(solution)/shard_map/ppermute | solution.py:361
  40.0 9.4 %collective-permute-start.14 = (bf16[112,1024]{1,0:T(8,128)(2,1)S(1)}, bf16[112,1024]{1,0:T(8,128)(2,1)S(1)}, u32[]{:S(2)}, u32[]{:S(2)}) collective-permute-start(bf16[112,1024]{1,0:T(8,128)(2,1)S(1)} %get-tuple-element.28), channel_id=1, source_target_pairs={{0,7},{1,6},{2,5},{3,4},{12,11},{13,10},{14,9},{15,8},{16,23},{17,... | collective-permute-start | bytes 688136 | tf_op jit(solution)/shard_map/ppermute | solution.py:361
  44.3 6.1 %collective-permute-start.5 = (bf16[112,1024]{1,0:T(8,128)(2,1)S(1)}, bf16[112,1024]{1,0:T(8,128)(2,1)S(1)}, u32[]{:S(2)}, u32[]{:S(2)}) collective-permute-start(bf16[112,1024]{1,0:T(8,128)(2,1)S(1)} %get-tuple-element.26), channel_id=1, source_target_pairs={{0,1},{1,0},{2,3},{3,2},{4,5},{5,4},{6,7},{7,6},{8,9},{9,8},{10,11... | collective-permute-start | bytes 688136 | tf_op jit(solution)/shard_map/ppermute | solution.py:361
  49.4 8.5 %collective-permute-start.6 = (bf16[112,1024]{1,0:T(8,128)(2,1)S(1)}, bf16[112,1024]{1,0:T(8,128)(2,1)S(1)}, u32[]{:S(2)}, u32[]{:S(2)}) collective-permute-start(bf16[112,1024]{1,0:T(8,128)(2,1)S(1)} %get-tuple-element.27), channel_id=1, source_target_pairs={{0,2},{1,3},{2,0},{3,1},{4,6},{5,7},{6,4},{7,5},{8,10},{9,11},{10,... | collective-permute-start | bytes 688136 | tf_op jit(solution)/shard_map/ppermute | solution.py:361
  50.4 10.1 %collective-permute-start.7 = (bf16[112,1024]{1,0:T(8,128)(2,1)S(1)}, bf16[112,1024]{1,0:T(8,128)(2,1)S(1)}, u32[]{:S(2)}, u32[]{:S(2)}) collective-permute-start(bf16[112,1024]{1,0:T(8,128)(2,1)S(1)} %get-tuple-element.28), channel_id=1, source_target_pairs={{0,3},{1,2},{2,1},{3,0},{4,7},{5,6},{6,5},{7,4},{8,11},{9,10},{10,... | collective-permute-start | bytes 688136 | tf_op jit(solution)/shard_map/ppermute | solution.py:361
  50.4 36.0 %copy-start.6 = (bf16[384,1024]{1,0:T(8,128)(2,1)}, bf16[384,1024]{1,0:T(8,128)(2,1)S(1)}, u32[]{:S(2)}) copy-start(bf16[384,1024]{1,0:T(8,128)(2,1)S(1)} %collective-permute-done.16.cross_set) | copy-start | bytes 2359300
  50.5 35.9 %collective-permute-start.17 = (bf16[384,1024]{1,0:T(8,128)(2,1)S(1)}, bf16[384,1024]{1,0:T(8,128)(2,1)S(1)}, u32[]{:S(2)}, u32[]{:S(2)}) collective-permute-start(bf16[384,1024]{1,0:T(8,128)(2,1)S(1)} %collective-permute-done.16.cross_set), channel_id=1, source_target_pairs={{4,0},{5,1},{6,2},{7,3},{8,12},{9,13},{10,14},{11,15},{20,16},{21,... | collective-permute-start | bytes 2359304 | tf_op jit(solution)/shard_map/ppermute | solution.py:361
  51.8 34.6 %collective-permute-start.18 = (bf16[384,1024]{1,0:T(8,128)(2,1)S(1)}, bf16[384,1024]{1,0:T(8,128)(2,1)S(1)}, u32[]{:S(2)}, u32[]{:S(2)}) collective-permute-start(bf16[384,1024]{1,0:T(8,128)(2,1)S(1)} %collective-permute-done.15.near_set), channel_id=1, source_target_pairs={{4,8},{5,9},{6,10},{7,11},{8,4},{9,5},{10,6},{11,7},{20,24},{21,25... | collective-permute-start | bytes 2359304 | tf_op jit(solution)/shard_map/ppermute | solution.py:361
  57.9 15.7 %collective-permute-start.10 = (bf16[288,1024]{1,0:T(8,128)(2,1)S(1)}, bf16[288,1024]{1,0:T(8,128)(2,1)S(1)}, u32[]{:S(2)}, u32[]{:S(2)}) collective-permute-start(bf16[288,1024]{1,0:T(8,128)(2,1)S(1)} %get-tuple-element.31), channel_id=1, source_target_pairs={{0,3},{1,2},{2,1},{3,0},{4,7},{5,6},{6,5},{7,4},{8,11},{9,10},{10,... | collective-permute-start | bytes 1769480 | tf_op jit(solution)/shard_map/ppermute | solution.py:361
  60.5 13.1 %collective-permute-start.8 = (bf16[288,1024]{1,0:T(8,128)(2,1)S(1)}, bf16[288,1024]{1,0:T(8,128)(2,1)S(1)}, u32[]{:S(2)}, u32[]{:S(2)}) collective-permute-start(bf16[288,1024]{1,0:T(8,128)(2,1)S(1)} %get-tuple-element.29), channel_id=1, source_target_pairs={{0,1},{1,0},{2,3},{3,2},{4,5},{5,4},{6,7},{7,6},{8,9},{9,8},{10,11... | collective-permute-start | bytes 1769480 | tf_op jit(solution)/shard_map/ppermute | solution.py:361
  61.3 25.1 %collective-permute-start.9 = (bf16[288,1024]{1,0:T(8,128)(2,1)S(1)}, bf16[288,1024]{1,0:T(8,128)(2,1)S(1)}, u32[]{:S(2)}, u32[]{:S(2)}) collective-permute-start(bf16[288,1024]{1,0:T(8,128)(2,1)S(1)} %get-tuple-element.30), channel_id=1, source_target_pairs={{0,2},{1,3},{2,0},{3,1},{4,6},{5,7},{6,4},{7,5},{8,10},{9,11},{10,... | collective-permute-start | bytes 1769480 | tf_op jit(solution)/shard_map/ppermute | solution.py:361
  69.6 1.1 copy-start.2
  86.4 0.9 copy-start.7
  86.4 1.1 %copy-start.8 = (bf16[384,1024]{1,0:T(8,128)(2,1)}, bf16[384,1024]{1,0:T(8,128)(2,1)S(1)}, u32[]{:S(2)}) copy-start(bf16[384,1024]{1,0:T(8,128)(2,1)S(1)} %collective-permute-done.18.last_set) | copy-start | bytes 2359300

commit v3 on v0

--- a/solution.py
+++ b/solution.py
@@ -1,6 +1,10 @@
+import functools
+
 import jax
 import jax.numpy as jnp
 from jax import lax
+from jax.experimental import pallas as pl
+from jax.experimental.pallas import tpu as pltpu
 from jax.sharding import PartitionSpec as P
 
 BLOCK = 1024
@@ -39,7 +43,7 @@
     return jnp.sum(jnp.cumsum(matches, axis=0) * matches, axis=1) - 1
 
 
-def body(embeddings, probes, assigned, prior_counts, centroids, candidates, centroids2):
+def general_body(embeddings, probes, assigned, prior_counts, centroids, candidates, centroids2):
     devices = lax.axis_size("shard")
     emb_rows, width = embeddings.shape
     probe_count = probes.shape[1]
@@ -125,6 +129,285 @@
     return (density, new_centroids, fresh.reshape(-1), level_two)
 
 
+NT = (((1,), (1,)), ((), ()))
+PARAMS = pltpu.CompilerParams(vmem_limit_bytes=48 * 1024 * 1024)
+META = 16
+
+
+def position():
+    me = lax.axis_index("shard")
+    return me, me // 4, (me // 2) % 2, me % 2
+
+
+def unit_wide(wide):
+    power = jnp.mean(wide * wide, axis=-1, keepdims=True) + 1e-06
+    return (wide * lax.rsqrt(power)).astype(jnp.bfloat16)
+
+
+def weights(scores, width):
+    return jnp.exp(scores * (10.0 / width) - 10.0)
+
+
+def one_hot(hits):
+    return jnp.where(hits, 1.0, 0.0).astype(jnp.bfloat16)
+
+
+def column(row):
+    return jnp.transpose(jnp.broadcast_to(row, (8, row.shape[1])))[:, 0:1]
+
+
+def facts_kernel(emb_ref, probes_ref, assigned_ref, out):
+    count, width = emb_ref.shape
+    square = (count, count)
+    same = lax.broadcasted_iota(jnp.int32, square, 0) == lax.broadcasted_iota(jnp.int32, square, 1)
+    slot = jnp.sum(jnp.where(same, assigned_ref[...], 0).astype(jnp.float32), axis=1, keepdims=True).astype(jnp.int32)
+    probe_count = probes_ref.shape[1]
+    lane = lax.broadcasted_iota(jnp.int32, (count, 128), 1)
+    facts = jnp.where(lane == probe_count, slot >> 5, jnp.where(lane == probe_count + 1, slot & 31, 0))
+    for p in range(probe_count):
+        facts = jnp.where(lane == p, probes_ref[:, p : p + 1], facts)
+    out[:, 0:width] = emb_ref[...]
+    out[:, width:] = facts.astype(jnp.float32).astype(jnp.bfloat16)
+
+
+def pick_rows(slot, first, count):
+    return one_hot(slot == lax.broadcasted_iota(jnp.int32, (count, slot.shape[1]), 0) + first)
+
+
+def pack(slot, prior, cent, r, out):
+    count = out.shape[0] - META
+    rows = slot.shape[1]
+    ident = lax.broadcasted_iota(jnp.int32, (1, rows), 1) + 1
+    line = lax.broadcasted_iota(jnp.int32, (META, rows), 0)
+    facts = jnp.where(line == 0, ident >> 5, jnp.where(line == 1, ident & 31, jnp.where(line == 2, prior, 0)))
+    facts = facts.astype(jnp.float32).astype(jnp.bfloat16)
+    pick = pick_rows(slot, r * count, count)
+    out[0:count, :] = jnp.dot(pick, cent, preferred_element_type=jnp.float32).astype(jnp.bfloat16)
+    out[count:, :] = jnp.zeros((META, out.shape[1]), jnp.bfloat16)
+    out[count:, 0:count] = lax.dot_general(facts, pick, NT, preferred_element_type=jnp.float32).astype(jnp.bfloat16)
+
+
+def pack_kernel(cap, per, cand_any, prior_any, cent_any, rows2, rows3, info, cand_ref, prior_ref, cent_ref, sems):
+    copies = [
+        pltpu.make_async_copy(src, dst, sems.at[i])
+        for i, (src, dst) in enumerate(((cand_any, cand_ref), (prior_any, prior_ref), (cent_any, cent_ref)))
+    ]
+    for copy in copies:
+        copy.start()
+    me, z, y, core = position()
+    rows = cand_ref.shape[1]
+    buckets = 16 * per
+    before = lax.broadcasted_iota(jnp.int32, (rows, rows), 0) <= lax.broadcasted_iota(jnp.int32, (rows, rows), 1)
+    before = one_hot(before)
+    copies[0].wait()
+    cand = cand_ref[...]
+    dev = sum((cand >= per * step).astype(jnp.int32) for step in range(1, 16))
+    near = dev >> 2
+    plane = jnp.where(z >= 2, 3 - near, near)
+    rel = (((dev >> 1) & 1) ^ y) * 2 + ((dev & 1) ^ core)
+    named = cand == lax.broadcasted_iota(jnp.int32, (buckets, rows), 0)
+    counted = jnp.dot(one_hot(named), before, preferred_element_type=jnp.float32)
+    rank = jnp.sum(jnp.where(named, counted, 0.0), axis=0, keepdims=True).astype(jnp.int32) - 1
+    kind = plane * per + cand - dev * per
+    slot = (rel * 4 * per + kind) * cap + rank
+    info[0:1, :] = slot
+    info[1:2, :] = rel * 4 + (kind >> 2)
+    info[2:3, :] = (kind & 3) * cap + rank
+    copies[1].wait()
+    copies[2].wait()
+    pack(slot, prior_ref[...], cent_ref[...], 2, rows2)
+    pack(slot, prior_ref[...], cent_ref[...], 3, rows3)
+
+
+def pack_beside_kernel(info, prior_ref, cent_ref, rows1):
+    pack(info[0:1, :], prior_ref[...], cent_ref[...], 1, rows1)
+
+
+def first_kernel(mine_ref, other_ref, cent_ref, prior_ref, info, scaled, facts, share, fresh_rows, fresh_counts, own_rows, units):
+    me, z, y, core = position()
+    half = mine_ref.shape[0]
+    count = 2 * half
+    rows, width = cent_ref.shape
+    scaled[0:half, :] = unit_wide(mine_ref[:, 0:width].astype(jnp.float32))
+    scaled[half:count, :] = unit_wide(other_ref[:, 0:width].astype(jnp.float32))
+    aux = jnp.concatenate([mine_ref[:, width:], other_ref[:, width:]], axis=0).astype(jnp.float32)
+    aux = jnp.transpose(aux)[0:16, :].astype(jnp.int32)
+    facts[...] = aux
+    target = jnp.where(aux[0:1, :] == me, aux[8:9, :] * 32 + aux[9:10, :], -1)
+    member = jnp.sum((aux[0:8, :] == me).astype(jnp.float32), axis=0, keepdims=True)
+    prior = column(prior_ref[...].astype(jnp.float32))
+    step = 256
+    total = jnp.zeros((1, count), jnp.float32)
+    for start in range(0, rows, step):
+        old = cent_ref[start : start + step, :].astype(jnp.float32)
+        scores = lax.dot_general(unit_wide(old), scaled[...], NT, preferred_element_type=jnp.float32)
+        total = total + jnp.sum(weights(scores, width), axis=0, keepdims=True)
+        hits = one_hot(target == lax.broadcasted_iota(jnp.int32, (step, count), 0) + start)
+        sums = jnp.dot(hits, scaled[...], preferred_element_type=jnp.float32)
+        gained = jnp.sum(hits.astype(jnp.float32), axis=1, keepdims=True)
+        ahead = prior[start : start + step, :]
+        updated = (ahead * old + sums) / (ahead + gained)
+        fresh_rows[start : start + step, :] = updated.astype(jnp.bfloat16)
+        units[start : start + step, :] = unit_wide(updated)
+        gained_row = lax.dot_general(
+            jnp.ones((8, count), jnp.bfloat16), hits, NT, preferred_element_type=jnp.float32
+        )
+        fresh_counts[0:1, start : start + step] = prior_ref[0:1, start : start + step] + gained_row[0:1, :].astype(jnp.int32)
+    piece = count // 16
+    lane = lax.broadcasted_iota(jnp.int32, (16, count), 1)
+    line = lax.broadcasted_iota(jnp.int32, (16, count), 0)
+    apart = jnp.where((member > 0.0) & (lane >= line * piece) & (lane < (line + 1) * piece), total, 0.0)
+    spot = lax.broadcasted_iota(jnp.int32, (count, 128), 0)
+    block = sum((spot >= piece * step).astype(jnp.int32) for step in range(1, 16))
+    together = jnp.where(spot - block * piece == lax.broadcasted_iota(jnp.int32, (count, 128), 1), 1.0, 0.0)
+    share[...] = jnp.dot(apart, together, precision=lax.Precision.HIGHEST, preferred_element_type=jnp.float32)
+    pick = pick_rows(info[0:1, :], 0, own_rows.shape[0])
+    own_rows[...] = jnp.dot(pick, units[...], preferred_element_type=jnp.float32).astype(jnp.bfloat16)
+
+
+def level_sums(two, packed, w, per):
+    block = two.shape[0] // per
+    lines = []
+    for j in range(per):
+        scores = lax.dot_general(two[j * block : (j + 1) * block, :], packed[w, j], NT, preferred_element_type=jnp.float32)
+        lines.append(jnp.sum(weights(scores, two.shape[1]), axis=0, keepdims=True))
+    return lines
+
+
+def second_kernel(cap, per, scaled, facts_in, own_rows, rows1, rows2, rows3, own_set, near_set, packed, sums):
+    me, z, y, core = position()
+    end = (z == 0) | (z == 3)
+    part = per * cap
+    probe0 = facts_in[0:1, :]
+    slots = facts_in[8:9, :] * 32 + facts_in[9:10, :]
+    for r, ref in enumerate((own_rows, rows1, rows2, rows3)):
+        if r:
+            facts = jnp.transpose(ref[4 * part :, 0 : 4 * part].astype(jnp.float32))
+            target = jnp.where(probe0 == (me ^ r), slots + 1, -1)
+        for w in range(4):
+            rows = ref[w * part : (w + 1) * part, :]
+            if r:
+                known = facts[w * part : (w + 1) * part, :]
+                hits = one_hot((known[:, 0:1] * 32.0 + known[:, 1:2]).astype(jnp.int32) == target)
+                gained = jnp.sum(hits.astype(jnp.float32), axis=1, keepdims=True)
+                added = jnp.dot(hits, scaled[...], preferred_element_type=jnp.float32)
+                ahead = known[:, 2:3]
+                rows = unit_wide((ahead * rows.astype(jnp.float32) + added) / jnp.maximum(ahead + gained, 1.0))
+            for j in range(per):
+                packed[w, j, r * cap : (r + 1) * cap, :] = rows[j * cap : (j + 1) * cap, :]
+    for w in range(2):
+        two = jnp.where(end, own_set[...], near_set[...]) if w == 0 else jnp.where(end, near_set[...], own_set[...])
+        for j, line in enumerate(level_sums(unit_wide(two.astype(jnp.float32)), packed, w, per)):
+            sums[w * per + j : w * per + j + 1, :] = line
+
+
+def third_kernel(cap, per, packed, sums, cross_set, passed, last_set, far_set, out0, out1, out2, out3):
+    me, z, y, core = position()
+    end = (z == 0) | (z == 3)
+    lines = [sums[0 : 2 * per, :]]
+    for w, (at_end, at_mid) in enumerate(((passed, cross_set), (far_set, last_set))):
+        two = jnp.where(end, at_end[...], at_mid[...])
+        lines += level_sums(unit_wide(two.astype(jnp.float32)), packed, w + 2, per)
+    together = jnp.concatenate(lines + [jnp.zeros((4, 4 * cap), jnp.float32)], axis=0)
+    lane = lax.broadcasted_iota(jnp.int32, together.shape, 1)
+    line = lax.broadcasted_iota(jnp.int32, together.shape, 0)
+    for r, out in enumerate((out0, out1, out2, out3)):
+        spread = jnp.zeros_like(together)
+        for s in range(4):
+            turned = together if s == r else pltpu.roll(together, ((s - r) % 4) * cap, 1)
+            spread = jnp.where((line % 4 == s) & (lane >= s * cap) & (lane < (s + 1) * cap), turned, spread)
+        for t in range(4):
+            out[t : t + 1, :] = jnp.sum(spread[4 * t : 4 * t + 4], axis=0, keepdims=True)
+
+
+def last_kernel(cap, scale, info, got0, got1, got2, got3, level_two):
+    values = jnp.concatenate([got[0:4, :] for got in (got0, got1, got2, got3)], axis=0)
+    rows = info.shape[1]
+    chosen = jnp.where(info[2:3, :] == lax.broadcasted_iota(jnp.int32, (4 * cap, rows), 0), 1.0, 0.0)
+    spread = jnp.dot(values, chosen, precision=lax.Precision.HIGHEST, preferred_element_type=jnp.float32)
+    found = jnp.where(info[1:2, :] == lax.broadcasted_iota(jnp.int32, (16, rows), 0), spread, 0.0)
+    level_two[...] = jnp.log(jnp.sum(found, axis=0, keepdims=True) / scale)
+
+
+def call(kernel, outs, scratch=(), **kw):
+    return pl.pallas_call(
+        kernel,
+        out_shape=outs,
+        scratch_shapes=list(scratch),
+        compiler_params=PARAMS,
+        **kw,
+    )
+
+
+def line_body(embeddings, probes, assigned, prior_counts, centroids, candidates, centroids2):
+    emb_rows, width = embeddings.shape
+    probe_count = probes.shape[1]
+    rows = centroids.shape[0]
+    per = BLOCKS2_DEV
+    cap = max(2, 3 * rows // (2 * per * 16))
+    column_rows = 4 * per * cap
+    bf16, f32, i32 = jnp.bfloat16, jnp.float32, jnp.int32
+    shape = jax.ShapeDtypeStruct
+
+    def exchange(value, apart, sources=range(16)):
+        return lax.ppermute(value, "shard", [(i, i ^ apart) for i in sources])
+
+    mids = range(4, 12)
+    near_set = exchange(centroids2, 4)
+    cross_set = exchange(centroids2, 12, mids)
+    mine = call(facts_kernel, shape((emb_rows, width + 128), bf16))(embeddings, probes, assigned.reshape(1, emb_rows))
+    mine = jnp.concatenate([mine] + [exchange(mine, apart) for apart in (4, 8, 12)], axis=0)
+    mine = jnp.concatenate([mine, exchange(mine, 2)], axis=0)
+    other = exchange(mine, 1)
+    cand_row = candidates.reshape(1, rows)
+    prior_row = prior_counts.reshape(1, rows)
+    sent = shape((column_rows + META, width), bf16)
+    anywhere = pl.BlockSpec(memory_space=pl.ANY)
+    rows2, rows3, info = call(
+        functools.partial(pack_kernel, cap, per),
+        (sent, sent, shape((8, rows), i32)),
+        [
+            pltpu.VMEM((1, rows), i32),
+            pltpu.VMEM((1, rows), i32),
+            pltpu.VMEM((rows, width), bf16),
+            pltpu.SemaphoreType.DMA((3,)),
+        ],
+        in_specs=[anywhere] * 3,
+    )(cand_row, prior_row, centroids)
+    rows2, rows3 = exchange(rows2, 2), exchange(rows3, 3)
+    rows1 = exchange(call(pack_beside_kernel, sent)(info, prior_row, centroids), 1)
+    passed = exchange(cross_set, 4, mids)
+    last_set = exchange(near_set, 12, mids)
+    far_set = exchange(last_set, 4, mids)
+    scaled, facts, share, new_centroids, counts, own_rows = call(
+        first_kernel,
+        (
+            shape((16 * emb_rows, width), bf16),
+            shape((16, 16 * emb_rows), i32),
+            shape((16, 4 * cap), f32),
+            shape((rows, width), bf16),
+            shape((1, rows), i32),
+            shape((column_rows, width), bf16),
+        ),
+        [pltpu.VMEM((rows, width), bf16)],
+    )(mine, other, centroids, prior_row, info)
+    apart = jnp.arange(16, dtype=i32) ^ lax.axis_index("shard")
+    share = share[((apart & 1) << 3) | ((apart & 2) << 1) | (apart >> 2)]
+    share = lax.all_to_all(share, "shard", split_axis=0, concat_axis=0, tiled=True)
+    density = jnp.log(jnp.sum(share, axis=0)[:emb_rows] / (probe_count * BLOCK))
+    packed, sums = call(
+        functools.partial(second_kernel, cap, per),
+        (shape((4, per, 4 * cap, width), bf16), shape((8, 4 * cap), f32)),
+    )(scaled, facts, own_rows, rows1, rows2, rows3, centroids2, near_set)
+    tile = shape((8, 4 * cap), f32)
+    tiles = call(functools.partial(third_kernel, cap, per), (tile,) * 4)(
+        packed, sums, cross_set, passed, last_set, far_set
+    )
+    tiles = [tile if r == 0 else exchange(tile, r) for r, tile in enumerate(tiles)]
+    level_two = call(functools.partial(last_kernel, cap, BLOCK2), shape((1, rows), f32))(info, *tiles)
+    return (density, new_centroids, counts.reshape(-1), level_two.reshape(-1))
+
+
 def solution(mesh):
     placed = (
         P(("groups", "shard"), None),
@@ -135,6 +418,7 @@
         P(("groups", "shard"), None),
         P(("groups", "shard"), None),
     )
+    body = line_body if mesh.shape["shard"] == 16 else general_body
     return jax.shard_map(
         body,
         mesh=mesh,

time: 185 us -> 98.8 us (0.53)
  waiting for transfers between devices: 63.9 us -> 28.1 us
  other arithmetic: 28 us -> 0.6 us
  local copies, waits for them, and re-layouts: 38.2 us -> 11.1 us
  Pallas kernels: 0 us -> 25.4 us
  matrix products: 11.8 us -> 0 us
  starting transfers between devices: 41.5 us -> 32.2 us
    all_to_all x5 -> x1, waiting for transfers between devices: 63.9 us -> 0.01 us  [line_body(): lax.all_to_all(share, 'shard', split_axis=0, concat_axis=0, tiled=True)]
    ppermute x0 -> x16, waiting for transfers between devices: none -> 28.1 us  [exchange(): return lax.ppermute(value, 'shard', [(i, i ^ apart) for i in sources])]
    all_to_all x5 -> x1, starting transfers between devices: 41.5 us -> 13.8 us  [line_body(): lax.all_to_all(share, 'shard', split_axis=0, concat_axis=0, tiled=True)]
    pallas_call x0 -> x7, Pallas kernels: none -> 25.4 us  [the longest x1 8.34 us: line_body(): call(functools.partial(second_kernel, cap, per), (shape((4, per, 4 * cap,...]
    ppermute x0 -> x16, starting transfers between devices: none -> 18.5 us  [exchange(): return lax.ppermute(value, 'shard', [(i, i ^ apart) for i in sources])]
    another operation x8 -> x0, other arithmetic: 15.3 us -> none
    scatter x3 -> x0, local copies, waits for them, and re-layouts: 14 us -> none  [the longest x1 8.06 us: body(): jnp.zeros((buckets_two * second_capacity, width), jnp.bfloat16)]
    dot_general x5 -> x0, matrix products: 11.8 us -> none  [the longest x4 7.92 us: kernel_sums(): lax.dot_general(rows, unit, (((1,), (1,)), ((), ())), preferred_element_t...]
  transfers between devices with their start and end apart: 5 -> 17, of which waited for: 4 -> 5; matrix products, arithmetic and copies ran while one was open for 29% -> 2% of each run, Pallas kernels for 0% -> 21%
where the time goes in v3:
time: 98.8 us; the launch traced here: 98.3 us
  starting transfers between devices  32.2 us (33%)
  waiting for transfers between devices  28.1 us (28%)
  Pallas kernels  25.4 us (26%)
  local copies, waits for them, and re-layouts  11.1 us (11%)
    ppermute x16, waiting for transfers between devices, exchange(): return lax.ppermute(value, 'shard', [(i, i ^ apart) for i in sources])  28.1 us
    ppermute x16, starting transfers between devices, exchange(): return lax.ppermute(value, 'shard', [(i, i ^ apart) for i in sources])  18.5 us
    all_to_all x1, starting transfers between devices, line_body(): lax.all_to_all(share, 'shard', split_axis=0, concat_axis=0, tiled=True)  13.8 us
    unnamed x33, local copies, waits for them, and re-layouts  9.93 us
    pallas_call x1, Pallas kernels, line_body(): call(functools.partial(second_kernel, cap, per), (shape((4, per, 4 * cap,...  8.34 us
    pallas_call x1, Pallas kernels, line_body(): call(first_kernel, (shape((16 * emb_rows, width), bf16), shape((16, 16 *...  6.34 us
    pallas_call x1, Pallas kernels, line_body(): call(functools.partial(third_kernel, cap, per), (tile,) * 4)  3.82 us
    pallas_call x1, Pallas kernels, line_body(): call(functools.partial(pack_kernel, cap, per), (sent, sent, shape((8, row...  3.73 us
  transfers between devices with their start and end apart: 17, of which 5 were waited for; matrix products, arithmetic and copies ran while one was open for 2% of the time, Pallas kernels for 21%

profile of v3, /device:TPU:0, one launch (start us, length us, event | category | flops | bytes accessed | tf_op | source)
XLA Modules:
  0.0 98.3 jit_solution(12439773996796506210)
XLA Ops:
  0.6 0.0 copy-start
  0.6 0.9 copy.12.probes_ref
  1.6 0.0 copy-start.10
  1.6 0.9 copy-done.10
  2.4 0.7 copy-done.13
  3.1 0.0 copy-start.11
  3.1 0.2 shard_map.102
  3.3 3.1 %collective-permute-start = (bf16[40,1152]{1,0:T(8,128)(2,1)S(1)}, bf16[40,1152]{1,0:T(8,128)(2,1)S(1)}, u32[]{:S(2)}, u32[]{:S(2)}) collective-permute-start(bf16[40,1152]{1,0:T(8,128)(2,1)S(1)} %shard_map.102), channel_id=1, source_target_pairs={{0,4},{1,5},{2,6},{3,7},{4,0},{5,1},{6,2},{7,3},{8,12},{9,13},{10,... | collective-permute-start | bytes 276488 | tf_op jit(solution)/shard_map/ppermute | solution.py:353
  6.3 2.6 %collective-permute-start.1 = (bf16[40,1152]{1,0:T(8,128)(2,1)S(1)}, bf16[40,1152]{1,0:T(8,128)(2,1)S(1)}, u32[]{:S(2)}, u32[]{:S(2)}) collective-permute-start(bf16[40,1152]{1,0:T(8,128)(2,1)S(1)} %shard_map.102), channel_id=1, source_target_pairs={{0,8},{1,9},{2,10},{3,11},{4,12},{5,13},{6,14},{7,15},{8,0},{9,1},... | collective-permute-start | bytes 276488 | tf_op jit(solution)/shard_map/ppermute | solution.py:353
  8.9 0.0 collective-permute-start.2
  8.9 0.9 collective-permute-start.8
  9.8 1.6 %collective-permute-start.9 = (bf16[384,1024]{1,0:T(8,128)(2,1)}, bf16[384,1024]{1,0:T(8,128)(2,1)}, u32[]{:S(2)}, u32[]{:S(2)}) collective-permute-start(bf16[384,1024]{1,0:T(8,128)(2,1)} %own_set.1), channel_id=1, source_target_pairs={{4,8},{5,9},{6,10},{7,11},{8,4},{9,5},{10,6},{11,7},{20,24},{21,25... | collective-permute-start | bytes 2359304 | tf_op jit(solution)/shard_map/ppermute | solution.py:353
  11.4 0.0 collective-permute-done
  11.4 5.0 %collective-permute-done.1 = bf16[40,1152]{1,0:T(8,128)(2,1)S(1)} collective-permute-done((bf16[40,1152]{1,0:T(8,128)(2,1)S(1)}, bf16[40,1152]{1,0:T(8,128)(2,1)S(1)}, u32[]{:S(2)}, u32[]{:S(2)}) %collective-permute-start.1) | collective-permute-done | bytes 92192 | tf_op jit(solution)/shard_map/ppermute | solution.py:353
  16.4 0.0 collective-permute-done.2
  16.4 1.6 %collective-permute-start.3 = (bf16[160,1152]{1,0:T(8,128)(2,1)S(1)}, bf16[160,1152]{1,0:T(8,128)(2,1)S(1)}, u32[]{:S(2)}, u32[]{:S(2)}) collective-permute-start(bf16[160,1152]{1,0:T(8,128)(2,1)S(1)} %pad_maximum_fusion), channel_id=1, source_target_pairs={{0,2},{1,3},{2,0},{3,1},{4,6},{5,7},{6,4},{7,5},{8,10},{9,11},{10,... | collective-permute-start | bytes 1105928 | tf_op jit(solution)/shard_map/ppermute | solution.py:353
  18.1 12.7 %collective-permute-done.8.near_set = bf16[384,1024]{1,0:T(8,128)(2,1)S(1)} collective-permute-done((bf16[384,1024]{1,0:T(8,128)(2,1)}, bf16[384,1024]{1,0:T(8,128)(2,1)S(1)}, u32[]{:S(2)}, u32[]{:S(2)}) %collective-permute-start.8) | collective-permute-done | bytes 786464 | tf_op jit(solution)/shard_map/ppermute | solution.py:353
  30.8 1.5 %collective-permute-start.11 = (bf16[384,1024]{1,0:T(8,128)(2,1)S(1)}, bf16[384,1024]{1,0:T(8,128)(2,1)}, u32[]{:S(2)}, u32[]{:S(2)}) collective-permute-start(bf16[384,1024]{1,0:T(8,128)(2,1)S(1)} %collective-permute-done.8.near_set), channel_id=1, source_target_pairs={{4,8},{5,9},{6,10},{7,11},{8,4},{9,5},{10,6},{11,7},{20,24},{21,25... | collective-permute-start | bytes 2359304 | tf_op jit(solution)/shard_map/ppermute | solution.py:353
  32.3 0.0 collective-permute-done.3
  32.4 0.0 copy-start.1
  32.4 0.1 collective-permute-start.4
  32.5 0.0 copy-done
  32.5 0.0 copy-done.11
  32.5 0.0 copy-done.12
  32.5 3.7 %shard_map.103 = (bf16[400,1024]{1,0:T(8,128)(2,1)}, bf16[400,1024]{1,0:T(8,128)(2,1)}, s32[8,1024]{1,0:T(8,128)S(1)}) custom-call(s32[1,1024]{1,0:T(1,128)S(1)} %bitcast.13, s32[1,1024]{1,0:T(1,128)S(1)} %bitcast.10, bf16[1024,1024]{1,0:T(8,128)(2,1)S(1)} %copy-done), custom_call_target="tpu_custom_call" | custom-call | tf_op jit(solution)/shard_map/pallas_call | solution.py:366
  36.2 2.0 %shard_map.105 = bf16[400,1024]{1,0:T(8,128)(2,1)} custom-call(s32[8,1024]{1,0:T(8,128)S(1)} %get-tuple-element.19.info, s32[1,1024]{1,0:T(1,128)S(1)} %bitcast.11, bf16[1024,1024]{1,0:T(8,128)(2,1)S(1)} %copy-done), custom_call_target="tpu_custom_call" | custom-call | tf_op jit(solution)/shard_map/pallas_call | solution.py:378
  38.3 0.0 copy-done.4
  38.3 0.0 copy-done.1
  38.3 0.5 collective-permute-start.5
  38.7 1.5 %collective-permute-start.6 = (bf16[400,1024]{1,0:T(8,128)(2,1)}, bf16[400,1024]{1,0:T(8,128)(2,1)}, u32[]{:S(2)}, u32[]{:S(2)}) collective-permute-start(bf16[400,1024]{1,0:T(8,128)(2,1)} %get-tuple-element.26), channel_id=1, source_target_pairs={{0,2},{1,3},{2,0},{3,1},{4,6},{5,7},{6,4},{7,5},{8,10},{9,11},{10,... | collective-permute-start | bytes 2457608 | tf_op jit(solution)/shard_map/ppermute | solution.py:353
  40.3 0.0 collective-permute-done.9.cross_set
  40.3 0.0 collective-permute-start.7
  40.3 0.0 collective-permute-done.4.other_ref
  40.3 0.0 copy-start.8
  40.3 0.9 copy-done.8
  41.2 1.3 %collective-permute-start.10 = (bf16[384,1024]{1,0:T(8,128)(2,1)}, bf16[384,1024]{1,0:T(8,128)(2,1)}, u32[]{:S(2)}, u32[]{:S(2)}) collective-permute-start(bf16[384,1024]{1,0:T(8,128)(2,1)} %collective-permute-done.9.cross_set), channel_id=1, source_target_pairs={{4,0},{5,1},{6,2},{7,3},{8,12},{9,13},{10,14},{11,15},{20,16},{21,... | collective-permute-start | bytes 2359304 | tf_op jit(solution)/shard_map/ppermute | solution.py:353
  42.4 0.0 collective-permute-done.11.last_set
  42.4 1.3 %collective-permute-start.12 = (bf16[384,1024]{1,0:T(8,128)(2,1)}, bf16[384,1024]{1,0:T(8,128)(2,1)}, u32[]{:S(2)}, u32[]{:S(2)}) collective-permute-start(bf16[384,1024]{1,0:T(8,128)(2,1)} %collective-permute-done.11.last_set), channel_id=1, source_target_pairs={{4,0},{5,1},{6,2},{7,3},{8,12},{9,13},{10,14},{11,15},{20,16},{21,... | collective-permute-start | bytes 2359304 | tf_op jit(solution)/shard_map/ppermute | solution.py:353
  43.8 0.0 copy-start.2
  43.8 1.1 %copy-done.2 = bf16[320,1152]{1,0:T(8,128)(2,1)S(1)} copy-done((bf16[320,1152]{1,0:T(8,128)(2,1)S(1)}, bf16[320,1152]{1,0:T(8,128)(2,1)}, u32[]{:S(2)}) %copy-start.2) | copy-done | bytes 737304
  44.9 1.1 %copy-done.9 = bf16[320,1152]{1,0:T(8,128)(2,1)S(1)} copy-done((bf16[320,1152]{1,0:T(8,128)(2,1)S(1)}, bf16[320,1152]{1,0:T(8,128)(2,1)}, u32[]{:S(2)}) %copy-start.9) | copy-done | bytes 737304
  46.0 6.3 %shard_map.104 = (bf16[640,1024]{1,0:T(8,128)(2,1)S(1)}, s32[16,640]{1,0:T(8,128)S(1)}, f32[16,128]{1,0:T(8,128)S(1)}, bf16[1024,1024]{1,0:T(8,128)(2,1)}, s32[1...) custom-call(bf16[320,1152]{1,0:T(8,128)(2,1)S(1)} %copy-done.2, bf16[320,1152]{1,0:T(8,128)(2,1)S(1)} %copy-done.9, ...), custom_call_target="tpu_custom_call" | custom-call | tf_op jit(solution)/shard_map/pallas_call | solution.py:382
  52.4 0.9 copy-done.6
  53.3 1.1 %gather_fusion = f32[16,128]{1,0:T(8,128)} fusion(f32[16,128]{1,0:T(8,128)S(1)} %get-tuple-element.20, s32[1024]{0:T(1024)S(1)} %pad_clamp_fusion), kind=kCustom, calls=%fused_computation | custom fusion | bytes 16448 | tf_op jit(solution)/shard_map/gather | solution.py:395
  54.4 13.8 %all-to-all-start = ((f32[16,1,128]{2,1,0:T(1,128)}), f32[16,1,128]{2,1,0:T(1,128)S(1)}, u32[]{:S(2)}, u32[]{:S(2)}) async-start(f32[16,1,128]{2,1,0:T(1,128)} %bitcast.5), calls=%async_computation | async-start | bytes 16384 | tf_op jit(solution)/shard_map/all_to_all | solution.py:396
  68.2 0.0 collective-permute-done.5.rows1
  68.2 0.0 collective-permute-done.6.rows2
  68.2 7.8 %collective-permute-done.7.rows3 = bf16[400,1024]{1,0:T(8,128)(2,1)} collective-permute-done((bf16[400,1024]{1,0:T(8,128)(2,1)}, bf16[400,1024]{1,0:T(8,128)(2,1)}, u32[]{:S(2)}, u32[]{:S(2)}) %collective-permute-start.7) | collective-permute-done | bytes 819232 | tf_op jit(solution)/shard_map/ppermute | solution.py:353
  76.0 1.1 %copy-done.3 = bf16[384,1024]{1,0:T(8,128)(2,1)S(1)} copy-done((bf16[384,1024]{1,0:T(8,128)(2,1)S(1)}, bf16[384,1024]{1,0:T(8,128)(2,1)}, u32[]{:S(2)}) %copy-start.3) | copy-done | bytes 786456
  77.1 1.1 %copy-done.5 = bf16[384,1024]{1,0:T(8,128)(2,1)S(1)} copy-done((bf16[384,1024]{1,0:T(8,128)(2,1)S(1)}, bf16[384,1024]{1,0:T(8,128)(2,1)}, u32[]{:S(2)}) %copy-start.5) | copy-done | bytes 786456
  78.2 1.1 %copy-done.7 = bf16[384,1024]{1,0:T(8,128)(2,1)S(1)} copy-done((bf16[384,1024]{1,0:T(8,128)(2,1)S(1)}, bf16[384,1024]{1,0:T(8,128)(2,1)}, u32[]{:S(2)}) %copy-start.7) | copy-done | bytes 786456
  79.4 8.3 %shard_map.106 = (bf16[4,3,128,1024]{3,2,1,0:T(8,128)(2,1)}, f32[8,128]{1,0:T(8,128)S(1)}) custom-call(bf16[640,1024]{1,0:T(8,128)(2,1)S(1)} %get-tuple-element.23.scaled, s32[16,640]{1,0:T(8,128)S(1)} %get-tuple-element.24.facts_in, bf16[384,1024]{1,0:T(8,128)(2,1)S(1)} %copy-done.7, bf16[400,1024]{1,0:T(8,128)(2,1)} %collective-permute-done.5.rows1, ...), custom_call_target="tpu_custom_call" | custom-call | tf_op jit(solution)/shard_map/pallas_call | solution.py:398
  87.7 0.0 all-to-all-done
  87.8 0.0 collective-permute-done.10.passed
  87.8 0.0 collective-permute-done.12.far_set
  87.8 3.8 %shard_map.107 = (f32[8,128]{1,0:T(8,128)S(1)}, f32[8,128]{1,0:T(8,128)S(1)}, f32[8,128]{1,0:T(8,128)S(1)}, f32[8,128]{1,0:T(8,128)S(1)}) custom-call(bf16[4,3,128,1024]{3,2,1,0:T(8,128)(2,1)} %get-tuple-element.28.packed, f32[8,128]{1,0:T(8,128)S(1)} %get-tuple-element.29.sums, bf16[384,1024]{1,0:T(8,128)(2,1)} %collective-permute-done.9.cross_set, ...), custom_call_target="tpu_custom_call" | custom-call | tf_op jit(solution)/shard_map/pallas_call | solution.py:403
  91.6 1.1 %collective-permute-start.13 = (f32[8,128]{1,0:T(8,128)S(1)}, f32[8,128]{1,0:T(8,128)S(1)}, u32[]{:S(2)}, u32[]{:S(2)}) collective-permute-start(f32[8,128]{1,0:T(8,128)S(1)} %get-tuple-element.31), channel_id=1, source_target_pairs={{0,1},{1,0},{2,3},{3,2},{4,5},{5,4},{6,7},{7,6},{8,9},{9,8},{10,11... | collective-permute-start | bytes 12296 | tf_op jit(solution)/shard_map/ppermute | solution.py:353
  92.7 1.5 %collective-permute-start.14 = (f32[8,128]{1,0:T(8,128)S(1)}, f32[8,128]{1,0:T(8,128)S(1)}, u32[]{:S(2)}, u32[]{:S(2)}) collective-permute-start(f32[8,128]{1,0:T(8,128)S(1)} %get-tuple-element.32), channel_id=1, source_target_pairs={{0,2},{1,3},{2,0},{3,1},{4,6},{5,7},{6,4},{7,5},{8,10},{9,11},{10,... | collective-permute-start | bytes 12296 | tf_op jit(solution)/shard_map/ppermute | solution.py:353
  94.2 0.0 collective-permute-start.15
  94.2 0.5 multiply_log_fusion
  94.7 0.0 collective-permute-done.13.got1
  94.7 1.6 %collective-permute-done.14.got2 = f32[8,128]{1,0:T(8,128)S(1)} collective-permute-done((f32[8,128]{1,0:T(8,128)S(1)}, f32[8,128]{1,0:T(8,128)S(1)}, u32[]{:S(2)}, u32[]{:S(2)}) %collective-permute-start.14) | collective-permute-done | bytes 4128 | tf_op jit(solution)/shard_map/ppermute | solution.py:353
  96.3 1.0 collective-permute-done.15.got3
  97.3 1.0 %shard_map.108 = f32[1,1024]{1,0:T(1,128)} custom-call(s32[8,1024]{1,0:T(8,128)S(1)} %get-tuple-element.19.info, f32[8,128]{1,0:T(8,128)S(1)} %get-tuple-element.30.got0, f32[8,128]{1,0:T(8,128)S(1)} %collective-permute-done.13.got1, f32[8,128]{1,0:T(8,128)S(1)} %collective-permute-done.14.got2, f32[8,128]{1,0:T(8,128)S(1)} %collective-permute-done.15.got3), custom_call_target="tpu_custom_call" | custom-call | tf_op jit(solution)/shard_map/pallas_call | solution.py:407
  (17 shorter events, 0.2 us)
Async XLA Ops:
  0.6 31.8 %copy-start = (bf16[1024,1024]{1,0:T(8,128)(2,1)S(1)}, bf16[1024,1024]{1,0:T(8,128)(2,1)}, u32[]{:S(2)}) copy-start(bf16[1024,1024]{1,0:T(8,128)(2,1)} %cent_ref.3) | copy-start | bytes 6291460
  1.6 0.9 copy-start.10
  2.4 0.7 copy-start.13
  3.1 29.4 %copy-start.11 = (s32[1024]{0:T(1024)S(1)}, s32[1024]{0:T(1024)}, u32[]{:S(2)}) copy-start(s32[1024]{0:T(1024)} %param.10) | copy-start | bytes 12292
  3.1 29.4 %copy-start.12 = (s32[1024,1]{0,1:T(1,128)S(1)}, s32[1024,1]{0,1:T(1,128)}, u32[]{:S(2)}) copy-start(s32[1024,1]{0,1:T(1,128)} %param.12) | copy-start | bytes 12292
  3.3 8.1 %collective-permute-start = (bf16[40,1152]{1,0:T(8,128)(2,1)S(1)}, bf16[40,1152]{1,0:T(8,128)(2,1)S(1)}, u32[]{:S(2)}, u32[]{:S(2)}) collective-permute-start(bf16[40,1152]{1,0:T(8,128)(2,1)S(1)} %shard_map.102), channel_id=1, source_target_pairs={{0,4},{1,5},{2,6},{3,7},{4,0},{5,1},{6,2},{7,3},{8,12},{9,13},{10,... | collective-permute-start | bytes 276488 | tf_op jit(solution)/shard_map/ppermute | solution.py:353
  6.3 10.1 %collective-permute-start.1 = (bf16[40,1152]{1,0:T(8,128)(2,1)S(1)}, bf16[40,1152]{1,0:T(8,128)(2,1)S(1)}, u32[]{:S(2)}, u32[]{:S(2)}) collective-permute-start(bf16[40,1152]{1,0:T(8,128)(2,1)S(1)} %shard_map.102), channel_id=1, source_target_pairs={{0,8},{1,9},{2,10},{3,11},{4,12},{5,13},{6,14},{7,15},{8,0},{9,1},... | collective-permute-start | bytes 276488 | tf_op jit(solution)/shard_map/ppermute | solution.py:353
  8.9 7.5 %collective-permute-start.2 = (bf16[40,1152]{1,0:T(8,128)(2,1)S(1)}, bf16[40,1152]{1,0:T(8,128)(2,1)S(1)}, u32[]{:S(2)}, u32[]{:S(2)}) collective-permute-start(bf16[40,1152]{1,0:T(8,128)(2,1)S(1)} %shard_map.102), channel_id=1, source_target_pairs={{0,12},{1,13},{2,14},{3,15},{4,8},{5,9},{6,10},{7,11},{8,4},{9,5},... | collective-permute-start | bytes 276488 | tf_op jit(solution)/shard_map/ppermute | solution.py:353
  8.9 21.9 %collective-permute-start.8 = (bf16[384,1024]{1,0:T(8,128)(2,1)}, bf16[384,1024]{1,0:T(8,128)(2,1)S(1)}, u32[]{:S(2)}, u32[]{:S(2)}) collective-permute-start(bf16[384,1024]{1,0:T(8,128)(2,1)} %own_set.1), channel_id=1, source_target_pairs={{0,4},{1,5},{2,6},{3,7},{4,0},{5,1},{6,2},{7,3},{8,12},{9,13},{10,... | collective-permute-start | bytes 2359304 | tf_op jit(solution)/shard_map/ppermute | solution.py:353
  9.8 30.4 %collective-permute-start.9 = (bf16[384,1024]{1,0:T(8,128)(2,1)}, bf16[384,1024]{1,0:T(8,128)(2,1)}, u32[]{:S(2)}, u32[]{:S(2)}) collective-permute-start(bf16[384,1024]{1,0:T(8,128)(2,1)} %own_set.1), channel_id=1, source_target_pairs={{4,8},{5,9},{6,10},{7,11},{8,4},{9,5},{10,6},{11,7},{20,24},{21,25... | collective-permute-start | bytes 2359304 | tf_op jit(solution)/shard_map/ppermute | solution.py:353
  16.4 15.9 %collective-permute-start.3 = (bf16[160,1152]{1,0:T(8,128)(2,1)S(1)}, bf16[160,1152]{1,0:T(8,128)(2,1)S(1)}, u32[]{:S(2)}, u32[]{:S(2)}) collective-permute-start(bf16[160,1152]{1,0:T(8,128)(2,1)S(1)} %pad_maximum_fusion), channel_id=1, source_target_pairs={{0,2},{1,3},{2,0},{3,1},{4,6},{5,7},{6,4},{7,5},{8,10},{9,11},{10,... | collective-permute-start | bytes 1105928 | tf_op jit(solution)/shard_map/ppermute | solution.py:353
  30.8 7.4 %copy-start.4 = (bf16[384,1024]{1,0:T(8,128)(2,1)}, bf16[384,1024]{1,0:T(8,128)(2,1)S(1)}, u32[]{:S(2)}) copy-start(bf16[384,1024]{1,0:T(8,128)(2,1)S(1)} %collective-permute-done.8.near_set) | copy-start | bytes 2359300
  30.8 11.6 %collective-permute-start.11 = (bf16[384,1024]{1,0:T(8,128)(2,1)S(1)}, bf16[384,1024]{1,0:T(8,128)(2,1)}, u32[]{:S(2)}, u32[]{:S(2)}) collective-permute-start(bf16[384,1024]{1,0:T(8,128)(2,1)S(1)} %collective-permute-done.8.near_set), channel_id=1, source_target_pairs={{4,8},{5,9},{6,10},{7,11},{8,4},{9,5},{10,6},{11,7},{20,24},{21,25... | collective-permute-start | bytes 2359304 | tf_op jit(solution)/shard_map/ppermute | solution.py:353
  32.4 5.9 %copy-start.1 = (bf16[320,1152]{1,0:T(8,128)(2,1)}, bf16[320,1152]{1,0:T(8,128)(2,1)S(1)}, u32[]{:S(2)}) copy-start(bf16[320,1152]{1,0:T(8,128)(2,1)S(1)} %constant_dynamic-update-slice_fusion.mine_ref) | copy-start | bytes 2211844
  32.4 7.9 %collective-permute-start.4 = (bf16[320,1152]{1,0:T(8,128)(2,1)S(1)}, bf16[320,1152]{1,0:T(8,128)(2,1)S(1)}, u32[]{:S(2)}, u32[]{:S(2)}) collective-permute-start(bf16[320,1152]{1,0:T(8,128)(2,1)S(1)} %constant_dynamic-update-slice_fusion.mine_ref), channel_id=1, source_target_pairs={{0,1},{1,0},{2,3},{3,2},{4,5},{5,4},{6,7},{7,6},{8,9},{9,8},{10,11... | collective-permute-start | bytes 2211848 | tf_op jit(solution)/shard_map/ppermute | solution.py:353
  38.3 29.9 %collective-permute-start.5 = (bf16[400,1024]{1,0:T(8,128)(2,1)}, bf16[400,1024]{1,0:T(8,128)(2,1)}, u32[]{:S(2)}, u32[]{:S(2)}) collective-permute-start(bf16[400,1024]{1,0:T(8,128)(2,1)} %shard_map.105), channel_id=1, source_target_pairs={{0,1},{1,0},{2,3},{3,2},{4,5},{5,4},{6,7},{7,6},{8,9},{9,8},{10,11... | collective-permute-start | bytes 2457608 | tf_op jit(solution)/shard_map/ppermute | solution.py:353
  38.7 29.5 %collective-permute-start.6 = (bf16[400,1024]{1,0:T(8,128)(2,1)}, bf16[400,1024]{1,0:T(8,128)(2,1)}, u32[]{:S(2)}, u32[]{:S(2)}) collective-permute-start(bf16[400,1024]{1,0:T(8,128)(2,1)} %get-tuple-element.26), channel_id=1, source_target_pairs={{0,2},{1,3},{2,0},{3,1},{4,6},{5,7},{6,4},{7,5},{8,10},{9,11},{10,... | collective-permute-start | bytes 2457608 | tf_op jit(solution)/shard_map/ppermute | solution.py:353
  40.3 35.7 %collective-permute-start.7 = (bf16[400,1024]{1,0:T(8,128)(2,1)}, bf16[400,1024]{1,0:T(8,128)(2,1)}, u32[]{:S(2)}, u32[]{:S(2)}) collective-permute-start(bf16[400,1024]{1,0:T(8,128)(2,1)} %get-tuple-element.27), channel_id=1, source_target_pairs={{0,3},{1,2},{2,1},{3,0},{4,7},{5,6},{6,5},{7,4},{8,11},{9,10},{10,... | collective-permute-start | bytes 2457608 | tf_op jit(solution)/shard_map/ppermute | solution.py:353
  40.3 0.9 copy-start.8
  41.2 46.6 %collective-permute-start.10 = (bf16[384,1024]{1,0:T(8,128)(2,1)}, bf16[384,1024]{1,0:T(8,128)(2,1)}, u32[]{:S(2)}, u32[]{:S(2)}) collective-permute-start(bf16[384,1024]{1,0:T(8,128)(2,1)} %collective-permute-done.9.cross_set), channel_id=1, source_target_pairs={{4,0},{5,1},{6,2},{7,3},{8,12},{9,13},{10,14},{11,15},{20,16},{21,... | collective-permute-start | bytes 2359304 | tf_op jit(solution)/shard_map/ppermute | solution.py:353
  42.4 45.3 %collective-permute-start.12 = (bf16[384,1024]{1,0:T(8,128)(2,1)}, bf16[384,1024]{1,0:T(8,128)(2,1)}, u32[]{:S(2)}, u32[]{:S(2)}) collective-permute-start(bf16[384,1024]{1,0:T(8,128)(2,1)} %collective-permute-done.11.last_set), channel_id=1, source_target_pairs={{4,0},{5,1},{6,2},{7,3},{8,12},{9,13},{10,14},{11,15},{20,16},{21,... | collective-permute-start | bytes 2359304 | tf_op jit(solution)/shard_map/ppermute | solution.py:353
  43.8 1.1 %copy-start.2 = (bf16[320,1152]{1,0:T(8,128)(2,1)S(1)}, bf16[320,1152]{1,0:T(8,128)(2,1)}, u32[]{:S(2)}) copy-start(bf16[320,1152]{1,0:T(8,128)(2,1)} %copy-done.1) | copy-start | bytes 2211844
  44.9 1.1 %copy-start.9 = (bf16[320,1152]{1,0:T(8,128)(2,1)S(1)}, bf16[320,1152]{1,0:T(8,128)(2,1)}, u32[]{:S(2)}) copy-start(bf16[320,1152]{1,0:T(8,128)(2,1)} %copy-done.8) | copy-start | bytes 2211844
  52.4 0.9 copy-start.6
  54.4 33.3 %all-to-all-start = ((f32[16,1,128]{2,1,0:T(1,128)}), f32[16,1,128]{2,1,0:T(1,128)S(1)}, u32[]{:S(2)}, u32[]{:S(2)}) async-start(f32[16,1,128]{2,1,0:T(1,128)} %bitcast.5), calls=%async_computation | async-start | bytes 16384 | tf_op jit(solution)/shard_map/all_to_all | solution.py:396
  76.0 1.1 %copy-start.3 = (bf16[384,1024]{1,0:T(8,128)(2,1)S(1)}, bf16[384,1024]{1,0:T(8,128)(2,1)}, u32[]{:S(2)}) copy-start(bf16[384,1024]{1,0:T(8,128)(2,1)} %own_set.1) | copy-start | bytes 2359300
  77.1 1.1 %copy-start.5 = (bf16[384,1024]{1,0:T(8,128)(2,1)S(1)}, bf16[384,1024]{1,0:T(8,128)(2,1)}, u32[]{:S(2)}) copy-start(bf16[384,1024]{1,0:T(8,128)(2,1)} %copy-done.4) | copy-start | bytes 2359300
  78.2 1.1 %copy-start.7 = (bf16[384,1024]{1,0:T(8,128)(2,1)S(1)}, bf16[384,1024]{1,0:T(8,128)(2,1)}, u32[]{:S(2)}) copy-start(bf16[384,1024]{1,0:T(8,128)(2,1)} %copy-done.6) | copy-start | bytes 2359300
  91.6 3.1 %collective-permute-start.13 = (f32[8,128]{1,0:T(8,128)S(1)}, f32[8,128]{1,0:T(8,128)S(1)}, u32[]{:S(2)}, u32[]{:S(2)}) collective-permute-start(f32[8,128]{1,0:T(8,128)S(1)} %get-tuple-element.31), channel_id=1, source_target_pairs={{0,1},{1,0},{2,3},{3,2},{4,5},{5,4},{6,7},{7,6},{8,9},{9,8},{10,11... | collective-permute-start | bytes 12296 | tf_op jit(solution)/shard_map/ppermute | solution.py:353
  92.7 3.6 %collective-permute-start.14 = (f32[8,128]{1,0:T(8,128)S(1)}, f32[8,128]{1,0:T(8,128)S(1)}, u32[]{:S(2)}, u32[]{:S(2)}) collective-permute-start(f32[8,128]{1,0:T(8,128)S(1)} %get-tuple-element.32), channel_id=1, source_target_pairs={{0,2},{1,3},{2,0},{3,1},{4,6},{5,7},{6,4},{7,5},{8,10},{9,11},{10,... | collective-permute-start | bytes 12296 | tf_op jit(solution)/shard_map/ppermute | solution.py:353
  94.2 3.1 %collective-permute-start.15 = (f32[8,128]{1,0:T(8,128)S(1)}, f32[8,128]{1,0:T(8,128)S(1)}, u32[]{:S(2)}, u32[]{:S(2)}) collective-permute-start(f32[8,128]{1,0:T(8,128)S(1)} %get-tuple-element.33), channel_id=1, source_target_pairs={{0,3},{1,2},{2,1},{3,0},{4,7},{5,6},{6,5},{7,4},{8,11},{9,10},{10,... | collective-permute-start | bytes 12296 | tf_op jit(solution)/shard_map/ppermute | solution.py:353

commit v4 on v3

--- a/solution.py
+++ b/solution.py
@@ -132,6 +132,8 @@
 NT = (((1,), (1,)), ((), ()))
 PARAMS = pltpu.CompilerParams(vmem_limit_bytes=48 * 1024 * 1024)
 META = 16
+HBM = pl.BlockSpec(memory_space=pltpu.HBM)
+VMEM = pl.BlockSpec(memory_space=pltpu.VMEM)
 
 
 def position():
@@ -156,44 +158,45 @@
     return jnp.transpose(jnp.broadcast_to(row, (8, row.shape[1])))[:, 0:1]
 
 
-def facts_kernel(emb_ref, probes_ref, assigned_ref, out):
-    count, width = emb_ref.shape
-    square = (count, count)
-    same = lax.broadcasted_iota(jnp.int32, square, 0) == lax.broadcasted_iota(jnp.int32, square, 1)
-    slot = jnp.sum(jnp.where(same, assigned_ref[...], 0).astype(jnp.float32), axis=1, keepdims=True).astype(jnp.int32)
-    probe_count = probes_ref.shape[1]
-    lane = lax.broadcasted_iota(jnp.int32, (count, 128), 1)
-    facts = jnp.where(lane == probe_count, slot >> 5, jnp.where(lane == probe_count + 1, slot & 31, 0))
-    for p in range(probe_count):
-        facts = jnp.where(lane == p, probes_ref[:, p : p + 1], facts)
-    out[:, 0:width] = emb_ref[...]
-    out[:, width:] = facts.astype(jnp.float32).astype(jnp.bfloat16)
+def fetch(pairs, sems):
+    copies = [pltpu.make_async_copy(src, dst, sems.at[i]) for i, (src, dst) in enumerate(pairs)]
+    for copy in copies:
+        copy.start()
+    return copies
 
 
 def pick_rows(slot, first, count):
     return one_hot(slot == lax.broadcasted_iota(jnp.int32, (count, slot.shape[1]), 0) + first)
 
 
-def pack(slot, prior, cent, r, out):
+def pack(slot, prior, cent, first, out):
     count = out.shape[0] - META
     rows = slot.shape[1]
     ident = lax.broadcasted_iota(jnp.int32, (1, rows), 1) + 1
     line = lax.broadcasted_iota(jnp.int32, (META, rows), 0)
     facts = jnp.where(line == 0, ident >> 5, jnp.where(line == 1, ident & 31, jnp.where(line == 2, prior, 0)))
     facts = facts.astype(jnp.float32).astype(jnp.bfloat16)
-    pick = pick_rows(slot, r * count, count)
+    pick = pick_rows(slot, first, count)
     out[0:count, :] = jnp.dot(pick, cent, preferred_element_type=jnp.float32).astype(jnp.bfloat16)
     out[count:, :] = jnp.zeros((META, out.shape[1]), jnp.bfloat16)
     out[count:, 0:count] = lax.dot_general(facts, pick, NT, preferred_element_type=jnp.float32).astype(jnp.bfloat16)
 
 
-def pack_kernel(cap, per, cand_any, prior_any, cent_any, rows2, rows3, info, cand_ref, prior_ref, cent_ref, sems):
-    copies = [
-        pltpu.make_async_copy(src, dst, sems.at[i])
-        for i, (src, dst) in enumerate(((cand_any, cand_ref), (prior_any, prior_ref), (cent_any, cent_ref)))
-    ]
-    for copy in copies:
-        copy.start()
+def pack_kernel(
+    cap, per, cand_any, emb_any, probes_any, assigned_any, prior_any, cent_any, mine, rows2, rows3, info,
+    cand_ref, emb_ref, probes_ref, assigned_ref, prior_ref, cent_ref, sems,
+):
+    copies = fetch(
+        (
+            (cand_any, cand_ref),
+            (emb_any, emb_ref),
+            (probes_any, probes_ref),
+            (assigned_any, assigned_ref),
+            (prior_any, prior_ref),
+            (cent_any, cent_ref),
+        ),
+        sems,
+    )
     me, z, y, core = position()
     rows = cand_ref.shape[1]
     buckets = 16 * per
@@ -213,29 +216,52 @@
     info[0:1, :] = slot
     info[1:2, :] = rel * 4 + (kind >> 2)
     info[2:3, :] = (kind & 3) * cap + rank
-    copies[1].wait()
-    copies[2].wait()
-    pack(slot, prior_ref[...], cent_ref[...], 2, rows2)
-    pack(slot, prior_ref[...], cent_ref[...], 3, rows3)
-
-
-def pack_beside_kernel(info, prior_ref, cent_ref, rows1):
-    pack(info[0:1, :], prior_ref[...], cent_ref[...], 1, rows1)
-
-
-def first_kernel(mine_ref, other_ref, cent_ref, prior_ref, info, scaled, facts, share, fresh_rows, fresh_counts, own_rows, units):
+    for copy in copies[1:5]:
+        copy.wait()
+    count, width = emb_ref.shape
+    probe_count = probes_ref.shape[0]
+    slots = assigned_ref[...]
+    facts = jnp.concatenate([probes_ref[...], slots >> 5, slots & 31], axis=0).astype(jnp.float32)
+    facts = jnp.concatenate([facts, jnp.zeros((128 - probe_count - 2, count), jnp.float32)], axis=0)
+    same = lax.broadcasted_iota(jnp.int32, (count, count), 0) == lax.broadcasted_iota(jnp.int32, (count, count), 1)
+    mine[:, 0:width] = emb_ref[...]
+    mine[:, width:] = lax.dot_general(
+        one_hot(same), facts.astype(jnp.bfloat16), NT, preferred_element_type=jnp.float32
+    ).astype(jnp.bfloat16)
+    copies[5].wait()
+    pack(slot, prior_ref[...], cent_ref[...], 2 * 4 * per * cap, rows2)
+    pack(slot, prior_ref[...], cent_ref[...], 3 * 4 * per * cap, rows3)
+
+
+def pack_more_kernel(info, prior_ref, cent_ref, rows2, rows3):
+    half = rows2.shape[0] - META
+    pack(info[0:1, :], prior_ref[...], cent_ref[...], 5 * half, rows2)
+    pack(info[0:1, :], prior_ref[...], cent_ref[...], 7 * half, rows3)
+
+
+def order_kernel(*refs):
+    pass
+
+
+def first_kernel(
+    mine_any, other_any, cent_ref, prior_ref, info, early2, early3,
+    scaled, facts, share, fresh_rows, fresh_counts, own_rows, beside_rows, units, mine_ref, other_ref, sems,
+):
+    copies = fetch(((mine_any, mine_ref), (other_any, other_ref)), sems)
     me, z, y, core = position()
     half = mine_ref.shape[0]
     count = 2 * half
     rows, width = cent_ref.shape
+    prior = column(prior_ref[...].astype(jnp.float32))
+    copies[0].wait()
     scaled[0:half, :] = unit_wide(mine_ref[:, 0:width].astype(jnp.float32))
+    copies[1].wait()
     scaled[half:count, :] = unit_wide(other_ref[:, 0:width].astype(jnp.float32))
     aux = jnp.concatenate([mine_ref[:, width:], other_ref[:, width:]], axis=0).astype(jnp.float32)
     aux = jnp.transpose(aux)[0:16, :].astype(jnp.int32)
     facts[...] = aux
     target = jnp.where(aux[0:1, :] == me, aux[8:9, :] * 32 + aux[9:10, :], -1)
     member = jnp.sum((aux[0:8, :] == me).astype(jnp.float32), axis=0, keepdims=True)
-    prior = column(prior_ref[...].astype(jnp.float32))
     step = 256
     total = jnp.zeros((1, count), jnp.float32)
     for start in range(0, rows, step):
@@ -261,54 +287,88 @@
     block = sum((spot >= piece * step).astype(jnp.int32) for step in range(1, 16))
     together = jnp.where(spot - block * piece == lax.broadcasted_iota(jnp.int32, (count, 128), 1), 1.0, 0.0)
     share[...] = jnp.dot(apart, together, precision=lax.Precision.HIGHEST, preferred_element_type=jnp.float32)
-    pick = pick_rows(info[0:1, :], 0, own_rows.shape[0])
-    own_rows[...] = jnp.dot(pick, units[...], preferred_element_type=jnp.float32).astype(jnp.bfloat16)
-
-
-def level_sums(two, packed, w, per):
+    for r, out in enumerate((own_rows, beside_rows)):
+        pick = pick_rows(info[0:1, :], r * out.shape[0], out.shape[0])
+        out[...] = jnp.dot(pick, units[...], preferred_element_type=jnp.float32).astype(jnp.bfloat16)
+
+
+def level_sums(two, rows, per):
     block = two.shape[0] // per
     lines = []
     for j in range(per):
-        scores = lax.dot_general(two[j * block : (j + 1) * block, :], packed[w, j], NT, preferred_element_type=jnp.float32)
+        scores = lax.dot_general(two[j * block : (j + 1) * block, :], rows(j), NT, preferred_element_type=jnp.float32)
         lines.append(jnp.sum(weights(scores, two.shape[1]), axis=0, keepdims=True))
-    return lines
-
-
-def second_kernel(cap, per, scaled, facts_in, own_rows, rows1, rows2, rows3, own_set, near_set, packed, sums):
+    return jnp.concatenate(lines, axis=0)
+
+
+def second_kernel(cap, per, second, scaled, facts_in, own_any, beside_any, rows2_any, rows3_any, *refs):
+    sets, refs = refs[: 2 if not second else 3], refs[2 if not second else 3 :]
+    if second:
+        kept, sums, own, beside, rows2, rows3, two, packed, sems = refs
+    else:
+        sums, own, beside, rows2, rows3, two, two_more, packed, sems = refs
     me, z, y, core = position()
     end = (z == 0) | (z == 3)
     part = per * cap
+    half = pl.ds(2 * part if second else 0, 2 * part)
+    pairs = [(own_any.at[half], own), (beside_any.at[half], beside), (rows2_any, rows2), (rows3_any, rows3)]
+    if second:
+        at_end = pltpu.make_async_copy(sets[1], two, sems.at[4])
+        at_mid = pltpu.make_async_copy(sets[0], two, sems.at[4])
+        pl.when(end)(at_end.start)
+        pl.when(jnp.logical_not(end))(at_mid.start)
+    else:
+        pairs += [(sets[0], two), (sets[1], two_more)]
+    copies = fetch(pairs, sems)
     probe0 = facts_in[0:1, :]
     slots = facts_in[8:9, :] * 32 + facts_in[9:10, :]
-    for r, ref in enumerate((own_rows, rows1, rows2, rows3)):
-        if r:
-            facts = jnp.transpose(ref[4 * part :, 0 : 4 * part].astype(jnp.float32))
-            target = jnp.where(probe0 == (me ^ r), slots + 1, -1)
-        for w in range(4):
-            rows = ref[w * part : (w + 1) * part, :]
-            if r:
-                known = facts[w * part : (w + 1) * part, :]
-                hits = one_hot((known[:, 0:1] * 32.0 + known[:, 1:2]).astype(jnp.int32) == target)
-                gained = jnp.sum(hits.astype(jnp.float32), axis=1, keepdims=True)
-                added = jnp.dot(hits, scaled[...], preferred_element_type=jnp.float32)
-                ahead = known[:, 2:3]
-                rows = unit_wide((ahead * rows.astype(jnp.float32) + added) / jnp.maximum(ahead + gained, 1.0))
+    for r, ref in ((0, own), (1, beside), (2, rows2), (3, rows3)):
+        copies[r].wait()
+        if r >= 2:
+            facts = jnp.transpose(ref[2 * part :, 0 : 2 * part].astype(jnp.float32))
+            hits = (facts[:, 0:1] * 32.0 + facts[:, 1:2]).astype(jnp.int32) == jnp.where(probe0 == (me ^ r), slots + 1, -1)
+            hits = one_hot(hits)
+            gained = jnp.sum(hits.astype(jnp.float32), axis=1, keepdims=True)
+            added = jnp.dot(hits, scaled[...], preferred_element_type=jnp.float32)
+            ahead = facts[:, 2:3]
+            wide = (ahead * ref[0 : 2 * part, :].astype(jnp.float32) + added) / jnp.maximum(ahead + gained, 1.0)
+            rows = unit_wide(wide)
+        else:
+            rows = ref[...]
+        for w in range(2):
             for j in range(per):
-                packed[w, j, r * cap : (r + 1) * cap, :] = rows[j * cap : (j + 1) * cap, :]
-    for w in range(2):
-        two = jnp.where(end, own_set[...], near_set[...]) if w == 0 else jnp.where(end, near_set[...], own_set[...])
-        for j, line in enumerate(level_sums(unit_wide(two.astype(jnp.float32)), packed, w, per)):
-            sums[w * per + j : w * per + j + 1, :] = line
-
-
-def third_kernel(cap, per, packed, sums, cross_set, passed, last_set, far_set, out0, out1, out2, out3):
+                start = w * part + j * cap
+                packed[w, j, r * cap : (r + 1) * cap, :] = rows[start : start + cap, :]
+    if second:
+        pl.when(end)(at_end.wait)
+        pl.when(jnp.logical_not(end))(at_mid.wait)
+        sums[0:per, :] = level_sums(unit_wide(two[...].astype(jnp.float32)), lambda j: packed[0, j], per)
+        kept[...] = packed[1]
+    else:
+        copies[4].wait()
+        copies[5].wait()
+        own_unit = unit_wide(two[...].astype(jnp.float32))
+        near_unit = unit_wide(two_more[...].astype(jnp.float32))
+        first = jnp.where(end, 0, 1)
+        sums[pl.ds(first * 8, per), :] = level_sums(own_unit, lambda j: packed[first, j], per)
+        sums[pl.ds(8 - first * 8, per), :] = level_sums(near_unit, lambda j: packed[1 - first, j], per)
+
+
+def third_kernel(cap, per, early, later, kept_any, last_any, far_any, out0, out1, out2, out3, kept, two, sems):
     me, z, y, core = position()
     end = (z == 0) | (z == 3)
-    lines = [sums[0 : 2 * per, :]]
-    for w, (at_end, at_mid) in enumerate(((passed, cross_set), (far_set, last_set))):
-        two = jnp.where(end, at_end[...], at_mid[...])
-        lines += level_sums(unit_wide(two.astype(jnp.float32)), packed, w + 2, per)
-    together = jnp.concatenate(lines + [jnp.zeros((4, 4 * cap), jnp.float32)], axis=0)
+    at_end = pltpu.make_async_copy(far_any, two, sems.at[1])
+    at_mid = pltpu.make_async_copy(last_any, two, sems.at[1])
+    pl.when(end)(at_end.start)
+    pl.when(jnp.logical_not(end))(at_mid.start)
+    copies = fetch([(kept_any, kept)], sems)
+    pl.when(end)(at_end.wait)
+    pl.when(jnp.logical_not(end))(at_mid.wait)
+    two_unit = unit_wide(two[...].astype(jnp.float32))
+    copies[0].wait()
+    final = level_sums(two_unit, lambda j: kept[j], per)
+    lines = [early[0:per, :], early[8 : 8 + per, :], later[0:per, :], final]
+    together = jnp.concatenate(lines + [jnp.zeros((16 - 4 * per, 4 * cap), jnp.float32)], axis=0)
     lane = lax.broadcasted_iota(jnp.int32, together.shape, 1)
     line = lax.broadcasted_iota(jnp.int32, together.shape, 0)
     for r, out in enumerate((out0, out1, out2, out3)):
@@ -345,7 +405,7 @@
     rows = centroids.shape[0]
     per = BLOCKS2_DEV
     cap = max(2, 3 * rows // (2 * per * 16))
-    column_rows = 4 * per * cap
+    half = 2 * per * cap
     bf16, f32, i32 = jnp.bfloat16, jnp.float32, jnp.int32
     shape = jax.ShapeDtypeStruct
 
@@ -355,31 +415,38 @@
     mids = range(4, 12)
     near_set = exchange(centroids2, 4)
     cross_set = exchange(centroids2, 12, mids)
-    mine = call(facts_kernel, shape((emb_rows, width + 128), bf16))(embeddings, probes, assigned.reshape(1, emb_rows))
+    prior_row = prior_counts.reshape(1, rows)
+    sent = shape((half + META, width), bf16)
+    line = pltpu.VMEM((1, rows), i32)
+    mine, early2, early3, info = call(
+        functools.partial(pack_kernel, cap, per),
+        (shape((emb_rows, width + 128), bf16), sent, sent, shape((8, rows), i32)),
+        [
+            line,
+            pltpu.VMEM((emb_rows, width), bf16),
+            pltpu.VMEM((probe_count, emb_rows), i32),
+            pltpu.VMEM((1, emb_rows), i32),
+            line,
+            pltpu.VMEM((rows, width), bf16),
+            pltpu.SemaphoreType.DMA((6,)),
+        ],
+        in_specs=[HBM] * 6,
+    )(candidates.reshape(1, rows), embeddings, probes.T, assigned.reshape(1, emb_rows), prior_row, centroids)
+    early2, early3 = exchange(early2, 2), exchange(early3, 3)
+    late2, late3 = call(pack_more_kernel, (sent, sent))(info, prior_row, centroids)
+    late2, late3 = call(
+        order_kernel, (sent, sent), in_specs=[HBM] * 4, out_specs=(HBM, HBM), input_output_aliases={0: 0, 1: 1}
+    )(late2, late3, early2, early3)
+    late2, late3 = exchange(late2, 2), exchange(late3, 3)
     mine = jnp.concatenate([mine] + [exchange(mine, apart) for apart in (4, 8, 12)], axis=0)
     mine = jnp.concatenate([mine, exchange(mine, 2)], axis=0)
     other = exchange(mine, 1)
-    cand_row = candidates.reshape(1, rows)
-    prior_row = prior_counts.reshape(1, rows)
-    sent = shape((column_rows + META, width), bf16)
-    anywhere = pl.BlockSpec(memory_space=pl.ANY)
-    rows2, rows3, info = call(
-        functools.partial(pack_kernel, cap, per),
-        (sent, sent, shape((8, rows), i32)),
-        [
-            pltpu.VMEM((1, rows), i32),
-            pltpu.VMEM((1, rows), i32),
-            pltpu.VMEM((rows, width), bf16),
-            pltpu.SemaphoreType.DMA((3,)),
-        ],
-        in_specs=[anywhere] * 3,
-    )(cand_row, prior_row, centroids)
-    rows2, rows3 = exchange(rows2, 2), exchange(rows3, 3)
-    rows1 = exchange(call(pack_beside_kernel, sent)(info, prior_row, centroids), 1)
     passed = exchange(cross_set, 4, mids)
     last_set = exchange(near_set, 12, mids)
     far_set = exchange(last_set, 4, mids)
-    scaled, facts, share, new_centroids, counts, own_rows = call(
+    gathered = pltpu.VMEM((8 * emb_rows, width + 128), bf16)
+    units = shape((2 * half, width), bf16)
+    scaled, facts, share, new_centroids, counts, own_rows, beside_rows = call(
         first_kernel,
         (
             shape((16 * emb_rows, width), bf16),
@@ -387,22 +454,41 @@
             shape((16, 4 * cap), f32),
             shape((rows, width), bf16),
             shape((1, rows), i32),
-            shape((column_rows, width), bf16),
+            units,
+            units,
         ),
-        [pltpu.VMEM((rows, width), bf16)],
-    )(mine, other, centroids, prior_row, info)
+        [pltpu.VMEM((rows, width), bf16), gathered, gathered, pltpu.SemaphoreType.DMA((2,))],
+        in_specs=[HBM, HBM, VMEM, VMEM, VMEM, HBM, HBM],
+    )(mine, other, centroids, prior_row, info, early2, early3)
+    beside_rows = exchange(beside_rows, 1)
     apart = jnp.arange(16, dtype=i32) ^ lax.axis_index("shard")
     share = share[((apart & 1) << 3) | ((apart & 2) << 1) | (apart >> 2)]
     share = lax.all_to_all(share, "shard", split_axis=0, concat_axis=0, tiled=True)
     density = jnp.log(jnp.sum(share, axis=0)[:emb_rows] / (probe_count * BLOCK))
-    packed, sums = call(
-        functools.partial(second_kernel, cap, per),
-        (shape((4, per, 4 * cap, width), bf16), shape((8, 4 * cap), f32)),
-    )(scaled, facts, own_rows, rows1, rows2, rows3, centroids2, near_set)
+    held = pltpu.VMEM((half, width), bf16)
+    arrived = pltpu.VMEM((half + META, width), bf16)
+    block_set = pltpu.VMEM((per * BLOCK2, width), bf16)
+    packed = pltpu.VMEM((2, per, 4 * cap, width), bf16)
+    early = call(
+        functools.partial(second_kernel, cap, per, False),
+        shape((16, 4 * cap), f32),
+        [held, held, arrived, arrived, block_set, block_set, packed, pltpu.SemaphoreType.DMA((6,))],
+        in_specs=[VMEM, VMEM] + [HBM] * 6,
+    )(scaled, facts, own_rows, beside_rows, early2, early3, centroids2, near_set)
+    kept = shape((per, 4 * cap, width), bf16)
+    kept_rows, later = call(
+        functools.partial(second_kernel, cap, per, True),
+        (kept, shape((8, 4 * cap), f32)),
+        [held, held, arrived, arrived, block_set, packed, pltpu.SemaphoreType.DMA((5,))],
+        in_specs=[VMEM, VMEM] + [HBM] * 6 + [HBM],
+    )(scaled, facts, own_rows, beside_rows, late2, late3, cross_set, passed, early)
     tile = shape((8, 4 * cap), f32)
-    tiles = call(functools.partial(third_kernel, cap, per), (tile,) * 4)(
-        packed, sums, cross_set, passed, last_set, far_set
-    )
+    tiles = call(
+        functools.partial(third_kernel, cap, per),
+        (tile,) * 4,
+        [pltpu.VMEM(kept.shape, bf16), block_set, pltpu.SemaphoreType.DMA((2,))],
+        in_specs=[VMEM, VMEM, HBM, HBM, HBM],
+    )(early, later, kept_rows, last_set, far_set)
     tiles = [tile if r == 0 else exchange(tile, r) for r, tile in enumerate(tiles)]
     level_two = call(functools.partial(last_kernel, cap, BLOCK2), shape((1, rows), f32))(info, *tiles)
     return (density, new_centroids, counts.reshape(-1), level_two.reshape(-1))

time: 98.8 us -> 126 us (1.28)
  blocking collectives: 0 us -> 33.4 us
  starting transfers between devices: 32.2 us -> 19.7 us
  waiting for transfers between devices: 28.1 us -> 38.1 us
  local copies, waits for them, and re-layouts: 11.1 us -> 8.11 us
    all_to_all x0 -> x1, blocking collectives: none -> 33.4 us  [line_body(): lax.all_to_all(share, 'shard', split_axis=0, concat_axis=0, tiled=True)]
    all_to_all x1 -> x0, starting transfers between devices: 13.8 us -> none  [line_body(): lax.all_to_all(share, 'shard', split_axis=0, concat_axis=0, tiled=True)]
    ppermute x16 -> x18, waiting for transfers between devices: 28.1 us -> 38.1 us  [exchange(): return lax.ppermute(value, 'shard', [(i, i ^ apart) for i in sources])]
    pallas_call x5 -> x6, Pallas kernels: 18.1 us -> 13.5 us  [the longest x1 3.8 us: line_body(): call(functools.partial(second_kernel, cap, per, True), (kept, shape((8, 4...]
    pallas_call x1, Pallas kernels: 6.34 us -> 10.3 us  [line_body(): call(first_kernel, (shape((16 * emb_rows, width), bf16), shape((16, 16 *...]
    unnamed x33 -> x28, local copies, waits for them, and re-layouts: 9.93 us -> 7.51 us
    ppermute x16 -> x18, starting transfers between devices: 18.5 us -> 19.7 us  [exchange(): return lax.ppermute(value, 'shard', [(i, i ^ apart) for i in sources])]
  transfers between devices with their start and end apart: 17 -> 18, of which waited for: 5 -> 6; matrix products, arithmetic and copies ran while one was open for 2% -> 1% of each run, Pallas kernels for 21% -> 16%
where the time goes in v4:
time: 126 us
  waiting for transfers between devices  38.1 us (30%)
  blocking collectives  33.4 us (27%)
  Pallas kernels  24.9 us (20%)
  starting transfers between devices  19.7 us (16%)
  local copies, waits for them, and re-layouts  8.11 us (6%)
    ppermute x18, waiting for transfers between devices, exchange(): return lax.ppermute(value, 'shard', [(i, i ^ apart) for i in sources])  38.1 us
    all_to_all x1, blocking collectives, line_body(): lax.all_to_all(share, 'shard', split_axis=0, concat_axis=0, tiled=True)  33.4 us
    ppermute x18, starting transfers between devices, exchange(): return lax.ppermute(value, 'shard', [(i, i ^ apart) for i in sources])  19.7 us
    pallas_call x1, Pallas kernels, line_body(): call(first_kernel, (shape((16 * emb_rows, width), bf16), shape((16, 16 *...  10.3 us
    unnamed x28, local copies, waits for them, and re-layouts  7.51 us
    pallas_call x1, Pallas kernels, line_body(): call(functools.partial(second_kernel, cap, per, True), (kept, shape((8, 4...  3.8 us
    pallas_call x1, Pallas kernels, line_body(): call(functools.partial(second_kernel, cap, per, False), shape((16, 4 * ca...  3.78 us
  transfers between devices with their start and end apart: 18, of which 6 were waited for; matrix products, arithmetic and copies ran while one was open for 1% of the time, Pallas kernels for 16%

profile of v4, /device:TPU:0, one launch (start us, length us, event | category | flops | bytes accessed | tf_op | source)
XLA Modules:
  0.0 125.6 jit_solution(3517052753983285395)
XLA Ops:
  0.6 0.0 copy-start
  0.6 1.6 %copy-done = bf16[1024,1024]{1,0:T(8,128)(2,1)S(1)} copy-done((bf16[1024,1024]{1,0:T(8,128)(2,1)S(1)}, bf16[1024,1024]{1,0:T(8,128)(2,1)}, u32[]{:S(2)}) %copy-start) | copy-done | bytes 2097176
  2.2 0.0 copy-start.6
  2.2 0.9 copy-done.6
  3.1 0.0 copy-start.7
  3.1 0.7 copy-done.7
  3.8 0.0 copy-start.9
  3.8 0.7 copy-done.9
  4.5 0.0 copy-start.10
  4.5 0.7 copy-done.10
  5.2 0.0 copy-start.11
  5.2 0.7 copy-done.11
  5.8 2.1 %shard_map.102 = (bf16[40,1152]{1,0:T(8,128)(2,1)S(1)}, bf16[208,1024]{1,0:T(8,128)(2,1)S(1)}, bf16[208,1024]{1,0:T(8,128)(2,1)S(1)}, s32[8,1024]{1,0:T(8,128)S(1)}) custom-call(s32[1,1024]{1,0:T(1,128)S(1)} %bitcast.14, bf16[40,1024]{1,0:T(8,128)(2,1)S(1)} %copy-done.6, s32[8,40]{1,0:T(8,128)S(1)} %bitcast.15, s32[1,40]{1,0:T(1,128)S(1)} %bitcast.16, ...), custom_call_target="tpu_custom_call" | custom-call | tf_op jit(solution)/shard_map/pallas_call | solution.py:421
  7.9 3.1 %collective-permute-start = (bf16[40,1152]{1,0:T(8,128)(2,1)S(1)}, bf16[40,1152]{1,0:T(8,128)(2,1)S(1)}, u32[]{:S(2)}, u32[]{:S(2)}) collective-permute-start(bf16[40,1152]{1,0:T(8,128)(2,1)S(1)} %get-tuple-element.25), channel_id=1, source_target_pairs={{0,4},{1,5},{2,6},{3,7},{4,0},{5,1},{6,2},{7,3},{8,12},{9,13},{10,... | collective-permute-start | bytes 276488 | tf_op jit(solution)/shard_map/ppermute | solution.py:413
  11.0 2.6 %collective-permute-start.1 = (bf16[40,1152]{1,0:T(8,128)(2,1)S(1)}, bf16[40,1152]{1,0:T(8,128)(2,1)S(1)}, u32[]{:S(2)}, u32[]{:S(2)}) collective-permute-start(bf16[40,1152]{1,0:T(8,128)(2,1)S(1)} %get-tuple-element.25), channel_id=1, source_target_pairs={{0,8},{1,9},{2,10},{3,11},{4,12},{5,13},{6,14},{7,15},{8,0},{9,1},... | collective-permute-start | bytes 276488 | tf_op jit(solution)/shard_map/ppermute | solution.py:413
  13.6 0.0 collective-permute-start.2
  13.6 0.0 copy-done.2
  13.6 0.9 collective-permute-start.8
  14.5 1.6 %collective-permute-start.11 = (bf16[384,1024]{1,0:T(8,128)(2,1)S(1)}, bf16[384,1024]{1,0:T(8,128)(2,1)}, u32[]{:S(2)}, u32[]{:S(2)}) collective-permute-start(bf16[384,1024]{1,0:T(8,128)(2,1)S(1)} %copy-done.2), channel_id=1, source_target_pairs={{4,8},{5,9},{6,10},{7,11},{8,4},{9,5},{10,6},{11,7},{20,24},{21,25... | collective-permute-start | bytes 2359304 | tf_op jit(solution)/shard_map/ppermute | solution.py:413
  16.1 0.0 collective-permute-done
  16.1 5.0 %collective-permute-done.1 = bf16[40,1152]{1,0:T(8,128)(2,1)S(1)} collective-permute-done((bf16[40,1152]{1,0:T(8,128)(2,1)S(1)}, bf16[40,1152]{1,0:T(8,128)(2,1)S(1)}, u32[]{:S(2)}, u32[]{:S(2)}) %collective-permute-start.1) | collective-permute-done | bytes 92192 | tf_op jit(solution)/shard_map/ppermute | solution.py:413
  21.1 0.0 collective-permute-done.2
  21.1 1.6 %collective-permute-start.3 = (bf16[160,1152]{1,0:T(8,128)(2,1)S(1)}, bf16[160,1152]{1,0:T(8,128)(2,1)S(1)}, u32[]{:S(2)}, u32[]{:S(2)}) collective-permute-start(bf16[160,1152]{1,0:T(8,128)(2,1)S(1)} %pad_maximum_fusion), channel_id=1, source_target_pairs={{0,2},{1,3},{2,0},{3,1},{4,6},{5,7},{6,4},{7,5},{8,10},{9,11},{10,... | collective-permute-start | bytes 1105928 | tf_op jit(solution)/shard_map/ppermute | solution.py:413
  22.8 12.5 %collective-permute-done.8.refs_1_ = bf16[384,1024]{1,0:T(8,128)(2,1)S(1)} collective-permute-done((bf16[384,1024]{1,0:T(8,128)(2,1)S(1)}, bf16[384,1024]{1,0:T(8,128)(2,1)S(1)}, u32[]{:S(2)}, u32[]{:S(2)}) %collective-permute-start.8) | collective-permute-done | bytes 786464 | tf_op jit(solution)/shard_map/ppermute | solution.py:413
  35.3 1.6 %collective-permute-start.13 = (bf16[384,1024]{1,0:T(8,128)(2,1)S(1)}, bf16[384,1024]{1,0:T(8,128)(2,1)}, u32[]{:S(2)}, u32[]{:S(2)}) collective-permute-start(bf16[384,1024]{1,0:T(8,128)(2,1)S(1)} %collective-permute-done.8.refs_1_), channel_id=1, source_target_pairs={{4,8},{5,9},{6,10},{7,11},{8,4},{9,5},{10,6},{11,7},{20,24},{21,25... | collective-permute-start | bytes 2359304 | tf_op jit(solution)/shard_map/ppermute | solution.py:413
  36.9 0.0 collective-permute-done.3
  36.9 0.1 collective-permute-start.4
  37.0 1.6 %collective-permute-start.5 = (bf16[208,1024]{1,0:T(8,128)(2,1)S(1)}, bf16[208,1024]{1,0:T(8,128)(2,1)S(1)}, u32[]{:S(2)}, u32[]{:S(2)}) collective-permute-start(bf16[208,1024]{1,0:T(8,128)(2,1)S(1)} %get-tuple-element.27), channel_id=1, source_target_pairs={{0,2},{1,3},{2,0},{3,1},{4,6},{5,7},{6,4},{7,5},{8,10},{9,11},{10,... | collective-permute-start | bytes 1277960 | tf_op jit(solution)/shard_map/ppermute | solution.py:413
  38.6 0.3 collective-permute-start.6
  38.8 10.8 %collective-permute-done.5.early2.rows2_any.refs_2_ = bf16[208,1024]{1,0:T(8,128)(2,1)S(1)} collective-permute-done((bf16[208,1024]{1,0:T(8,128)(2,1)S(1)}, bf16[208,1024]{1,0:T(8,128)(2,1)S(1)}, u32[]{:S(2)}, u32[]{:S(2)}) %collective-permute-start.5) | collective-permute-done | bytes 426016 | tf_op jit(solution)/shard_map/ppermute | solution.py:413
  49.7 8.2 %collective-permute-done.6.early3.rows3_any.refs_3_ = bf16[208,1024]{1,0:T(8,128)(2,1)S(1)} collective-permute-done((bf16[208,1024]{1,0:T(8,128)(2,1)S(1)}, bf16[208,1024]{1,0:T(8,128)(2,1)S(1)}, u32[]{:S(2)}, u32[]{:S(2)}) %collective-permute-start.6) | collective-permute-done | bytes 426016 | tf_op jit(solution)/shard_map/ppermute | solution.py:413
  57.9 0.0 collective-permute-done.4.other_any
  57.9 0.0 copy-done.8
  57.9 10.3 %shard_map.103 = (bf16[640,1024]{1,0:T(8,128)(2,1)S(1)}, s32[16,640]{1,0:T(8,128)S(1)}, f32[16,128]{1,0:T(8,128)S(1)}, bf16[1024,1024]{1,0:T(8,128)(2,1)}, s32[1...) custom-call(bf16[320,1152]{1,0:T(8,128)(2,1)S(1)} %constant_dynamic-update-slice_fusion.mine_any, ...), custom_call_target="tpu_custom_call" | custom-call | tf_op jit(solution)/shard_map/pallas_call | solution.py:449
  68.2 0.0 copy-done.4
  68.2 0.3 collective-permute-start.7
  68.6 0.0 collective-permute-done.11.refs_0_
  68.6 1.3 %collective-permute-start.12 = (bf16[384,1024]{1,0:T(8,128)(2,1)}, bf16[384,1024]{1,0:T(8,128)(2,1)}, u32[]{:S(2)}, u32[]{:S(2)}) collective-permute-start(bf16[384,1024]{1,0:T(8,128)(2,1)} %collective-permute-done.11.refs_0_), channel_id=1, source_target_pairs={{4,0},{5,1},{6,2},{7,3},{8,12},{9,13},{10,14},{11,15},{20,16},{21,... | collective-permute-start | bytes 2359304 | tf_op jit(solution)/shard_map/ppermute | solution.py:413
  69.9 0.0 collective-permute-done.13.last_any
  69.9 1.3 %collective-permute-start.14 = (bf16[384,1024]{1,0:T(8,128)(2,1)}, bf16[384,1024]{1,0:T(8,128)(2,1)}, u32[]{:S(2)}, u32[]{:S(2)}) collective-permute-start(bf16[384,1024]{1,0:T(8,128)(2,1)} %collective-permute-done.13.last_any), channel_id=1, source_target_pairs={{4,0},{5,1},{6,2},{7,3},{8,12},{9,13},{10,14},{11,15},{20,16},{21,... | collective-permute-start | bytes 2359304 | tf_op jit(solution)/shard_map/ppermute | solution.py:413
  71.2 0.0 copy-done.1
  71.2 2.0 %shard_map.105 = (bf16[208,1024]{1,0:T(8,128)(2,1)S(1)}, bf16[208,1024]{1,0:T(8,128)(2,1)}) custom-call(s32[8,1024]{1,0:T(8,128)S(1)} %get-tuple-element.26.info, s32[1,1024]{1,0:T(1,128)S(1)} %bitcast.13, bf16[1024,1024]{1,0:T(8,128)(2,1)S(1)} %copy-done.1), custom_call_target="tpu_custom_call" | custom-call | tf_op jit(solution)/shard_map/pallas_call | solution.py:436
  73.2 1.5 %collective-permute-start.9 = (bf16[208,1024]{1,0:T(8,128)(2,1)S(1)}, bf16[208,1024]{1,0:T(8,128)(2,1)}, u32[]{:S(2)}, u32[]{:S(2)}) collective-permute-start(bf16[208,1024]{1,0:T(8,128)(2,1)S(1)} %get-tuple-element.38), channel_id=1, source_target_pairs={{0,2},{1,3},{2,0},{3,1},{4,6},{5,7},{6,4},{7,5},{8,10},{9,11},{10,... | collective-permute-start | bytes 1277960 | tf_op jit(solution)/shard_map/ppermute | solution.py:413
  74.7 0.1 collective-permute-start.10
  74.8 0.6 gather_fusion
  75.3 33.4 %all_to_all.9 = f32[16,1,128]{2,1,0:T(1,128)S(1)} all-to-all(f32[16,1,128]{2,1,0:T(1,128)S(1)} %bitcast.17), channel_id=1, replica_groups=mesh['groups'=2,'shard'=16] {'shard'}, dimensions={0} | all-to-all | bytes 16384 | tf_op jit(solution)/shard_map/all_to_all | solution.py:466
  108.8 0.0 collective-permute-done.7.beside_any
  108.8 1.1 copy-done.3
  109.9 1.1 copy-done.5
  111.1 3.8 %shard_map.104.refs_2_.early = f32[16,128]{1,0:T(8,128)S(1)} custom-call(bf16[640,1024]{1,0:T(8,128)(2,1)S(1)} %get-tuple-element.32.scaled, s32[16,640]{1,0:T(8,128)S(1)} %get-tuple-element.33.facts_in, bf16[384,1024]{1,0:T(8,128)(2,1)S(1)} %get-tuple-element.34.own_any, bf16[384,1024]{1,0:T(8,128)(2,1)} %collective-permute-done.7.beside_any, ...), custom_call_target="tpu_custom_call" | custom-call | tf_op jit(solution)/shard_map/pallas_call | solution.py:472
  114.9 0.0 collective-permute-done.9.rows2_any
  114.9 0.0 collective-permute-done.10.rows3_any
  114.9 0.0 collective-permute-done.12.refs_1_
  114.9 3.8 %shard_map.107 = (bf16[3,128,1024]{2,1,0:T(8,128)(2,1)S(1)}, f32[8,128]{1,0:T(8,128)S(1)}) custom-call(bf16[640,1024]{1,0:T(8,128)(2,1)S(1)} %get-tuple-element.32.scaled, s32[16,640]{1,0:T(8,128)S(1)} %get-tuple-element.33.facts_in, bf16[384,1024]{1,0:T(8,128)(2,1)S(1)} %get-tuple-element.34.own_any, bf16[384,1024]{1,0:T(8,128)(2,1)} %collective-permute-done.7.beside_any, ...), custom_call_target="tpu_custom_call" | custom-call | tf_op jit(solution)/shard_map/pallas_call | solution.py:479
  118.7 0.0 collective-permute-done.14.far_any
  118.7 1.9 %shard_map.108 = (f32[8,128]{1,0:T(8,128)S(1)}, f32[8,128]{1,0:T(8,128)S(1)}, f32[8,128]{1,0:T(8,128)S(1)}, f32[8,128]{1,0:T(8,128)S(1)}) custom-call(f32[16,128]{1,0:T(8,128)S(1)} %shard_map.104.refs_2_.early, f32[8,128]{1,0:T(8,128)S(1)} %get-tuple-element.40.later, bf16[3,128,1024]{2,1,0:T(8,128)(2,1)S(1)} %get-tuple-element.41.kept_any, ...), custom_call_target="tpu_custom_call" | custom-call | tf_op jit(solution)/shard_map/pallas_call | solution.py:486
  120.6 0.1 collective-permute-start.15
  120.7 0.8 collective-permute-start.16
  121.5 1.0 collective-permute-start.17
  122.6 0.5 multiply_log_fusion
  123.1 0.0 collective-permute-done.15.got1
  123.1 1.3 %collective-permute-done.16.got2 = f32[8,128]{1,0:T(8,128)S(1)} collective-permute-done((f32[8,128]{1,0:T(8,128)S(1)}, f32[8,128]{1,0:T(8,128)S(1)}, u32[]{:S(2)}, u32[]{:S(2)}) %collective-permute-start.16) | collective-permute-done | bytes 4128 | tf_op jit(solution)/shard_map/ppermute | solution.py:413
  124.4 0.2 collective-permute-done.17.got3
  124.6 1.0 shard_map.109
  (16 shorter events, 0.2 us)
Async XLA Ops:
  0.6 1.6 %copy-start = (bf16[1024,1024]{1,0:T(8,128)(2,1)S(1)}, bf16[1024,1024]{1,0:T(8,128)(2,1)}, u32[]{:S(2)}) copy-start(bf16[1024,1024]{1,0:T(8,128)(2,1)} %cent_ref.3) | copy-start | bytes 6291460
  2.2 0.9 copy-start.6
  3.1 0.7 copy-start.7
  3.8 0.7 copy-start.9
  4.5 0.7 copy-start.10
  5.2 0.7 copy-start.11
  5.8 7.8 %copy-start.2 = (bf16[384,1024]{1,0:T(8,128)(2,1)S(1)}, bf16[384,1024]{1,0:T(8,128)(2,1)}, u32[]{:S(2)}) copy-start(bf16[384,1024]{1,0:T(8,128)(2,1)} %refs_0_.1) | copy-start | bytes 2359300
  5.8 52.1 %copy-start.8 = (s32[1024]{0:T(1024)S(1)}, s32[1024]{0:T(1024)}, u32[]{:S(2)}) copy-start(s32[1024]{0:T(1024)} %param.10) | copy-start | bytes 12292
  7.9 8.2 %collective-permute-start = (bf16[40,1152]{1,0:T(8,128)(2,1)S(1)}, bf16[40,1152]{1,0:T(8,128)(2,1)S(1)}, u32[]{:S(2)}, u32[]{:S(2)}) collective-permute-start(bf16[40,1152]{1,0:T(8,128)(2,1)S(1)} %get-tuple-element.25), channel_id=1, source_target_pairs={{0,4},{1,5},{2,6},{3,7},{4,0},{5,1},{6,2},{7,3},{8,12},{9,13},{10,... | collective-permute-start | bytes 276488 | tf_op jit(solution)/shard_map/ppermute | solution.py:413
  11.0 10.1 %collective-permute-start.1 = (bf16[40,1152]{1,0:T(8,128)(2,1)S(1)}, bf16[40,1152]{1,0:T(8,128)(2,1)S(1)}, u32[]{:S(2)}, u32[]{:S(2)}) collective-permute-start(bf16[40,1152]{1,0:T(8,128)(2,1)S(1)} %get-tuple-element.25), channel_id=1, source_target_pairs={{0,8},{1,9},{2,10},{3,11},{4,12},{5,13},{6,14},{7,15},{8,0},{9,1},... | collective-permute-start | bytes 276488 | tf_op jit(solution)/shard_map/ppermute | solution.py:413
  13.6 7.5 %collective-permute-start.2 = (bf16[40,1152]{1,0:T(8,128)(2,1)S(1)}, bf16[40,1152]{1,0:T(8,128)(2,1)S(1)}, u32[]{:S(2)}, u32[]{:S(2)}) collective-permute-start(bf16[40,1152]{1,0:T(8,128)(2,1)S(1)} %get-tuple-element.25), channel_id=1, source_target_pairs={{0,12},{1,13},{2,14},{3,15},{4,8},{5,9},{6,10},{7,11},{8,4},{9,5},... | collective-permute-start | bytes 276488 | tf_op jit(solution)/shard_map/ppermute | solution.py:413
  13.6 21.7 %collective-permute-start.8 = (bf16[384,1024]{1,0:T(8,128)(2,1)S(1)}, bf16[384,1024]{1,0:T(8,128)(2,1)S(1)}, u32[]{:S(2)}, u32[]{:S(2)}) collective-permute-start(bf16[384,1024]{1,0:T(8,128)(2,1)S(1)} %copy-done.2), channel_id=1, source_target_pairs={{0,4},{1,5},{2,6},{3,7},{4,0},{5,1},{6,2},{7,3},{8,12},{9,13},{10,... | collective-permute-start | bytes 2359304 | tf_op jit(solution)/shard_map/ppermute | solution.py:413
  14.5 54.1 %collective-permute-start.11 = (bf16[384,1024]{1,0:T(8,128)(2,1)S(1)}, bf16[384,1024]{1,0:T(8,128)(2,1)}, u32[]{:S(2)}, u32[]{:S(2)}) collective-permute-start(bf16[384,1024]{1,0:T(8,128)(2,1)S(1)} %copy-done.2), channel_id=1, source_target_pairs={{4,8},{5,9},{6,10},{7,11},{8,4},{9,5},{10,6},{11,7},{20,24},{21,25... | collective-permute-start | bytes 2359304 | tf_op jit(solution)/shard_map/ppermute | solution.py:413
  21.1 15.8 %collective-permute-start.3 = (bf16[160,1152]{1,0:T(8,128)(2,1)S(1)}, bf16[160,1152]{1,0:T(8,128)(2,1)S(1)}, u32[]{:S(2)}, u32[]{:S(2)}) collective-permute-start(bf16[160,1152]{1,0:T(8,128)(2,1)S(1)} %pad_maximum_fusion), channel_id=1, source_target_pairs={{0,2},{1,3},{2,0},{3,1},{4,6},{5,7},{6,4},{7,5},{8,10},{9,11},{10,... | collective-permute-start | bytes 1105928 | tf_op jit(solution)/shard_map/ppermute | solution.py:413
  35.3 32.9 %copy-start.4 = (bf16[384,1024]{1,0:T(8,128)(2,1)}, bf16[384,1024]{1,0:T(8,128)(2,1)S(1)}, u32[]{:S(2)}) copy-start(bf16[384,1024]{1,0:T(8,128)(2,1)S(1)} %collective-permute-done.8.refs_1_) | copy-start | bytes 2359300
  35.3 34.6 %collective-permute-start.13 = (bf16[384,1024]{1,0:T(8,128)(2,1)S(1)}, bf16[384,1024]{1,0:T(8,128)(2,1)}, u32[]{:S(2)}, u32[]{:S(2)}) collective-permute-start(bf16[384,1024]{1,0:T(8,128)(2,1)S(1)} %collective-permute-done.8.refs_1_), channel_id=1, source_target_pairs={{4,8},{5,9},{6,10},{7,11},{8,4},{9,5},{10,6},{11,7},{20,24},{21,25... | collective-permute-start | bytes 2359304 | tf_op jit(solution)/shard_map/ppermute | solution.py:413
  36.9 21.0 %collective-permute-start.4 = (bf16[320,1152]{1,0:T(8,128)(2,1)S(1)}, bf16[320,1152]{1,0:T(8,128)(2,1)S(1)}, u32[]{:S(2)}, u32[]{:S(2)}) collective-permute-start(bf16[320,1152]{1,0:T(8,128)(2,1)S(1)} %constant_dynamic-update-slice_fusion.mine_any), channel_id=1, source_target_pairs={{0,1},{1,0},{2,3},{3,2},{4,5},{5,4},{6,7},{7,6},{8,9},{9,8},{10,11... | collective-permute-start | bytes 2211848 | tf_op jit(solution)/shard_map/ppermute | solution.py:413
  37.0 12.7 %collective-permute-start.5 = (bf16[208,1024]{1,0:T(8,128)(2,1)S(1)}, bf16[208,1024]{1,0:T(8,128)(2,1)S(1)}, u32[]{:S(2)}, u32[]{:S(2)}) collective-permute-start(bf16[208,1024]{1,0:T(8,128)(2,1)S(1)} %get-tuple-element.27), channel_id=1, source_target_pairs={{0,2},{1,3},{2,0},{3,1},{4,6},{5,7},{6,4},{7,5},{8,10},{9,11},{10,... | collective-permute-start | bytes 1277960 | tf_op jit(solution)/shard_map/ppermute | solution.py:413
  38.6 19.3 %collective-permute-start.6 = (bf16[208,1024]{1,0:T(8,128)(2,1)S(1)}, bf16[208,1024]{1,0:T(8,128)(2,1)S(1)}, u32[]{:S(2)}, u32[]{:S(2)}) collective-permute-start(bf16[208,1024]{1,0:T(8,128)(2,1)S(1)} %get-tuple-element.28), channel_id=1, source_target_pairs={{0,3},{1,2},{2,1},{3,0},{4,7},{5,6},{6,5},{7,4},{8,11},{9,10},{10,... | collective-permute-start | bytes 1277960 | tf_op jit(solution)/shard_map/ppermute | solution.py:413
  57.9 13.3 %copy-start.1 = (bf16[1024,1024]{1,0:T(8,128)(2,1)S(1)}, bf16[1024,1024]{1,0:T(8,128)(2,1)}, u32[]{:S(2)}) copy-start(bf16[1024,1024]{1,0:T(8,128)(2,1)} %cent_ref.3) | copy-start | bytes 6291460
  68.2 40.5 %collective-permute-start.7 = (bf16[384,1024]{1,0:T(8,128)(2,1)}, bf16[384,1024]{1,0:T(8,128)(2,1)}, u32[]{:S(2)}, u32[]{:S(2)}) collective-permute-start(bf16[384,1024]{1,0:T(8,128)(2,1)} %get-tuple-element.35), channel_id=1, source_target_pairs={{0,1},{1,0},{2,3},{3,2},{4,5},{5,4},{6,7},{7,6},{8,9},{9,8},{10,11... | collective-permute-start | bytes 2359304 | tf_op jit(solution)/shard_map/ppermute | solution.py:413
  68.6 46.3 %collective-permute-start.12 = (bf16[384,1024]{1,0:T(8,128)(2,1)}, bf16[384,1024]{1,0:T(8,128)(2,1)}, u32[]{:S(2)}, u32[]{:S(2)}) collective-permute-start(bf16[384,1024]{1,0:T(8,128)(2,1)} %collective-permute-done.11.refs_0_), channel_id=1, source_target_pairs={{4,0},{5,1},{6,2},{7,3},{8,12},{9,13},{10,14},{11,15},{20,16},{21,... | collective-permute-start | bytes 2359304 | tf_op jit(solution)/shard_map/ppermute | solution.py:413
  69.9 48.8 %collective-permute-start.14 = (bf16[384,1024]{1,0:T(8,128)(2,1)}, bf16[384,1024]{1,0:T(8,128)(2,1)}, u32[]{:S(2)}, u32[]{:S(2)}) collective-permute-start(bf16[384,1024]{1,0:T(8,128)(2,1)} %collective-permute-done.13.last_any), channel_id=1, source_target_pairs={{4,0},{5,1},{6,2},{7,3},{8,12},{9,13},{10,14},{11,15},{20,16},{21,... | collective-permute-start | bytes 2359304 | tf_op jit(solution)/shard_map/ppermute | solution.py:413
  73.2 41.7 %collective-permute-start.9 = (bf16[208,1024]{1,0:T(8,128)(2,1)S(1)}, bf16[208,1024]{1,0:T(8,128)(2,1)}, u32[]{:S(2)}, u32[]{:S(2)}) collective-permute-start(bf16[208,1024]{1,0:T(8,128)(2,1)S(1)} %get-tuple-element.38), channel_id=1, source_target_pairs={{0,2},{1,3},{2,0},{3,1},{4,6},{5,7},{6,4},{7,5},{8,10},{9,11},{10,... | collective-permute-start | bytes 1277960 | tf_op jit(solution)/shard_map/ppermute | solution.py:413
  74.7 40.2 %collective-permute-start.10 = (bf16[208,1024]{1,0:T(8,128)(2,1)}, bf16[208,1024]{1,0:T(8,128)(2,1)}, u32[]{:S(2)}, u32[]{:S(2)}) collective-permute-start(bf16[208,1024]{1,0:T(8,128)(2,1)} %get-tuple-element.39), channel_id=1, source_target_pairs={{0,3},{1,2},{2,1},{3,0},{4,7},{5,6},{6,5},{7,4},{8,11},{9,10},{10,... | collective-permute-start | bytes 1277960 | tf_op jit(solution)/shard_map/ppermute | solution.py:413
  108.8 1.1 copy-start.3
  109.9 1.1 copy-start.5
  120.6 2.5 %collective-permute-start.15 = (f32[8,128]{1,0:T(8,128)S(1)}, f32[8,128]{1,0:T(8,128)S(1)}, u32[]{:S(2)}, u32[]{:S(2)}) collective-permute-start(f32[8,128]{1,0:T(8,128)S(1)} %get-tuple-element.43), channel_id=1, source_target_pairs={{0,1},{1,0},{2,3},{3,2},{4,5},{5,4},{6,7},{7,6},{8,9},{9,8},{10,11... | collective-permute-start | bytes 12296 | tf_op jit(solution)/shard_map/ppermute | solution.py:413
  120.7 3.7 %collective-permute-start.16 = (f32[8,128]{1,0:T(8,128)S(1)}, f32[8,128]{1,0:T(8,128)S(1)}, u32[]{:S(2)}, u32[]{:S(2)}) collective-permute-start(f32[8,128]{1,0:T(8,128)S(1)} %get-tuple-element.44), channel_id=1, source_target_pairs={{0,2},{1,3},{2,0},{3,1},{4,6},{5,7},{6,4},{7,5},{8,10},{9,11},{10,... | collective-permute-start | bytes 12296 | tf_op jit(solution)/shard_map/ppermute | solution.py:413
  121.5 3.0 %collective-permute-start.17 = (f32[8,128]{1,0:T(8,128)S(1)}, f32[8,128]{1,0:T(8,128)S(1)}, u32[]{:S(2)}, u32[]{:S(2)}) collective-permute-start(f32[8,128]{1,0:T(8,128)S(1)} %get-tuple-element.45), channel_id=1, source_target_pairs={{0,3},{1,2},{2,1},{3,0},{4,7},{5,6},{6,5},{7,4},{8,11},{9,10},{10,... | collective-permute-start | bytes 12296 | tf_op jit(solution)/shard_map/ppermute | solution.py:413
